TPU v7x, 32 devices: a whole 2x2x4 slice. The times are simulated.
32 devices in a mesh: frames: 4 (over x, core), mp: 8 (over z, y).
Axes of the slice: x: 2, y: 2, z: 4, core: 2. Of those that a mesh axis runs over, the one named last changes fastest.
Arguments:
- inputs: bfloat16 [1536, 16, 1024], P(('frames', 'mp')), may hold values from -6 to 6
- counts: int32 [4], P('frames'), may hold values from 96 to 384, as said below
- norm_gains: float32 [2, 16, 1024], replicated, may hold values from 0.5 to 1.5
- in_weight: bfloat16 [16, 3, 1024, 1024], P(None, None, None, 'mp'), may hold values from -0.1875 to 0.1875
- out_weight: bfloat16 [16, 1024, 1024], P(None, 'mp'), may hold values from -0.5 to 0.5
- gate_up: bfloat16 [16, 2, 1024, 4096], P(None, None, None, 'mp'), may hold values from -0.1875 to 0.1875
- down_weight: bfloat16 [16, 4096, 1024], P(None, 'mp'), may hold values from -0.09375 to 0.09375
- cotangent: bfloat16 [1536, 16, 1024], P(('frames', 'mp')), may hold values from -6 to 6
Outputs:
- output: bfloat16 [1536, 16, 1024], P(('frames', 'mp'))
- input_grad: bfloat16 [1536, 16, 1024], P(('frames', 'mp'))
- grad_in_weight: float32 [16, 3, 1024, 1024], P(None, None, 'frames', 'mp')
- grad_out_weight: float32 [16, 1024, 1024], P(None, 'mp', 'frames')
- grad_gate_up: float32 [16, 2, 1024, 4096], P(None, None, 'frames', 'mp')
- grad_down: float32 [16, 4096, 1024], P(None, 'mp', 'frames')
- grad_gains: float32 [2, 16, 1024], P(None, None, 'frames')
Inputs may be any that keep to these rules, and one draw needn't show every extreme that they name: counts[i] valid frames start each block of 384 frames; at least one block is completely valid.
All inputs are finite; a program needn't handle non-finite values.
Results may differ from a plain program's by a relative error of at most 0.014.
Values may be sent and summed in bfloat16 or wider, within the bound.
A program may use at most 384 MiB of HBM per device.

v0:
```python
import jax
import jax.numpy as jnp
from jax import lax
from jax.sharding import PartitionSpec as P

HDIM = 64


epsilon = 1e-05


def inverse_rms(values):
    return lax.rsqrt(jnp.mean(values * values, axis=-1, keepdims=True) + epsilon)


def norm_back(grad_normed, normed, factor, gain):
    scaled = grad_normed * gain
    return factor * (scaled - normed * jnp.mean(scaled * normed, axis=-1, keepdims=True))


def group_rows(values):
    return lax.all_gather(values, "mp", axis=0, tiled=True)


def group_total(term_fn, rows):
    return lax.psum_scatter(
        term_fn(jnp.int32(0), rows * lax.axis_size("mp")), "mp", scatter_dimension=0, tiled=True
    )


def sum_all_grads(grad_qkv, grad_proj_out, grad_gu, grad_dn, gain_terms):
    return (
        lax.psum_scatter(
            grad_qkv.astype(jnp.bfloat16), "frames", scatter_dimension=2, tiled=True
        ).astype(jnp.float32),
        lax.psum_scatter(
            grad_proj_out.astype(jnp.bfloat16), "frames", scatter_dimension=2, tiled=True
        ).astype(jnp.float32),
        lax.psum_scatter(
            grad_gu.astype(jnp.bfloat16), "frames", scatter_dimension=2, tiled=True
        ).astype(jnp.float32),
        lax.psum_scatter(
            grad_dn.astype(jnp.bfloat16), "frames", scatter_dimension=2, tiled=True
        ).astype(jnp.float32),
        lax.psum_scatter(
            gain_terms.astype(jnp.bfloat16), "frames", scatter_dimension=2, tiled=True
        ).astype(jnp.float32),
    )


def causal_logits(queries, keys):
    positions = queries.shape[1]
    causal = jnp.arange(positions)[:, None] >= jnp.arange(positions)[None, :]
    logits = jnp.einsum(
        "fphe,fqhe->fhpq", queries, keys, preferred_element_type=jnp.float32
    ) * HDIM ** (-0.5)
    return jnp.where(causal, logits, -1e30)


def attend_forward(projected):
    frame_count, positions, three, width = projected.shape
    split_heads = projected.reshape(frame_count, positions, 3, width // HDIM, HDIM)
    queries, keys, values = (split_heads[:, :, 0], split_heads[:, :, 1], split_heads[:, :, 2])
    logits = causal_logits(queries, keys)
    top = jnp.max(logits, axis=-1, keepdims=True)
    log_total = top + jnp.log(jnp.sum(jnp.exp(logits - top), axis=-1, keepdims=True))
    probs = jnp.exp(logits - log_total)
    mixed = jnp.einsum(
        "fhpq,fqhe->fphe", probs.astype(jnp.bfloat16), values, preferred_element_type=jnp.float32
    )
    return (mixed.astype(jnp.bfloat16).reshape(frame_count, positions, width), log_total)


def attend_backward(projected, log_total, grad_mixed):
    frame_count, positions, three, width = projected.shape
    split_heads = projected.reshape(frame_count, positions, 3, width // HDIM, HDIM)
    queries, keys, values = (split_heads[:, :, 0], split_heads[:, :, 1], split_heads[:, :, 2])
    grad_heads = grad_mixed.reshape(frame_count, positions, width // HDIM, HDIM)
    probs = jnp.exp(causal_logits(queries, keys) - log_total)
    grad_values = jnp.einsum(
        "fhpq,fphe->fqhe",
        probs.astype(jnp.bfloat16),
        grad_heads,
        preferred_element_type=jnp.float32,
    )
    grad_probs = jnp.einsum(
        "fphe,fqhe->fhpq", grad_heads, values, preferred_element_type=jnp.float32
    )
    row_dots = jnp.sum(grad_probs * probs, axis=-1, keepdims=True)
    grad_scores = (probs * (grad_probs - row_dots)).astype(jnp.bfloat16)
    factor = HDIM ** (-0.5)
    grad_queries = (
        jnp.einsum("fhpq,fqhe->fphe", grad_scores, keys, preferred_element_type=jnp.float32)
        * factor
    )
    grad_keys = (
        jnp.einsum("fhpq,fphe->fqhe", grad_scores, queries, preferred_element_type=jnp.float32)
        * factor
    )
    grad_proj = jnp.stack([grad_queries, grad_keys, grad_values], axis=2).astype(jnp.bfloat16)
    return grad_proj.reshape(frame_count, positions, 3, width)


def body(inputs, counts, norm_gains, in_weight, out_weight, gate_up, down_weight, cotangent):
    f32 = jnp.float32
    bf16 = jnp.bfloat16
    local_frames = inputs.shape[0]
    mp_size = lax.axis_size("mp")
    group_frames = local_frames * mp_size
    limit = counts[0]
    group_valid = (jnp.arange(group_frames) < limit)[:, None, None]
    local_ids = lax.axis_index("mp") * local_frames + jnp.arange(local_frames)
    local_mask = (local_ids < limit).astype(f32)[:, None, None]
    residual = inputs.astype(f32)
    scale_first = inverse_rms(residual)
    normed_first = residual * scale_first
    attn_in = group_rows((normed_first * norm_gains[0]).astype(bf16))
    projected = jnp.einsum("fpd,pcde->fpce", attn_in, in_weight, preferred_element_type=f32).astype(
        bf16
    )
    mixed, log_total = attend_forward(projected)

    def attn_term(start, count):
        return jnp.einsum("fpe,ped->fpd", mixed, out_weight, preferred_element_type=f32)

    attn_out = group_total(attn_term, local_frames)
    hidden_mid = residual + local_mask * attn_out
    scale_second = inverse_rms(hidden_mid)
    normed_second = hidden_mid * scale_second
    ffn_in = group_rows((normed_second * norm_gains[1]).astype(bf16))
    gate_pair = jnp.einsum("fpd,pcdk->fpck", ffn_in, gate_up, preferred_element_type=f32)
    gate = gate_pair[:, :, 0]
    upper = gate_pair[:, :, 1]
    sigma = jax.nn.sigmoid(gate)
    silu_gate = gate * sigma
    activated = (silu_gate * upper).astype(bf16)

    def ffn_term(start, count):
        return jnp.einsum("fpk,pkd->fpd", activated, down_weight, preferred_element_type=f32)

    ffn_out = group_total(ffn_term, local_frames)
    output = (hidden_mid + local_mask * ffn_out).astype(bf16)
    grad_rows = group_rows(cotangent)
    grad_ffn = jnp.where(group_valid, grad_rows, jnp.zeros_like(grad_rows))
    grad_down = jnp.einsum("fpk,fpd->pkd", activated, grad_ffn, preferred_element_type=f32)
    grad_act = jnp.einsum("fpd,pkd->fpk", grad_ffn, down_weight, preferred_element_type=f32)
    grad_gate = grad_act * upper * sigma * (1.0 + gate * (1.0 - sigma))
    grad_upper = grad_act * silu_gate
    grad_pair = jnp.stack([grad_gate, grad_upper], axis=2).astype(bf16)
    grad_gate_up = jnp.einsum("fpd,fpck->pcdk", ffn_in, grad_pair, preferred_element_type=f32)

    def ffn_back_term(start, count):
        return jnp.einsum("fpck,pcdk->fpd", grad_pair, gate_up, preferred_element_type=f32)

    grad_ffn_in = group_total(ffn_back_term, local_frames)
    gain_second = jnp.sum(grad_ffn_in * normed_second, axis=0)
    grad_mid = cotangent.astype(f32) + norm_back(
        grad_ffn_in, normed_second, scale_second, norm_gains[1]
    )
    grad_attn = group_rows((local_mask * grad_mid).astype(bf16))
    grad_out_w = jnp.einsum("fpe,fpd->ped", mixed, grad_attn, preferred_element_type=f32)
    grad_mixed = jnp.einsum(
        "fpd,ped->fpe", grad_attn, out_weight, preferred_element_type=f32
    ).astype(bf16)
    grad_proj = attend_backward(projected, log_total, grad_mixed)
    grad_in_w = jnp.einsum("fpd,fpce->pcde", attn_in, grad_proj, preferred_element_type=f32)

    def attn_back_term(start, count):
        return jnp.einsum("fpce,pcde->fpd", grad_proj, in_weight, preferred_element_type=f32)

    grad_attn_in = group_total(attn_back_term, local_frames)
    gain_first = jnp.sum(grad_attn_in * normed_first, axis=0)
    input_grad = (
        grad_mid + norm_back(grad_attn_in, normed_first, scale_first, norm_gains[0])
    ).astype(bf16)
    gain_terms = jnp.stack([gain_first, gain_second], axis=0)
    summed_in, summed_out, summed_gate_up, summed_down, summed_gains = sum_all_grads(
        grad_in_w, grad_out_w, grad_gate_up, grad_down, gain_terms
    )
    grad_gains = lax.psum(summed_gains, "mp")
    return (output, input_grad, summed_in, summed_out, summed_gate_up, summed_down, grad_gains)


def solution(mesh):
    placed = (
        P(("frames", "mp"), None, None),
        P("frames"),
        P(),
        P(None, None, None, "mp"),
        P(None, "mp", None),
        P(None, None, None, "mp"),
        P(None, "mp", None),
        P(("frames", "mp"), None, None),
    )
    return jax.shard_map(
        body,
        mesh=mesh,
        in_specs=placed,
        out_specs=(
            P(("frames", "mp"), None, None),
            P(("frames", "mp"), None, None),
            P(None, None, "frames", "mp"),
            P(None, "mp", "frames"),
            P(None, None, "frames", "mp"),
            P(None, "mp", "frames"),
            P(None, None, "frames"),
        ),
        check_vma=False,
    )
```

profile of v0, /device:TPU:0, one launch (start us, length us, event | category | flops | bytes accessed | tf_op | source)
XLA Modules:
  0.0 3090.3 jit_solution(15618004830701256146)
XLA Ops:
  15.3 16.7 copy.67
  32.1 162.5 %all-gather.5.cloned.1.call-done = bf16[384,16,1024]{2,0,1:T(8,128)(2,1)} async-done(((bf16[48,16,1024]{2,0,1:T(8,128)(2,1)}), bf16[384,16,1024]{2,0,1:T(8,128)(2,1)}) %all-gather.5.cloned.1.call-update) | async-done | bytes 12582928 | tf_op jit(solution)/shard_map/all_gather | solution.py:22
  194.6 13.8 fusion.70
  208.4 4.4 convert_element_type.96
  215.1 5.2 copy.106
  220.3 5.3 copy.105
  225.7 6.9 copy.107
  232.6 4.9 fusion.30
  244.1 4.5 copy.72
  248.6 14.5 convolution_bitcast_fusion.2
  264.8 400.4 %reduce-scatter.10.cloned.1.call-done = f32[48,16,1024]{2,0,1:T(8,128)} async-done(((f32[384,16,1024]{2,0,1:T(8,128)}), f32[48,16,1024]{2,0,1:T(8,128)}) %reduce-scatter.10.cloned.1.call-update) | async-done | bytes 3145744 | tf_op jit(solution)/shard_map/reduce_scatter | solution.py:26
  665.2 4.0 multiply_reduce_fusion.3
  671.1 171.9 %all-gather.9.cloned.1.call-done = bf16[384,16,1024]{2,1,0:T(8,128)(2,1)} async-done(((bf16[48,16,1024]{2,1,0:T(8,128)(2,1)}), bf16[384,16,1024]{2,1,0:T(8,128)(2,1)}) %all-gather.9.cloned.1.call-update) | async-done | bytes 12582928 | tf_op jit(solution)/shard_map/all_gather | solution.py:22
  843.0 11.2 broadcast_select_fusion
  854.2 166.1 %all-gather.7.cloned.1.call-done = bf16[384,16,1024]{2,0,1:T(8,128)(2,1)} async-done(((bf16[48,16,1024]{2,0,1:T(8,128)(2,1)}), bf16[384,16,1024]{2,0,1:T(8,128)(2,1)}) %all-gather.7.cloned.1.call-update) | async-done | bytes 12582928 | tf_op jit(solution)/shard_map/all_gather | solution.py:22
  1020.2 27.9 fusion.20
  1048.2 34.8 %fusion.29 = (bf16[384,16,1,512]{3,0,1,2:T(8,128)(2,1)}, bf16[384,16,1,512]{3,0,1,2:T(8,128)(2,1)}, bf16[384,16,512]{2,0,1:T(8,128)(2,1)}) fusion(f32[384,16,2,512]{3,0,2,1:T(8,128)} %fusion.20, bf16[16,512,1024]{2,1,0:T(8,128)(2,1)} %param.14, bf16[384,16,1024]{2,1,0:T(8,128)(2,1)} %broadcast_select_fusion), kind=kOutput, calls=%fused_computation.41 | convolution fusion | flops 6489636864 | bytes 73400320 | tf_op jit(solution)/shard_map/fpd,pkd->fpk/dot_general | solution.py:146
  1083.0 26.4 fusion.23
  1109.5 19.7 convolution_bitcast_fusion
  1129.2 382.2 %reduce-scatter.14.cloned.1.call-done = f32[48,16,1024]{2,0,1:T(8,128)} async-done(((f32[384,16,1024]{2,0,1:T(8,128)}), f32[48,16,1024]{2,0,1:T(8,128)}) %reduce-scatter.14.cloned.1.call-update) | async-done | bytes 3145744 | tf_op jit(solution)/shard_map/reduce_scatter | solution.py:26
  1514.9 403.2 %reduce-scatter.12.cloned.1.call-done = f32[48,16,1024]{2,0,1:T(8,128)} async-done(((f32[384,16,1024]{2,0,1:T(8,128)}), f32[48,16,1024]{2,0,1:T(8,128)}) %reduce-scatter.12.cloned.1.call-update) | async-done | bytes 3145744 | tf_op jit(solution)/shard_map/reduce_scatter | solution.py:26
  1918.1 5.4 multiply_convert_fusion.4
  1923.6 19.4 fusion.17
  1943.0 27.5 convert_bitcast_fusion
  1970.6 128.6 %all-gather.11.cloned.1.call-done = bf16[384,16,1024]{2,0,1:T(8,128)(2,1)} async-done(((bf16[48,16,1024]{2,0,1:T(8,128)(2,1)}), bf16[384,16,1024]{2,0,1:T(8,128)(2,1)}) %all-gather.11.cloned.1.call-update) | async-done | bytes 12582928 | tf_op jit(solution)/shard_map/all_gather | solution.py:22
  2099.3 8.9 convolution_convert_fusion
  2108.3 14.6 convolution_convert_fusion.1
  2122.9 5.7 copy.78
  2130.4 6.2 convert_bitcast_fusion.2
  2136.7 5.5 copy.83
  2144.8 7.8 multiply_reduce_fusion
  2159.0 5.6 copy.80
  2164.6 5.5 fusion.45
  2170.1 5.8 copy.81
  2180.5 13.3 convert_bitcast_fusion.1
  2193.9 15.2 convolution_bitcast_fusion.1
  2209.2 17.6 reduce-scatter.24.cloned.1.call-done
  2226.7 6.5 convert_element_type.119
  2235.2 229.2 %reduce-scatter.22.cloned.1.call-done = bf16[16,2,256,512]{2,3,1,0:T(8,128)(2,1)} async-done(((bf16[16,2,1024,512]{2,3,1,0:T(8,128)(2,1)}), bf16[16,2,256,512]{2,3,1,0:T(8,128)(2,1)}) %reduce-scatter.22.cloned.1.call-update) | async-done | bytes 8388624 | tf_op jit(solution)/shard_map/reduce_scatter | solution.py:39
  2464.4 13.4 copy.94
  2477.8 34.2 %reduce-scatter.20.cloned.1.call-done = bf16[16,128,256]{2,1,0:T(8,128)(2,1)} async-done(((bf16[16,128,1024]{2,1,0:T(8,128)(2,1)}), bf16[16,128,256]{2,1,0:T(8,128)(2,1)}) %reduce-scatter.20.cloned.1.call-update) | async-done | bytes 1048592 | tf_op jit(solution)/shard_map/reduce_scatter | solution.py:36
  2514.8 98.9 %reduce-scatter.18.cloned.1.call-done = bf16[16,3,256,128]{2,3,1,0:T(8,128)(2,1)} async-done(((bf16[16,3,1024,128]{2,3,1,0:T(8,128)(2,1)}), bf16[16,3,256,128]{2,3,1,0:T(8,128)(2,1)}) %reduce-scatter.18.cloned.1.call-update) | async-done | bytes 3145744 | tf_op jit(solution)/shard_map/reduce_scatter | solution.py:33
  2613.7 5.4 copy.93
  2619.1 401.9 %reduce-scatter.16.cloned.1.call-done = f32[48,16,1024]{2,0,1:T(8,128)} async-done(((f32[384,16,1024]{2,0,1:T(8,128)}), f32[48,16,1024]{2,0,1:T(8,128)}) %reduce-scatter.16.cloned.1.call-update) | async-done | bytes 3145744 | tf_op jit(solution)/shard_map/reduce_scatter | solution.py:26
  3021.1 4.6 fusion.42
  3026.3 6.1 fusion.41
  3034.4 10.5 reduce-scatter.26.cloned.1.call-done
  3045.0 38.4 %psum.7 = f32[2,16,256]{2,1,0:T(8,128)} all-reduce(bf16[2,16,256]{2,1,0:T(8,128)(2,1)} %reduce-scatter.26.cloned.1.call-done), channel_id=1, replica_groups=mesh['frames'=4,'mp'=8] {'mp'}, use_global_device_ids=true, to_apply=%region_18.19 | all-reduce | flops 8192 | bytes 49152 | tf_op jit(solution)/shard_map/psum | solution.py:180
  (106 shorter events, 46.6 us)
Async XLA Ops:
  7.2 187.4 %all-gather.5.cloned.1.call-start = ((), (), s32[]{:S(2)}) async-start(), calls=%async_computation.9 | async-start | bytes 14155776 | tf_op jit(solution)/shard_map/all_gather | solution.py:22
  10.0 0.9 copy-start.18
  10.9 0.6 copy-start.16
  10.9 1907.2 %copy-start.14 = (f32[16,1024]{1,0:T(8,128)}, f32[16,1024]{1,0:T(8,128)S(1)}, u32[]{:S(2)}) copy-start(f32[16,1024]{1,0:T(8,128)S(1)} %get-tuple-element.42) | copy-start | bytes 196612
  15.3 649.9 %reduce-scatter.10.cloned.1.call-start = ((), (), s32[]{:S(2)}) async-start(), calls=%async_computation.10 | async-start | bytes 28311552 | tf_op jit(solution)/shard_map/reduce_scatter | solution.py:26
  32.1 208.2 %copy-start.21 = (pred[16,16]{0,1:T(8,128)(4,1)}, pred[16,16]{0,1:T(8,128)(4,1)S(1)}, u32[]{:S(2)}) copy-start(pred[16,16]{0,1:T(8,128)(4,1)S(1)} %iota_compare_fusion) | copy-start | bytes 772
  225.7 14.6 copy-start.5
  237.5 2.8 copy-start
  240.3 0.8 copy-start.10
  248.6 14.5 copy-start.3
  263.2 579.8 %all-gather.9.cloned.1.call-start = ((), (), s32[]{:S(2)}) async-start(), calls=%async_computation.13 | async-start | bytes 14155776 | tf_op jit(solution)/shard_map/all_gather | solution.py:22
  263.9 756.3 %all-gather.7.cloned.1.call-start = ((), (), s32[]{:S(2)}) async-start(), calls=%async_computation.11 | async-start | bytes 14155776 | tf_op jit(solution)/shard_map/all_gather | solution.py:22
  669.2 1248.9 %copy-start.1 = (f32[48,16,1024]{2,0,1:T(8,128)}, f32[48,16,1024]{2,0,1:T(8,128)S(1)}, u32[]{:S(2)}) copy-start(f32[48,16,1024]{2,0,1:T(8,128)S(1)} %get-tuple-element.33) | copy-start | bytes 9437188
  671.0 840.4 %reduce-scatter.14.cloned.1.call-start = ((), (), s32[]{:S(2)}) async-start(), calls=%async_computation.14 | async-start | bytes 28311552 | tf_op jit(solution)/shard_map/reduce_scatter | solution.py:26
  1109.4 808.6 %reduce-scatter.12.cloned.1.call-start = ((), (), s32[]{:S(2)}) async-start(), calls=%async_computation.12 | async-start | bytes 28311552 | tf_op jit(solution)/shard_map/reduce_scatter | solution.py:26
  1129.2 970.1 %all-gather.11.cloned.1.call-start = ((), (), s32[]{:S(2)}) async-start(), calls=%async_computation.15 | async-start | bytes 14155776 | tf_op jit(solution)/shard_map/all_gather | solution.py:22
  1514.9 408.6 %copy-start.23 = (f32[48,16]{0,1:T(8,128)}, f32[48,16]{0,1:T(8,128)S(1)}, u32[]{:S(2)}) copy-start(f32[48,16]{0,1:T(8,128)S(1)} %broadcast_multiply_fusion.1) | copy-start | bytes 9220
  1923.5 303.2 %reduce-scatter.24.cloned.1.call-start = ((), (), s32[]{:S(2)}) async-start(), calls=%async_computation.20 | async-start | bytes 20971520 | tf_op jit(solution)/shard_map/reduce_scatter | solution.py:42
  1943.0 521.4 %reduce-scatter.22.cloned.1.call-start = ((), (), s32[]{:S(2)}) async-start(), calls=%async_computation.19 | async-start | bytes 41943040 | tf_op jit(solution)/shard_map/reduce_scatter | solution.py:39
  1970.5 128.7 %copy-start.4 = (bf16[384,16,2,64]{0,3,2,1:T(8,128)(2,1)S(1)}, bf16[384,16,2,64]{0,3,2,1:T(8,128)(2,1)}, u32[]{:S(2)}) copy-start(bf16[384,16,2,64]{0,3,2,1:T(8,128)(2,1)} %copy-done.3) | copy-start | bytes 4718596
  1970.6 541.5 %reduce-scatter.20.cloned.1.call-start = ((), (), s32[]{:S(2)}) async-start(), calls=%async_computation.18 | async-start | bytes 5242880 | tf_op jit(solution)/shard_map/reduce_scatter | solution.py:36
  2108.2 505.5 %reduce-scatter.18.cloned.1.call-start = ((), (), s32[]{:S(2)}) async-start(), calls=%async_computation.17 | async-start | bytes 15728640 | tf_op jit(solution)/shard_map/reduce_scatter | solution.py:33
  2122.9 7.5 copy-start.11
  2122.9 7.5 copy-start.22
  2128.6 1.8 copy-start.6
  2136.7 16.0 slice-start
  2144.8 7.8 slice-start.1
  2152.7 3.8 copy-start.9
  2154.8 1.7 copy-start.7
  2159.0 5.6 copy-start.8
  2170.1 10.4 copy-start.12
  2193.8 827.2 %reduce-scatter.16.cloned.1.call-start = ((), (), s32[]{:S(2)}) async-start(), calls=%async_computation.16 | async-start | bytes 28311552 | tf_op jit(solution)/shard_map/reduce_scatter | solution.py:26
  2209.1 24.1 copy-start.13
  2209.1 835.9 %reduce-scatter.26.cloned.1.call-start = ((), (), s32[]{:S(2)}) async-start(), calls=%async_computation.21 | async-start | bytes 81920 | tf_op jit(solution)/shard_map/reduce_scatter | solution.py:45
  2514.8 506.2 %copy-start.17 = (f32[16,1024]{1,0:T(8,128)S(1)}, f32[16,1024]{1,0:T(8,128)}, u32[]{:S(2)}) copy-start(f32[16,1024]{1,0:T(8,128)} %copy-done.16) | copy-start | bytes 196612
  2514.8 506.2 %copy-start.19 = (f32[48,16]{0,1:T(8,128)S(1)}, f32[48,16]{0,1:T(8,128)}, u32[]{:S(2)}) copy-start(f32[48,16]{0,1:T(8,128)} %copy-done.18) | copy-start | bytes 9220
  2619.1 406.5 %copy-start.20 = (bf16[16,1024]{1,0:T(8,128)(2,1)S(1)}, bf16[16,1024]{1,0:T(8,128)(2,1)}, u32[]{:S(2)}) copy-start(bf16[16,1024]{1,0:T(8,128)(2,1)} %get-tuple-element.28) | copy-start | bytes 98308
  2619.1 407.2 %copy-start.2 = (f32[48,16,1024]{2,0,1:T(8,128)S(1)}, f32[48,16,1024]{2,0,1:T(8,128)}, u32[]{:S(2)}) copy-start(f32[48,16,1024]{2,0,1:T(8,128)} %copy-done.1) | copy-start | bytes 9437188
  2619.1 407.2 %copy-start.15 = (f32[16,1024]{1,0:T(8,128)S(1)}, f32[16,1024]{1,0:T(8,128)}, u32[]{:S(2)}) copy-start(f32[16,1024]{1,0:T(8,128)} %copy-done.14) | copy-start | bytes 196612
  2619.1 407.2 %copy-start.24 = (f32[48,16]{0,1:T(8,128)S(1)}, f32[48,16]{0,1:T(8,128)}, u32[]{:S(2)}) copy-start(f32[48,16]{0,1:T(8,128)} %copy-done.23) | copy-start | bytes 9220
Sparse Core Ops, SparseCore 0:
  15.4 179.1 all-gather.4
  263.3 401.8 reduce-scatter.9
  667.4 175.5 all-gather.8
  845.6 174.6 all-gather.6
  1109.6 401.8 reduce-scatter.13
  1515.2 402.8 reduce-scatter.11
  1923.7 175.5 all-gather.10
  2102.4 124.2 reduce-scatter.23
  2229.5 234.8 reduce-scatter.21
  2467.5 44.5 reduce-scatter.19
  2514.7 99.0 reduce-scatter.17
  2617.5 403.5 reduce-scatter.15
  3026.4 18.4 reduce-scatter.25
where the time goes:
time: 3100 us; the launch traced here: 3090 us
  waiting for transfers between devices  2610 us (84%)
  matrix products  266 us (9%)
  local copies, waits for them, and re-layouts  99.4 us (3%)
  other arithmetic  62.3 us (2%)
  blocking collectives  38.4 us (1%)
    reduce_scatter x4, waiting for transfers between devices, group_total(): lax.psum_scatter(term_fn(jnp.int32(0), rows * lax.axis_size('mp')), 'mp',...  1590 us
    all_gather x4, waiting for transfers between devices, group_rows(): return lax.all_gather(values, 'mp', axis=0, tiled=True)  629 us
    reduce_scatter x1, waiting for transfers between devices, sum_all_grads(): lax.psum_scatter(grad_gu.astype(jnp.bfloat16), 'frames', scatter_dimensio...  229 us
    reduce_scatter x1, waiting for transfers between devices, sum_all_grads(): lax.psum_scatter(grad_qkv.astype(jnp.bfloat16), 'frames', scatter_dimensi...  98.9 us
  transfers between devices with their start and end apart: 13, of which 13 were waited for; matrix products, arithmetic and copies ran while one was open for 8% of the time, Pallas kernels for 0%

commit v1 on v0

v1 whole, which is shorter than its diff:
```python
import functools
import math

import jax
import jax.numpy as jnp
from jax import lax
from jax.experimental import pallas as pl
from jax.experimental.pallas import tpu as pltpu
from jax.sharding import PartitionSpec as P

HDIM = 64
EPSILON = 1e-05
Z_CHIPS = 4
FRAME_BLOCK = 16
CHUNKS = 4
VMEM_BYTES = 56 * 1024 * 1024

f32 = jnp.float32
bf16 = jnp.bfloat16


class Line:
    def __init__(self, total, n, stride):
        self.n = n
        self.stride = stride
        self.starts = [i for i in range(total) if (i // stride) % n == 0]

    def up(self, low, high):
        return [(s + i * self.stride, s + (i + 1) * self.stride) for s in self.starts for i in range(low, high)]

    def down(self, low, high):
        return [(s + (i + 1) * self.stride, s + i * self.stride) for s in self.starts for i in range(low, high)]

    def gather(self, own):
        n = self.n
        if n == 1:
            return [own]
        if n == 2:
            return [own, lax.ppermute(own, "mp", self.up(0, 1) + self.down(0, 1))]
        ups, downs = [own], [own]
        for k in range(1, n):
            ups.append(lax.ppermute(ups[-1], "mp", self.up(k - 1, n - 1)))
            downs.append(lax.ppermute(downs[-1], "mp", self.down(0, n - k)))
        return [own] + [ups[k] + downs[n - k] for k in range(1, n)]

    def reduce(self, term):
        n = self.n
        if n == 1:
            return [term(0)]
        if n == 2:
            return [term(0), lax.ppermute(term(1).astype(bf16), "mp", self.up(0, 1) + self.down(0, 1)).astype(f32)]
        up = down = None
        for s in range(1, n):
            send_up = term(s) if up is None else term(s) + up.astype(f32)
            send_down = term(n - s) if down is None else term(n - s) + down.astype(f32)
            up = lax.ppermute(send_up.astype(bf16), "mp", self.up(0, min(s, n - 1)))
            down = lax.ppermute(send_down.astype(bf16), "mp", self.down(n - 1 - s, n - 1))
        return [term(0), up.astype(f32), down.astype(f32)]


class Group:
    def __init__(self, size):
        self.nz = math.gcd(size, Z_CHIPS)
        self.ny = size // self.nz
        self.z = Line(size, self.nz, self.ny)
        self.y = Line(size, self.ny, 1)

    def gather(self, own, z_first):
        if z_first:
            column = jnp.stack(self.z.gather(own), axis=1)
            return jnp.stack(self.y.gather(column), axis=1)
        row = jnp.stack(self.y.gather(own), axis=1)
        return jnp.stack(self.z.gather(row), axis=2)

    def reduce(self, parts, z_first):
        if not z_first:
            if self.ny == 2:
                got = lax.ppermute(parts[1], "mp", self.y.up(0, 1) + self.y.down(0, 1))
                columns = [parts[0], got]

                def term(k):
                    return columns[0][:, k].astype(f32) + columns[1][:, k].astype(f32)

            else:
                terms = self.y.reduce(lambda k: parts[k].astype(f32))

                def term(k):
                    return sum(t[:, k] for t in terms)

            return sum(self.z.reduce(term))

        def row(k):
            return jnp.stack([part[:, k] for part in parts], axis=1).astype(f32)

        terms = self.z.reduce(row)
        return sum(self.y.reduce(lambda k: sum(t[:, k] for t in terms)))


def frames_sum(keep, send, size):
    step = 1
    while True:
        got = lax.ppermute(send, "frames", [(i, i ^ step) for i in range(size)])
        total = keep.astype(f32) + got.astype(f32)
        step *= 2
        if step == size:
            return total[:, 0]
        keep, send = total[:, 0::2], total[:, 1::2].astype(send.dtype)


def dot(a, b, dims):
    return lax.dot_general(a, b, (dims, ((), ())), preferred_element_type=f32)


NN = ((1,), (0,))
NT = ((1,), (1,))
TN = ((0,), (0,))


def params():
    return pltpu.CompilerParams(vmem_limit_bytes=VMEM_BYTES)


def cost(flops, nbytes):
    return pl.CostEstimate(flops=int(flops), bytes_accessed=int(nbytes), transcendentals=0)


def qkv_kernel(x_ref, w_ref, q_ref, k_ref, v_ref):
    x = x_ref[0]
    for c, out in enumerate((q_ref, k_ref, v_ref)):
        out[0] = dot(x, w_ref[0, c], NN).astype(bf16)


def qkv(x, weight, base):
    count, rows, depth = x.shape
    width = weight.shape[-1]
    out = jax.ShapeDtypeStruct((count, rows, width), bf16)
    return pl.pallas_call(
        qkv_kernel,
        grid=(count,),
        in_specs=[
            pl.BlockSpec((1, rows, depth), lambda i: (i, 0, 0)),
            pl.BlockSpec((1, 3, depth, width), lambda i: (base + i, 0, 0, 0)),
        ],
        out_specs=[pl.BlockSpec((1, rows, width), lambda i: (i, 0, 0))] * 3,
        out_shape=[out] * 3,
        compiler_params=params(),
        cost_estimate=cost(6 * count * rows * depth * width, 2 * count * depth * (rows + 3 * width)),
        name="qkv",
    )(x, weight)


def head_masks(rows, width):
    lane = lax.broadcasted_iota(jnp.int32, (rows, width), 1)
    return [(lane >= h * HDIM) & (lane < (h + 1) * HDIM) for h in range(width // HDIM)]


def attention_mask(count, base, columns):
    rows = count * FRAME_BLOCK
    row = lax.broadcasted_iota(jnp.int32, (rows, columns), 0)
    column = lax.broadcasted_iota(jnp.int32, (rows, columns), 1)
    same = (row % FRAME_BLOCK) == (column % FRAME_BLOCK)
    return same & (column // FRAME_BLOCK <= row // FRAME_BLOCK + base)


def block_of(refs, rows):
    pieces = [ref[:, rows, :] for ref in refs]
    pieces = [p.reshape(p.shape[0] * p.shape[1], p.shape[2]) for p in pieces]
    return pieces[0] if len(pieces) == 1 else jnp.concatenate(pieces, axis=0)


def softmax(scores):
    top = jnp.max(scores, axis=-1, keepdims=True)
    raised = jnp.exp(scores - top)
    return raised / jnp.sum(raised, axis=-1, keepdims=True)


def pick(masks, values):
    out = values[0]
    for mask, value in zip(masks[1:], values[1:]):
        out = jnp.where(mask, value, out)
    return out


def attend_kernel(base, n_kv, ny, q_ref, *refs):
    k_refs, v_refs = refs[:n_kv], refs[n_kv : 2 * n_kv]
    w_ref = refs[2 * n_kv]
    mixed_ref = refs[2 * n_kv + 1]
    part_refs = refs[2 * n_kv + 2 :]
    count, rows, width = q_ref.shape
    columns = sum(ref.shape[0] for ref in k_refs) * FRAME_BLOCK
    step = pl.program_id(0)

    @pl.when(step == 0)
    def _():
        heads = head_masks(count * FRAME_BLOCK, width)
        allowed = attention_mask(count, base, columns)

        def one(b):
            at = pl.ds(pl.multiple_of(b * FRAME_BLOCK, FRAME_BLOCK), FRAME_BLOCK)
            queries = block_of([q_ref], at) * HDIM ** (-0.5)
            keys, values = block_of(k_refs, at), block_of(v_refs, at)
            outs = []
            for head in heads:
                mine = jnp.where(head, queries, jnp.zeros_like(queries))
                scores = jnp.where(allowed, dot(mine, keys, NT), -1e30)
                outs.append(dot(softmax(scores).astype(bf16), values, NN))
            mixed_ref[:, at, :] = pick(heads, outs).astype(bf16).reshape(count, FRAME_BLOCK, width)

        lax.fori_loop(0, rows // FRAME_BLOCK, lambda b, c: (one(b), c)[1], 0, unroll=4)

    out = dot(mixed_ref[step], w_ref[0], NN)
    span = rows // ny
    for y, part in enumerate(part_refs):
        part[0] = out[y * span : (y + 1) * span].astype(bf16)


def attend(q, ks, vs, weight, base, ny):
    count, rows, width = q.shape
    depth = weight.shape[-1]
    whole = pl.BlockSpec((count, rows, width), lambda i: (0, 0, 0))
    part = jax.ShapeDtypeStruct((count, rows // ny, depth), bf16)
    n_kv = len(ks)
    return pl.pallas_call(
        functools.partial(attend_kernel, base, n_kv, ny),
        grid=(count,),
        in_specs=[whole] * (1 + 2 * n_kv) + [pl.BlockSpec((1, width, depth), lambda i: (base + i, 0, 0))],
        out_specs=[whole] + [pl.BlockSpec((1, rows // ny, depth), lambda i: (i, 0, 0))] * ny,
        out_shape=[jax.ShapeDtypeStruct(q.shape, bf16)] + [part] * ny,
        compiler_params=params(),
        cost_estimate=cost(4 * count * rows * depth * width, 2 * count * rows * (depth + (2 + 2 * n_kv) * width)),
        name="attend",
    )(q, *ks, *vs, weight)


def gradient_pieces(size, depth):
    return size if size > 1 and (depth // size) % 128 == 0 else 1


def piece_at(piece, mine, span):
    return pl.ds(pl.multiple_of((piece ^ mine) * span, span), span)


def ffn_kernel(ny, pieces, mine_ref, x_ref, g_ref, gu_ref, dn_ref, *refs):
    outs, backs = refs[:ny], refs[ny : 2 * ny]
    gain_ref = refs[2 * ny]
    grads = refs[2 * ny + 1 :]
    rows, depth = x_ref.shape[1:]
    span = rows // ny
    x, g = x_ref[0], g_ref[0]
    gate = dot(x, gu_ref[0, 0], NN)
    up = dot(x, gu_ref[0, 1], NN)
    grad_act = dot(g, dn_ref[0], NT)
    sigma = 1.0 / (1.0 + jnp.exp(-gate))
    silu = gate * sigma
    act = (silu * up).astype(bf16)
    grad_gate = (grad_act * up * sigma * (1.0 + gate * (1.0 - sigma))).astype(bf16)
    grad_up = (grad_act * silu).astype(bf16)
    out = dot(act, dn_ref[0], NN)
    for y in range(ny):
        outs[y][0] = out[y * span : (y + 1) * span].astype(bf16)
    back = dot(grad_gate, gu_ref[0, 0], NT) + dot(grad_up, gu_ref[0, 1], NT)
    for y in range(ny):
        backs[y][0] = back[y * span : (y + 1) * span].astype(bf16)
    gain_ref[0] = jnp.sum(back * x.astype(f32), axis=0, keepdims=True)
    if pieces == 1:
        grads[0][0, 0] = dot(x, grad_gate, TN).astype(bf16)
        grads[0][0, 1] = dot(x, grad_up, TN).astype(bf16)
        grads[1][0] = dot(act, g, TN).astype(bf16)
        return
    mine = mine_ref[0]
    width = depth // pieces
    for r in range(pieces):
        at = piece_at(r, mine, width)
        gu_out, dn_out = grads[r % 2], grads[2 + r % 2]
        columns = x_ref[0, :, at]
        gu_out[0, r // 2, 0] = dot(columns, grad_gate, TN).astype(bf16)
        gu_out[0, r // 2, 1] = dot(columns, grad_up, TN).astype(bf16)
        dn_out[0, r // 2] = dot(act, g_ref[0, :, at], TN).astype(bf16)


def split_specs(shape, pieces, axis):
    if pieces == 1:
        block = (1,) + shape[1:]
        return [pl.BlockSpec(block, lambda i: (i,) + (0,) * (len(block) - 1))], [jax.ShapeDtypeStruct(shape, bf16)]
    rest = list(shape[1:])
    rest[axis - 1] //= pieces
    block = (1, pieces // 2) + tuple(rest)
    spec = pl.BlockSpec(block, lambda i: (i,) + (0,) * (len(block) - 1))
    return [spec] * 2, [jax.ShapeDtypeStruct((shape[0],) + block[1:], bf16)] * 2


def ffn(x, g, gate_up, down, base, ny, frames, mine):
    count, rows, depth = x.shape
    width = down.shape[1]
    pieces = gradient_pieces(frames, depth)
    part = jax.ShapeDtypeStruct((count, rows // ny, depth), bf16)
    part_spec = pl.BlockSpec((1, rows // ny, depth), lambda i: (i, 0, 0))
    row_spec = pl.BlockSpec((1, rows, depth), lambda i: (i, 0, 0))
    gu_specs, gu_shapes = split_specs((count, 2, depth, width), pieces, 2)
    dn_specs, dn_shapes = split_specs((count, width, depth), pieces, 2)
    out = pl.pallas_call(
        functools.partial(ffn_kernel, ny, pieces),
        grid=(count,),
        in_specs=[
            pl.BlockSpec(memory_space=pltpu.SMEM),
            row_spec,
            row_spec,
            pl.BlockSpec((1, 2, depth, width), lambda i: (base + i, 0, 0, 0)),
            pl.BlockSpec((1, width, depth), lambda i: (base + i, 0, 0)),
        ],
        out_specs=[part_spec] * (2 * ny) + [pl.BlockSpec((1, 1, depth), lambda i: (i, 0, 0))] + gu_specs + dn_specs,
        out_shape=[part] * (2 * ny) + [jax.ShapeDtypeStruct((count, 1, depth), f32)] + gu_shapes + dn_shapes,
        compiler_params=params(),
        cost_estimate=cost(18 * count * rows * depth * width, 2 * count * depth * (4 * rows + 6 * width)),
        name="ffn",
    )(mine, x, g, gate_up, down)
    n = len(gu_specs)
    return out[:ny], out[ny : 2 * ny], out[2 * ny], out[2 * ny + 1 : 2 * ny + 1 + n], out[2 * ny + 1 + n :]


def attend_back_kernel(base, n_kv, first, ny, pieces, mine_ref, ga_ref, gp_ref, x_ref, q_ref, *refs):
    refs = list(refs)

    def take(n):
        got = refs[:n]
        del refs[:n]
        return got

    k_refs, v_refs = take(n_kv), take(n_kv)
    (mixed_ref, ow_all_ref, iw_ref) = take(3)
    dk_in = dv_in = ()
    if not first:
        dk_in, dv_in = take(n_kv), take(n_kv)
    part_refs = take(ny)
    (gain_ref,) = take(1)
    n_out = 1 if pieces == 1 else 2
    iw_grads, ow_grads = take(n_out), take(n_out)
    dk_out, dv_out = take(n_kv - 1), take(n_kv - 1)
    gmixed_ref, gproj_ref = take(2)
    count, rows, width = q_ref.shape
    columns = n_kv * count * FRAME_BLOCK
    block = count * FRAME_BLOCK
    step = pl.program_id(0)

    @pl.when(step == 0)
    def _():
        for p in range(count):
            gmixed_ref[p] = dot(ga_ref[p], ow_all_ref[p], NT).astype(bf16)
        heads = head_masks(block, width)
        allowed = attention_mask(count, base, columns)
        factor = HDIM ** (-0.5)

        def one(b):
            at = pl.ds(pl.multiple_of(b * FRAME_BLOCK, FRAME_BLOCK), FRAME_BLOCK)
            queries = block_of([q_ref], at) * factor
            grad_mixed = block_of([gmixed_ref], at)
            keys, values = block_of(k_refs, at), block_of(v_refs, at)
            dqs, dk, dv = [], None, None
            for head in heads:
                my_q = jnp.where(head, queries, jnp.zeros_like(queries))
                my_g = jnp.where(head, grad_mixed, jnp.zeros_like(grad_mixed))
                probs = softmax(jnp.where(allowed, dot(my_q, keys, NT), -1e30))
                grad_probs = dot(my_g, values, NT)
                weighted = probs * grad_probs
                grad_scores = (weighted - probs * jnp.sum(weighted, axis=-1, keepdims=True)).astype(bf16)
                dqs.append(dot(grad_scores, keys, NN))
                more_k = dot(grad_scores, my_q, TN)
                more_v = dot(probs.astype(bf16), my_g, TN)
                dk = more_k if dk is None else dk + more_k
                dv = more_v if dv is None else dv + more_v
            gproj_ref[:, 0, at, :] = (pick(heads, dqs) * factor).astype(bf16).reshape(count, FRAME_BLOCK, width)
            for c, total, earlier, later in ((1, dk, dk_in, dk_out), (2, dv, dv_in, dv_out)):
                for j in range(n_kv):
                    piece = total[j * block : (j + 1) * block].reshape(count, FRAME_BLOCK, width)
                    if not first:
                        piece = piece + earlier[j][:, at, :]
                    if j < n_kv - 1:
                        later[j][:, at, :] = piece
                    else:
                        gproj_ref[:, c, at, :] = piece.astype(bf16)

        lax.fori_loop(0, rows // FRAME_BLOCK, lambda b, c: (one(b), c)[1], 0, unroll=2)

    grads = [gproj_ref[step, c] for c in range(3)]
    back = dot(grads[0], iw_ref[0, 0], NT) + dot(grads[1], iw_ref[0, 1], NT) + dot(grads[2], iw_ref[0, 2], NT)
    span = rows // ny
    for y, part in enumerate(part_refs):
        part[0] = back[y * span : (y + 1) * span].astype(bf16)
    gain_ref[0] = jnp.sum(back * x_ref[0].astype(f32), axis=0, keepdims=True)
    mixed = mixed_ref[0]
    if pieces == 1:
        for c in range(3):
            iw_grads[0][0, c] = dot(x_ref[0], grads[c], TN).astype(bf16)
        ow_grads[0][0] = dot(mixed, gp_ref[0], TN).astype(bf16)
        return
    mine = mine_ref[0]
    depth = x_ref.shape[2]
    for r in range(pieces):
        at = piece_at(r, mine, depth // pieces)
        columns = x_ref[0, :, at]
        for c in range(3):
            iw_grads[r % 2][0, r // 2, c] = dot(columns, grads[c], TN).astype(bf16)
        ow_grads[r % 2][0, r // 2] = dot(mixed, gp_ref[0, :, at], TN).astype(bf16)


def attend_back(grad_rows, x, q, ks, vs, mixed, out_weight, in_weight, dks, dvs, base, ny, frames, mine):
    count, rows, depth = x.shape
    width = q.shape[-1]
    pieces = gradient_pieces(frames, depth)
    n_kv = len(ks)
    first = not dks
    whole = pl.BlockSpec((count, rows, width), lambda i: (0, 0, 0))
    row_spec = pl.BlockSpec((1, rows, depth), lambda i: (i, 0, 0))
    chunk = base // count
    part = jax.ShapeDtypeStruct((count, rows // ny, depth), bf16)
    part_spec = pl.BlockSpec((1, rows // ny, depth), lambda i: (i, 0, 0))
    iw_specs, iw_shapes = split_specs((count, 3, depth, width), pieces, 2)
    ow_specs, ow_shapes = split_specs((count, width, depth), pieces, 2)
    total = jax.ShapeDtypeStruct((count, rows, width), f32)
    out = pl.pallas_call(
        functools.partial(attend_back_kernel, base, n_kv, first, ny, pieces),
        grid=(count,),
        in_specs=[
            pl.BlockSpec(memory_space=pltpu.SMEM),
            pl.BlockSpec((count, rows, depth), lambda i: (0, 0, 0)),
            row_spec,
            row_spec,
        ]
        + [whole] * (1 + 2 * n_kv)
        + [
            pl.BlockSpec((1, rows, width), lambda i: (i, 0, 0)),
            pl.BlockSpec((count, width, depth), lambda i: (chunk, 0, 0)),
            pl.BlockSpec((1, 3, depth, width), lambda i: (base + i, 0, 0, 0)),
        ]
        + [whole] * (len(dks) + len(dvs)),
        out_specs=[part_spec] * ny
        + [pl.BlockSpec((1, 1, depth), lambda i: (i, 0, 0))]
        + iw_specs
        + ow_specs
        + [whole] * (2 * (n_kv - 1)),
        out_shape=[part] * ny
        + [jax.ShapeDtypeStruct((count, 1, depth), f32)]
        + iw_shapes
        + ow_shapes
        + [total] * (2 * (n_kv - 1)),
        scratch_shapes=[pltpu.VMEM((count, rows, width), bf16), pltpu.VMEM((count, 3, rows, width), bf16)],
        compiler_params=params(),
        cost_estimate=cost(16 * count * rows * depth * width, 2 * count * rows * (4 * depth + 8 * n_kv * width)),
        name="attend_back",
    )(mine, grad_rows, grad_rows, x, q, *ks, *vs, mixed, out_weight, in_weight, *dks, *dvs)
    out = list(out)
    n = len(iw_specs)
    parts, gain = out[:ny], out[ny]
    iw, ow = out[ny + 1 : ny + 1 + n], out[ny + 1 + n : ny + 1 + 2 * n]
    rest = out[ny + 1 + 2 * n :]
    return parts, gain, iw, ow, rest[: n_kv - 1], rest[n_kv - 1 :]


def inverse_rms(values):
    return lax.rsqrt(jnp.mean(values * values, axis=-1, keepdims=True) + EPSILON)


def norm_back(grad_normed, normed, factor, gain):
    scaled = grad_normed * gain
    return factor * (scaled - normed * jnp.mean(scaled * normed, axis=-1, keepdims=True))


def body(inputs, counts, norm_gains, in_weight, out_weight, gate_up, down_weight, cotangent):
    frames, group_size = lax.axis_size("frames"), lax.axis_size("mp")
    group = Group(group_size)
    ny, nz = group.ny, group.nz
    local, positions, depth = inputs.shape
    rows = local * group_size
    size = positions // CHUNKS
    ids = lax.axis_index("mp") * local + jnp.arange(local)
    mask = (ids < counts[0]).astype(f32)[None, :, None]
    mine = lax.axis_index("frames").astype(jnp.int32)[None]
    x_major = jnp.swapaxes(inputs, 0, 1)
    g_major = jnp.swapaxes(cotangent, 0, 1)
    gains = norm_gains[:, :, None, :]

    def at(c):
        return slice(c * size, (c + 1) * size)

    def gathered(own, z_first):
        return group.gather(own, z_first).reshape(size, rows, depth)

    def reduced(parts, z_first):
        return group.reduce([p.reshape(size, nz, local, depth) for p in parts], z_first)

    def summed(grads):
        if len(grads) == 1:
            return lax.psum_scatter(grads[0], "frames", scatter_dimension=grads[0].ndim - 1, tiled=True).astype(f32)
        return frames_sum(grads[0], grads[1], frames)

    def summed_middle(grads):
        if len(grads) == 1:
            return lax.psum_scatter(grads[0], "frames", scatter_dimension=2, tiled=True).astype(f32)
        return frames_sum(grads[0], grads[1], frames)

    order = list(range(CHUNKS))[::-1]
    attn_in, qs, ks, vs = {}, {}, {}, {}
    for c in order:
        residual = x_major[at(c)].astype(f32)
        own = (residual * inverse_rms(residual) * gains[0, at(c)]).astype(bf16)
        attn_in[c] = gathered(own, True)
        qs[c], ks[c], vs[c] = qkv(attn_in[c], in_weight, c * size)

    outputs, input_grads = {}, {}
    g_in, g_out, g_gu, g_dn, gain_terms = {}, {}, {}, {}, {}
    dks, dvs = [], []
    for c in order:
        base = c * size
        gain_first, gain_second = gains[0, at(c)], gains[1, at(c)]
        residual = x_major[at(c)].astype(f32)
        gy = g_major[at(c)].astype(f32)
        grad_rows = gathered((mask * gy).astype(bf16), c % 2 == 0)
        earlier_k, earlier_v = [ks[j] for j in range(c + 1)], [vs[j] for j in range(c + 1)]
        mixed, *parts = attend(qs[c], earlier_k, earlier_v, out_weight, base, ny)
        hmid = residual + mask * reduced(parts, False)
        scale_second = inverse_rms(hmid)
        normed_second = hmid * scale_second
        ffn_rows = gathered((normed_second * gain_second).astype(bf16), True)
        out_parts, back_parts, gain_back, grad_gu, grad_dn = ffn(
            ffn_rows, grad_rows, gate_up, down_weight, base, ny, frames, mine
        )
        grad_ffn_in = reduced(back_parts, False)
        grad_mid = gy + norm_back(grad_ffn_in, normed_second, scale_second, gain_second)
        grad_attn = gathered((mask * grad_mid).astype(bf16), True)
        outputs[c] = (hmid + mask * reduced(out_parts, True)).astype(bf16)
        back, gain_front, grad_iw, grad_ow, dks, dvs = attend_back(
            grad_attn, attn_in[c], qs[c], earlier_k, earlier_v, mixed, out_weight, in_weight,
            dks, dvs, base, ny, frames, mine,
        )
        grad_attn_in = reduced(back, c % 2 == 1)
        scale_first = inverse_rms(residual)
        input_grads[c] = (
            grad_mid + norm_back(grad_attn_in, residual * scale_first, scale_first, gain_first)
        ).astype(bf16)
        gain_terms[c] = jnp.stack([gain_front[:, 0] / norm_gains[0, at(c)], gain_back[:, 0] / norm_gains[1, at(c)]])
        g_gu[c], g_dn[c] = summed_middle(grad_gu), summed(grad_dn)
        g_in[c], g_out[c] = summed_middle(grad_iw), summed(grad_ow)

    def joined(pieces, axis=0):
        return jnp.concatenate([pieces[c] for c in range(CHUNKS)], axis=axis)

    terms = lax.psum_scatter(joined(gain_terms, 1), "frames", scatter_dimension=2, tiled=True)
    step = 1
    while step < group_size:
        terms = terms + lax.ppermute(terms, "mp", [(i, i ^ step) for i in range(group_size)])
        step *= 2
    return (
        jnp.swapaxes(joined(outputs), 0, 1),
        jnp.swapaxes(joined(input_grads), 0, 1),
        joined(g_in),
        joined(g_out),
        joined(g_gu),
        joined(g_dn),
        terms,
    )


def solution(mesh):
    placed = (
        P(("frames", "mp"), None, None),
        P("frames"),
        P(),
        P(None, None, None, "mp"),
        P(None, "mp", None),
        P(None, None, None, "mp"),
        P(None, "mp", None),
        P(("frames", "mp"), None, None),
    )
    return jax.shard_map(
        body,
        mesh=mesh,
        in_specs=placed,
        out_specs=(
            P(("frames", "mp"), None, None),
            P(("frames", "mp"), None, None),
            P(None, None, "frames", "mp"),
            P(None, "mp", "frames"),
            P(None, None, "frames", "mp"),
            P(None, "mp", "frames"),
            P(None, None, "frames"),
        ),
        check_vma=False,
    )
```

time: 3100 us -> 2160 us (0.70)
  waiting for transfers between devices: 2610 us -> 761 us
  starting transfers between devices: 0.71 us -> 548 us
  Pallas kernels: 0 us -> 330 us
  matrix products: 266 us -> 0 us
  other arithmetic: 62.3 us -> 309 us
  local copies, waits for them, and re-layouts: 99.4 us -> 175 us
  blocking collectives: 38.4 us -> 0 us
    reduce_scatter x9 -> x0, waiting for transfers between devices: 1980 us -> none  [the longest x4 1590 us: group_total(): lax.psum_scatter(term_fn(jnp.int32(0), rows * lax.axis_size('mp')), 'mp',...]
    ppermute x0 -> x259, waiting for transfers between devices: none -> 742 us  [the longest x48 221 us: gather(): downs.append(lax.ppermute(downs[-1], 'mp', self.down(0, n - k)))]
    all_gather x4 -> x0, waiting for transfers between devices: 629 us -> none  [group_rows(): return lax.all_gather(values, 'mp', axis=0, tiled=True)]
    ppermute x0 -> x259, starting transfers between devices: none -> 548 us  [the longest x48 233 us: reduce(): up = lax.ppermute(send_up.astype(bf16), 'mp', self.up(0, min(s, n - 1)))]
    pallas_call x0 -> x16, Pallas kernels: none -> 330 us  [the longest x4 134 us: attend_back(): pl.pallas_call(functools.partial(attend_back_kernel, base, n_kv, first, n...]
    dot_general x17 -> x0, matrix products: 252 us -> none  [the longest x1 34.8 us: body(): jnp.einsum('fpd,pkd->fpk', grad_ffn, down_weight, preferred_element_type=...]
    another operation x1 -> x99, other arithmetic: 0.64 us -> 133 us  [the longest x28 64.9 us: gather(): return jnp.stack(self.y.gather(column), axis=1)]
    convert_element_type x9 -> x83, other arithmetic: 32.8 us -> 88.8 us  [the longest x42 51.6 us: reduce(): up = lax.ppermute(send_up.astype(bf16), 'mp', self.up(0, min(s, n - 1)))]
  transfers between devices with their start and end apart: 13 -> 260, of which waited for: 13 -> 92; matrix products, arithmetic and copies ran while one was open for 8% -> 21% of each run, Pallas kernels for 0% -> 14%
where the time goes in v1:
time: 2160 us; the launch traced here: 2140 us
  waiting for transfers between devices  761 us (35%)
  starting transfers between devices  548 us (25%)
  Pallas kernels  330 us (15%)
  other arithmetic  309 us (14%)
  local copies, waits for them, and re-layouts  175 us (8%)
    ppermute x48, starting transfers between devices, reduce(): up = lax.ppermute(send_up.astype(bf16), 'mp', self.up(0, min(s, n - 1)))  233 us
    ppermute x48, waiting for transfers between devices, gather(): downs.append(lax.ppermute(downs[-1], 'mp', self.down(0, n - k)))  221 us
    ppermute x16, waiting for transfers between devices, gather(): return [own, lax.ppermute(own, 'mp', self.up(0, 1) + self.down(0, 1))]  179 us
    pallas_call x4, Pallas kernels, attend_back(): pl.pallas_call(functools.partial(attend_back_kernel, base, n_kv, first, n...  134 us
    ppermute x48, starting transfers between devices, gather(): ups.append(lax.ppermute(ups[-1], 'mp', self.up(k - 1, n - 1)))  130 us
    ppermute x10, waiting for transfers between devices, reduce(): got = lax.ppermute(parts[1], 'mp', self.y.up(0, 1) + self.y.down(0, 1))  116 us
    pallas_call x4, Pallas kernels, ffn(): pl.pallas_call(functools.partial(ffn_kernel, ny, pieces), grid=(count,),...  87.3 us
    pallas_call x4, Pallas kernels, attend(): pl.pallas_call(functools.partial(attend_kernel, base, n_kv, ny), grid=(co...  84.3 us
  transfers between devices with their start and end apart: 260, of which 92 were waited for; matrix products, arithmetic and copies ran while one was open for 21% of the time, Pallas kernels for 14%

profile of v1, /device:TPU:0, one launch (start us, length us, event | category | flops | bytes accessed | tf_op | source)
XLA Modules:
  0.0 2142.6 jit_solution(11781179108005088080)
XLA Ops:
  76.1 23.1 %collective-permute-done.73 = bf16[4,48,1024]{2,0,1:T(4,128)(2,1)S(1)} collective-permute-done((bf16[4,48,1024]{2,0,1:T(4,128)(2,1)}, bf16[4,48,1024]{2,0,1:T(4,128)(2,1)S(1)}, u32[]{:S(2)}, u32[]{:S(2)}) %collective-permute-start.73) | collective-permute-done | bytes 393248 | tf_op jit(solution)/shard_map/ppermute | solution.py:43
  131.5 12.4 collective-permute-done.59
  153.3 28.8 %collective-permute-done.41 = bf16[4,4,48,1024]{3,0,2,1:T(4,128)(2,1)S(1)} collective-permute-done((bf16[4,4,48,1024]{3,0,2,1:T(4,128)(2,1)S(1)}, bf16[4,4,48,1024]{3,0,2,1:T(4,128)(2,1)S(1)}, u32[]{:S(2)}, u32[]{:S(2)}) %collective-permute-start.41) | collective-permute-done | bytes 1572896 | tf_op jit(solution)/shard_map/ppermute | solution.py:39
  186.9 24.5 %collective-permute-done.6 = bf16[4,4,48,1024]{3,0,2,1:T(4,128)(2,1)S(1)} collective-permute-done((bf16[4,4,48,1024]{3,0,2,1:T(4,128)(2,1)S(1)}, bf16[4,4,48,1024]{3,0,2,1:T(4,128)(2,1)S(1)}, u32[]{:S(2)}, u32[]{:S(2)}) %collective-permute-start.6) | collective-permute-done | bytes 1572896 | tf_op jit(solution)/shard_map/ppermute | solution.py:39
  228.5 19.8 attend.4
  258.4 22.1 %attend.6 = (bf16[4,384,128]{2,1,0:T(8,128)(2,1)}, bf16[4,192,1024]{2,1,0:T(8,128)(2,1)}, bf16[4,192,1024]{2,1,0:T(8,128)(2,1)}) custom-call(bf16[4,384,128]{2,1,0:T(8,128)(2,1)} %get-tuple-element.121.q_ref, bf16[4,384,128]{2,1,0:T(8,128)(2,1)} %get-tuple-element.108.refs_0_, bf16[4,384,128]{2,1,0:T(8,128)(2,1)} %get-tuple-element.115.refs_1_, ...), custom_call_target="tpu_custom_call" | custom-call | flops 805306368 | bytes 6291456 | tf_op jit(solution)/shard_map/attend/pallas_call | solution.py:223
  286.0 20.8 attend.5
  325.1 26.7 %collective-permute-done.42 = bf16[4,4,48,1024]{3,0,2,1:T(4,128)(2,1)S(1)} collective-permute-done((bf16[4,4,48,1024]{3,0,2,1:T(4,128)(2,1)S(1)}, bf16[4,4,48,1024]{3,0,2,1:T(4,128)(2,1)S(1)}, u32[]{:S(2)}, u32[]{:S(2)}) %collective-permute-start.42) | collective-permute-done | bytes 1572896 | tf_op jit(solution)/shard_map/ppermute | solution.py:78
  497.3 13.1 collective-permute-done.52
  533.8 24.9 %collective-permute-done.55 = bf16[4,4,48,1024]{3,0,2,1:T(4,128)(2,1)S(1)} collective-permute-done((bf16[4,4,48,1024]{3,0,2,1:T(4,128)(2,1)S(1)}, bf16[4,4,48,1024]{3,0,2,1:T(4,128)(2,1)S(1)}, u32[]{:S(2)}, u32[]{:S(2)}) %collective-permute-start.55) | collective-permute-done | bytes 1572896 | tf_op jit(solution)/shard_map/ppermute | solution.py:39
  563.5 23.9 %collective-permute-done.111 = bf16[4,4,48,1024]{3,0,2,1:T(4,128)(2,1)S(1)} collective-permute-done((bf16[4,4,48,1024]{3,0,2,1:T(4,128)(2,1)S(1)}, bf16[4,4,48,1024]{3,0,2,1:T(4,128)(2,1)S(1)}, u32[]{:S(2)}, u32[]{:S(2)}) %collective-permute-start.111) | collective-permute-done | bytes 1572896 | tf_op jit(solution)/shard_map/ppermute | solution.py:39
  598.3 21.5 %attend.7 = (bf16[4,384,128]{2,1,0:T(8,128)(2,1)}, bf16[4,192,1024]{2,1,0:T(8,128)(2,1)}, bf16[4,192,1024]{2,1,0:T(8,128)(2,1)}) custom-call(bf16[4,384,128]{2,1,0:T(8,128)(2,1)} %get-tuple-element.128.q_ref, bf16[4,384,128]{2,1,0:T(8,128)(2,1)} %get-tuple-element.108.refs_0_, bf16[4,384,128]{2,1,0:T(8,128)(2,1)} %get-tuple-element.115.refs_1_, ...), custom_call_target="tpu_custom_call" | custom-call | flops 805306368 | bytes 7077888 | tf_op jit(solution)/shard_map/attend/pallas_call | solution.py:223
  625.1 22.0 %ffn.5 = (bf16[4,192,1024]{2,1,0:T(8,128)(2,1)}, bf16[4,192,1024]{2,1,0:T(8,128)(2,1)}, bf16[4,192,1024]{2,1,0:T(8,128)(2,1)}, bf16[4,192,1024]{2,1,0:T(8,128)(2...) custom-call(s32[1]{0:T(128)} %bitcast.20.mine_ref, ...), custom_call_target="tpu_custom_call" | custom-call | flops 14495514624 | bytes 37748736 | tf_op jit(solution)/shard_map/ffn/pallas_call | solution.py:301
  672.7 16.3 collective-permute-done.154
  706.6 8.7 collective-permute-start.156
  719.3 9.4 collective-permute-done.156
  731.7 10.7 collective-permute-start.157
  755.9 45.5 %collective-permute-done.69 = bf16[4,48,1024]{2,0,1:T(4,128)(2,1)S(1)} collective-permute-done((bf16[4,48,1024]{2,0,1:T(4,128)(2,1)S(1)}, bf16[4,48,1024]{2,0,1:T(4,128)(2,1)S(1)}, u32[]{:S(2)}, u32[]{:S(2)}) %collective-permute-start.69) | collective-permute-done | bytes 393248 | tf_op jit(solution)/shard_map/ppermute | solution.py:51
  813.9 15.4 collective-permute-start.161
  830.6 8.1 collective-permute-start.21
  861.9 14.6 collective-permute-done.23
  878.7 8.5 collective-permute-start.127
  891.5 9.6 collective-permute-done.24
  903.5 20.7 collective-permute-done.94
  953.3 11.0 collective-permute-done.129
  979.2 27.2 %collective-permute-done.97 = bf16[4,4,48,1024]{3,0,2,1:T(4,128)(2,1)} collective-permute-done((bf16[4,4,48,1024]{3,0,2,1:T(4,128)(2,1)S(1)}, bf16[4,4,48,1024]{3,0,2,1:T(4,128)(2,1)}, u32[]{:S(2)}, u32[]{:S(2)}) %collective-permute-start.97) | collective-permute-done | bytes 1572896 | tf_op jit(solution)/shard_map/ppermute | solution.py:39
  1013.0 21.7 %ffn.6 = (bf16[4,192,1024]{2,1,0:T(8,128)(2,1)}, bf16[4,192,1024]{2,1,0:T(8,128)(2,1)}, bf16[4,192,1024]{2,1,0:T(8,128)(2,1)}, bf16[4,192,1024]{2,1,0:T(8,128)(2...) custom-call(s32[1]{0:T(128)} %bitcast.20.mine_ref, ...), custom_call_target="tpu_custom_call" | custom-call | flops 14495514624 | bytes 37748736 | tf_op jit(solution)/shard_map/ffn/pallas_call | solution.py:301
  1045.9 21.8 %ffn.4 = (bf16[4,192,1024]{2,1,0:T(8,128)(2,1)}, bf16[4,192,1024]{2,1,0:T(8,128)(2,1)}, bf16[4,192,1024]{2,1,0:T(8,128)(2,1)}, bf16[4,192,1024]{2,1,0:T(8,128)(2...) custom-call(s32[1]{0:T(128)} %bitcast.20.mine_ref, ...), custom_call_target="tpu_custom_call" | custom-call | flops 14495514624 | bytes 37748736 | tf_op jit(solution)/shard_map/ffn/pallas_call | solution.py:301
  1129.5 12.3 collective-permute-done.29
  1255.4 15.9 collective-permute-done.243
  1275.4 18.4 collective-permute-done.253
  1301.1 12.8 collective-permute-done.249
  1354.3 9.2 collective-permute-done.122
  1398.4 15.9 collective-permute-done.125
  1420.8 21.8 %ffn.7 = (bf16[4,192,1024]{2,1,0:T(8,128)(2,1)}, bf16[4,192,1024]{2,1,0:T(8,128)(2,1)}, bf16[4,192,1024]{2,1,0:T(8,128)(2,1)}, bf16[4,192,1024]{2,1,0:T(8,128)(2...) custom-call(s32[1]{0:T(128)} %bitcast.20.mine_ref, ...), custom_call_target="tpu_custom_call" | custom-call | flops 14495514624 | bytes 37748736 | tf_op jit(solution)/shard_map/ffn/pallas_call | solution.py:301
  1471.6 10.1 collective-permute-done.181
  1486.6 24.1 %collective-permute-done.182 = bf16[4,4,48,1024]{3,0,2,1:T(4,128)(2,1)} collective-permute-done((bf16[4,4,48,1024]{3,0,2,1:T(4,128)(2,1)}, bf16[4,4,48,1024]{3,0,2,1:T(4,128)(2,1)}, u32[]{:S(2)}, u32[]{:S(2)}) %collective-permute-start.182) | collective-permute-done | bytes 1572896 | tf_op jit(solution)/shard_map/ppermute | solution.py:78
  1630.7 18.2 collective-permute-done.195
  1653.9 34.5 %attend_back.4 = (bf16[4,192,1024]{2,1,0:T(8,128)(2,1)}, bf16[4,192,1024]{2,1,0:T(8,128)(2,1)}, f32[4,1,1024]{2,1,0:T(1,128)}, bf16[4,2,3,256,128]{4,3,2,1,0:T(8...) custom-call(s32[1]{0:T(128)} %bitcast.20.mine_ref, ...), custom_call_target="tpu_custom_call" | custom-call | flops 3221225472 | bytes 25165824 | tf_op jit(solution)/shard_map/attend_back/pallas_call | solution.py:420
  1699.4 35.6 %attend_back.5 = (bf16[4,192,1024]{2,1,0:T(8,128)(2,1)}, bf16[4,192,1024]{2,1,0:T(8,128)(2,1)}, f32[4,1,1024]{2,1,0:T(1,128)}, bf16[4,2,3,256,128]{4,3,2,1,0:T(8...) custom-call(s32[1]{0:T(128)} %bitcast.20.mine_ref, ...), custom_call_target="tpu_custom_call" | custom-call | flops 3221225472 | bytes 22020096 | tf_op jit(solution)/shard_map/attend_back/pallas_call | solution.py:420
  1735.0 33.0 %attend_back.6 = (bf16[4,192,1024]{2,1,0:T(8,128)(2,1)}, bf16[4,192,1024]{2,1,0:T(8,128)(2,1)}, f32[4,1,1024]{2,1,0:T(1,128)}, bf16[4,2,3,256,128]{4,3,2,1,0:T(8...) custom-call(s32[1]{0:T(128)} %bitcast.20.mine_ref, ...), custom_call_target="tpu_custom_call" | custom-call | flops 3221225472 | bytes 18874368 | tf_op jit(solution)/shard_map/attend_back/pallas_call | solution.py:420
  1768.0 30.9 %attend_back.7 = (bf16[4,192,1024]{2,1,0:T(8,128)(2,1)}, bf16[4,192,1024]{2,1,0:T(8,128)(2,1)}, f32[4,1,1024]{2,1,0:T(1,128)}, bf16[4,2,3,256,128]{4,3,2,1,0:T(8...) custom-call(s32[1]{0:T(128)} %bitcast.20.mine_ref, ...), custom_call_target="tpu_custom_call" | custom-call | flops 3221225472 | bytes 15728640 | tf_op jit(solution)/shard_map/attend_back/pallas_call | solution.py:420
  1823.3 19.0 reduce-scatter.4.cloned.1.call-done
  1946.8 19.1 collective-permute-done.210
  1967.5 28.1 %collective-permute-done.196 = bf16[4,4,48,1024]{3,0,2,1:T(4,128)(2,1)S(1)} collective-permute-done((bf16[4,4,48,1024]{3,0,2,1:T(4,128)(2,1)S(1)}, bf16[4,4,48,1024]{3,0,2,1:T(4,128)(2,1)S(1)}, u32[]{:S(2)}, u32[]{:S(2)}) %collective-permute-start.196) | collective-permute-done | bytes 1572896 | tf_op jit(solution)/shard_map/ppermute | solution.py:78
  2037.8 30.1 %collective-permute-start.219 = (bf16[4,2,48,1024]{3,0,2,1:T(4,128)(2,1)S(1)}, bf16[4,2,48,1024]{3,0,2,1:T(4,128)(2,1)S(1)}, u32[]{:S(2)}, u32[]{:S(2)}) collective-permute-start(bf16[4,2,48,1024]{3,0,2,1:T(4,128)(2,1)S(1)} %add_convert_fusion.1), channel_id=1, source_target_pairs={{0,2},{2,4},{4,6},{1,3},{3,5},{5,7},{8,10},{10,12},{12,14},{9,11},... | collective-permute-start | bytes 2359304 | tf_op jit(solution)/shard_map/ppermute | solution.py:56
  2081.9 9.3 collective-permute-done.227
  2099.7 11.8 collective-permute-start.199
  (1252 shorter events, 1178.5 us)
Async XLA Ops:
  7.2 1835.1 %reduce-scatter.4.cloned.1.call-start = ((), (), s32[]{:S(2)}) async-start(), calls=%async_computation.1 | async-start | bytes 655360
  53.2 68.0 %collective-permute-start.57 = (bf16[4,2,48,1024]{3,0,2,1:T(4,128)(2,1)S(1)}, bf16[4,2,48,1024]{3,0,2,1:T(4,128)(2,1)S(1)}, u32[]{:S(2)}, u32[]{:S(2)}) collective-permute-start(bf16[4,2,48,1024]{3,0,2,1:T(4,128)(2,1)S(1)} %get-tuple-element.427), channel_id=1, source_target_pairs={{0,2},{2,4},{4,6},{1,3},{3,5},{5,7},{8,10},{10,12},{12,14},{9,11},... | collective-permute-start | bytes 2359304 | tf_op jit(solution)/shard_map/ppermute | solution.py:42
  65.3 57.5 %collective-permute-start.58 = (bf16[4,2,48,1024]{3,0,2,1:T(4,128)(2,1)S(1)}, bf16[4,2,48,1024]{3,0,2,1:T(4,128)(2,1)S(1)}, u32[]{:S(2)}, u32[]{:S(2)}) collective-permute-start(bf16[4,2,48,1024]{3,0,2,1:T(4,128)(2,1)S(1)} %get-tuple-element.427), channel_id=1, source_target_pairs={{2,0},{4,2},{6,4},{3,1},{5,3},{7,5},{10,8},{12,10},{14,12},{11,9},... | collective-permute-start | bytes 2359304 | tf_op jit(solution)/shard_map/ppermute | solution.py:43
  114.3 67.8 %collective-permute-start.41 = (bf16[4,4,48,1024]{3,0,2,1:T(4,128)(2,1)S(1)}, bf16[4,4,48,1024]{3,0,2,1:T(4,128)(2,1)S(1)}, u32[]{:S(2)}, u32[]{:S(2)}) collective-permute-start(bf16[4,4,48,1024]{3,0,2,1:T(4,128)(2,1)S(1)} %pad_maximum_fusion.23), channel_id=1, source_target_pairs={{0,1},{2,3},{4,5},{6,7},{1,0},{3,2},{5,4},{7,6},{8,9},{10,11},{12,... | collective-permute-start | bytes 4718600 | tf_op jit(solution)/shard_map/ppermute | solution.py:39
  120.6 90.8 %collective-permute-start.6 = (bf16[4,4,48,1024]{3,0,2,1:T(4,128)(2,1)S(1)}, bf16[4,4,48,1024]{3,0,2,1:T(4,128)(2,1)S(1)}, u32[]{:S(2)}, u32[]{:S(2)}) collective-permute-start(bf16[4,4,48,1024]{3,0,2,1:T(4,128)(2,1)S(1)} %pad_maximum_fusion.20), channel_id=1, source_target_pairs={{0,1},{2,3},{4,5},{6,7},{1,0},{3,2},{5,4},{7,6},{8,9},{10,11},{12,... | collective-permute-start | bytes 4718600 | tf_op jit(solution)/shard_map/ppermute | solution.py:39
  129.9 183.0 %collective-permute-start.62 = (bf16[4,2,48,1024]{3,0,2,1:T(4,128)(2,1)}, bf16[4,2,48,1024]{3,0,2,1:T(4,128)(2,1)}, u32[]{:S(2)}, u32[]{:S(2)}) collective-permute-start(bf16[4,2,48,1024]{3,0,2,1:T(4,128)(2,1)} %collective-permute-done.61), channel_id=1, source_target_pairs={{4,6},{5,7},{12,14},{13,15},{20,22},{21,23},{28,30},{29,31}} | collective-permute-start | bytes 2359304 | tf_op jit(solution)/shard_map/ppermute | solution.py:42
  143.8 171.6 %collective-permute-start.60 = (bf16[4,2,48,1024]{3,0,2,1:T(4,128)(2,1)}, bf16[4,2,48,1024]{3,0,2,1:T(4,128)(2,1)}, u32[]{:S(2)}, u32[]{:S(2)}) collective-permute-start(bf16[4,2,48,1024]{3,0,2,1:T(4,128)(2,1)} %collective-permute-done.59), channel_id=1, source_target_pairs={{2,0},{3,1},{10,8},{11,9},{18,16},{19,17},{26,24},{27,25}} | collective-permute-start | bytes 2359304 | tf_op jit(solution)/shard_map/ppermute | solution.py:43
  252.1 64.9 %collective-permute-start.7 = (bf16[4,4,48,1024]{3,0,2,1:T(4,128)(2,1)}, bf16[4,4,48,1024]{3,0,2,1:T(4,128)(2,1)S(1)}, u32[]{:S(2)}, u32[]{:S(2)}) collective-permute-start(bf16[4,4,48,1024]{3,0,2,1:T(4,128)(2,1)} %copy.164), channel_id=1, source_target_pairs={{0,1},{2,3},{4,5},{6,7},{1,0},{3,2},{5,4},{7,6},{8,9},{10,11},{12,... | collective-permute-start | bytes 4718600 | tf_op jit(solution)/shard_map/ppermute | solution.py:78
  524.5 63.0 %collective-permute-start.111 = (bf16[4,4,48,1024]{3,0,2,1:T(4,128)(2,1)S(1)}, bf16[4,4,48,1024]{3,0,2,1:T(4,128)(2,1)S(1)}, u32[]{:S(2)}, u32[]{:S(2)}) collective-permute-start(bf16[4,4,48,1024]{3,0,2,1:T(4,128)(2,1)S(1)} %pad_maximum_fusion.28), channel_id=1, source_target_pairs={{0,1},{2,3},{4,5},{6,7},{1,0},{3,2},{5,4},{7,6},{8,9},{10,11},{12,... | collective-permute-start | bytes 4718600 | tf_op jit(solution)/shard_map/ppermute | solution.py:39
  623.6 67.7 %collective-permute-start.112 = (bf16[4,4,48,1024]{3,0,2,1:T(4,128)(2,1)}, bf16[4,4,48,1024]{3,0,2,1:T(4,128)(2,1)S(1)}, u32[]{:S(2)}, u32[]{:S(2)}) collective-permute-start(bf16[4,4,48,1024]{3,0,2,1:T(4,128)(2,1)} %copy.212), channel_id=1, source_target_pairs={{0,1},{2,3},{4,5},{6,7},{1,0},{3,2},{5,4},{7,6},{8,9},{10,11},{12,... | collective-permute-start | bytes 4718600 | tf_op jit(solution)/shard_map/ppermute | solution.py:78
  671.4 60.3 %collective-permute-start.250 = (bf16[4,2,512,256]{3,2,0,1:T(8,128)(2,1)S(1)}, bf16[4,2,512,256]{3,2,0,1:T(8,128)(2,1)S(1)}, u32[]{:S(2)}, u32[]{:S(2)}) collective-permute-start(bf16[4,2,512,256]{3,2,0,1:T(8,128)(2,1)S(1)} %copy.297), channel_id=1, source_target_pairs={{0,8},{8,0},{16,24},{24,16},{1,9},{9,1},{17,25},{25,17},{2,10},{10... | collective-permute-start | bytes 6291464 | tf_op jit(solution)/shard_map/ppermute | solution.py:102
  728.7 77.8 %collective-permute-start.20 = (bf16[4,4,48,1024]{3,0,2,1:T(4,128)(2,1)S(1)}, bf16[4,4,48,1024]{3,0,2,1:T(4,128)(2,1)S(1)}, u32[]{:S(2)}, u32[]{:S(2)}) collective-permute-start(bf16[4,4,48,1024]{3,0,2,1:T(4,128)(2,1)S(1)} %pad_maximum_fusion.21), channel_id=1, source_target_pairs={{0,1},{2,3},{4,5},{6,7},{1,0},{3,2},{5,4},{7,6},{8,9},{10,11},{12,... | collective-permute-start | bytes 4718600 | tf_op jit(solution)/shard_map/ppermute | solution.py:39
  729.4 78.7 %collective-permute-start.90 = (bf16[4,4,48,1024]{3,0,2,1:T(4,128)(2,1)S(1)}, bf16[4,4,48,1024]{3,0,2,1:T(4,128)(2,1)S(1)}, u32[]{:S(2)}, u32[]{:S(2)}) collective-permute-start(bf16[4,4,48,1024]{3,0,2,1:T(4,128)(2,1)S(1)} %copy-done.60), channel_id=1, source_target_pairs={{0,1},{2,3},{4,5},{6,7},{1,0},{3,2},{5,4},{7,6},{8,9},{10,11},{12,... | collective-permute-start | bytes 4718600 | tf_op jit(solution)/shard_map/ppermute | solution.py:39
  744.7 69.1 %collective-permute-start.114 = (bf16[4,48,1024]{2,0,1:T(4,128)(2,1)}, bf16[4,48,1024]{2,0,1:T(4,128)(2,1)S(1)}, u32[]{:S(2)}, u32[]{:S(2)}) collective-permute-start(bf16[4,48,1024]{2,0,1:T(4,128)(2,1)} %get-tuple-element.265), channel_id=1, source_target_pairs={{0,2},{2,4},{1,3},{3,5},{8,10},{10,12},{9,11},{11,13},{16,18},{18,... | collective-permute-start | bytes 1179656 | tf_op jit(solution)/shard_map/ppermute | solution.py:56
  750.7 78.5 %collective-permute-start.117 = (bf16[4,48,1024]{2,0,1:T(4,128)(2,1)S(1)}, bf16[4,48,1024]{2,0,1:T(4,128)(2,1)S(1)}, u32[]{:S(2)}, u32[]{:S(2)}) collective-permute-start(bf16[4,48,1024]{2,0,1:T(4,128)(2,1)S(1)} %get-tuple-element.266), channel_id=1, source_target_pairs={{4,2},{6,4},{5,3},{7,5},{12,10},{14,12},{13,11},{15,13},{20,18},{2... | collective-permute-start | bytes 1179656 | tf_op jit(solution)/shard_map/ppermute | solution.py:57
  854.4 90.0 %collective-permute-start.242 = (bf16[4,2,2,256,512]{4,3,2,0,1:T(8,128)(2,1)S(1)}, bf16[4,2,2,256,512]{4,3,2,0,1:T(8,128)(2,1)}, u32[]{:S(2)}, u32[]{:S(2)}) collective-permute-start(bf16[4,2,2,256,512]{4,3,2,0,1:T(8,128)(2,1)S(1)} %copy.291), channel_id=1, source_target_pairs={{0,8},{8,0},{16,24},{24,16},{1,9},{9,1},{17,25},{25,17},{2,10},{10... | collective-permute-start | bytes 12582920 | tf_op jit(solution)/shard_map/ppermute | solution.py:102
  878.7 60.4 %collective-permute-start.127 = (bf16[4,2,48,1024]{3,0,2,1:T(4,128)(2,1)S(1)}, bf16[4,2,48,1024]{3,0,2,1:T(4,128)(2,1)}, u32[]{:S(2)}, u32[]{:S(2)}) collective-permute-start(bf16[4,2,48,1024]{3,0,2,1:T(4,128)(2,1)S(1)} %get-tuple-element.433), channel_id=1, source_target_pairs={{0,2},{2,4},{4,6},{1,3},{3,5},{5,7},{8,10},{10,12},{12,14},{9,11},... | collective-permute-start | bytes 2359304 | tf_op jit(solution)/shard_map/ppermute | solution.py:42
  889.3 51.4 %collective-permute-start.128 = (bf16[4,2,48,1024]{3,0,2,1:T(4,128)(2,1)S(1)}, bf16[4,2,48,1024]{3,0,2,1:T(4,128)(2,1)}, u32[]{:S(2)}, u32[]{:S(2)}) collective-permute-start(bf16[4,2,48,1024]{3,0,2,1:T(4,128)(2,1)S(1)} %get-tuple-element.433), channel_id=1, source_target_pairs={{2,0},{4,2},{6,4},{3,1},{5,3},{7,5},{10,8},{12,10},{14,12},{11,9},... | collective-permute-start | bytes 2359304 | tf_op jit(solution)/shard_map/ppermute | solution.py:43
  936.8 69.7 %collective-permute-start.97 = (bf16[4,4,48,1024]{3,0,2,1:T(4,128)(2,1)S(1)}, bf16[4,4,48,1024]{3,0,2,1:T(4,128)(2,1)}, u32[]{:S(2)}, u32[]{:S(2)}) collective-permute-start(bf16[4,4,48,1024]{3,0,2,1:T(4,128)(2,1)S(1)} %pad_maximum_fusion.27), channel_id=1, source_target_pairs={{0,1},{2,3},{4,5},{6,7},{1,0},{3,2},{5,4},{7,6},{8,9},{10,11},{12,... | collective-permute-start | bytes 4718600 | tf_op jit(solution)/shard_map/ppermute | solution.py:39
  944.3 129.5 %collective-permute-start.167 = (bf16[4,4,48,1024]{3,0,2,1:T(4,128)(2,1)}, bf16[4,4,48,1024]{3,0,2,1:T(4,128)(2,1)}, u32[]{:S(2)}, u32[]{:S(2)}) collective-permute-start(bf16[4,4,48,1024]{3,0,2,1:T(4,128)(2,1)} %pad_maximum_fusion.31), channel_id=1, source_target_pairs={{0,1},{2,3},{4,5},{6,7},{1,0},{3,2},{5,4},{7,6},{8,9},{10,11},{12,... | collective-permute-start | bytes 4718600 | tf_op jit(solution)/shard_map/ppermute | solution.py:39
  951.1 128.6 %collective-permute-start.132 = (bf16[4,2,48,1024]{3,0,2,1:T(4,128)(2,1)}, bf16[4,2,48,1024]{3,0,2,1:T(4,128)(2,1)}, u32[]{:S(2)}, u32[]{:S(2)}) collective-permute-start(bf16[4,2,48,1024]{3,0,2,1:T(4,128)(2,1)} %collective-permute-done.131), channel_id=1, source_target_pairs={{4,6},{5,7},{12,14},{13,15},{20,22},{21,23},{28,30},{29,31}} | collective-permute-start | bytes 2359304 | tf_op jit(solution)/shard_map/ppermute | solution.py:42
  964.3 119.4 %collective-permute-start.130 = (bf16[4,2,48,1024]{3,0,2,1:T(4,128)(2,1)}, bf16[4,2,48,1024]{3,0,2,1:T(4,128)(2,1)}, u32[]{:S(2)}, u32[]{:S(2)}) collective-permute-start(bf16[4,2,48,1024]{3,0,2,1:T(4,128)(2,1)} %collective-permute-done.129), channel_id=1, source_target_pairs={{2,0},{3,1},{10,8},{11,9},{18,16},{19,17},{26,24},{27,25}} | collective-permute-start | bytes 2359304 | tf_op jit(solution)/shard_map/ppermute | solution.py:43
  1040.2 52.0 %collective-permute-start.98 = (bf16[4,2,48,1024]{3,0,2,1:T(4,128)(2,1)S(1)}, bf16[4,2,48,1024]{3,0,2,1:T(4,128)(2,1)}, u32[]{:S(2)}, u32[]{:S(2)}) collective-permute-start(bf16[4,2,48,1024]{3,0,2,1:T(4,128)(2,1)S(1)} %copy_dynamic-update-slice_fusion.12), channel_id=1, source_target_pairs={{0,2},{1,3},{8,10},{9,11},{16,18},{17,19},{24,26},{25,27}} | collective-permute-start | bytes 2359304 | tf_op jit(solution)/shard_map/ppermute | solution.py:56
  1073.8 54.2 %collective-permute-start.168 = (bf16[4,4,48,1024]{3,0,2,1:T(4,128)(2,1)S(1)}, bf16[4,4,48,1024]{3,0,2,1:T(4,128)(2,1)S(1)}, u32[]{:S(2)}, u32[]{:S(2)}) collective-permute-start(bf16[4,4,48,1024]{3,0,2,1:T(4,128)(2,1)S(1)} %copy.239), channel_id=1, source_target_pairs={{0,1},{2,3},{4,5},{6,7},{1,0},{3,2},{5,4},{7,6},{8,9},{10,11},{12,... | collective-permute-start | bytes 4718600 | tf_op jit(solution)/shard_map/ppermute | solution.py:78
  1118.0 56.0 %collective-permute-start.252 = (bf16[4,2,512,256]{3,2,0,1:T(8,128)(2,1)S(1)}, bf16[4,2,512,256]{3,2,0,1:T(8,128)(2,1)S(1)}, u32[]{:S(2)}, u32[]{:S(2)}) collective-permute-start(bf16[4,2,512,256]{3,2,0,1:T(8,128)(2,1)S(1)} %copy.299), channel_id=1, source_target_pairs={{0,8},{8,0},{16,24},{24,16},{1,9},{9,1},{17,25},{25,17},{2,10},{10... | collective-permute-start | bytes 6291464 | tf_op jit(solution)/shard_map/ppermute | solution.py:102
  1224.2 69.5 %collective-permute-start.253 = (bf16[4,1,512,256]{3,2,0,1:T(8,128)(2,1)}, bf16[4,1,512,256]{3,2,0,1:T(8,128)(2,1)S(1)}, u32[]{:S(2)}, u32[]{:S(2)}) collective-permute-start(bf16[4,1,512,256]{3,2,0,1:T(8,128)(2,1)} %slice.1603), channel_id=1, source_target_pairs={{0,16},{8,24},{16,0},{24,8},{1,17},{9,25},{17,1},{25,9},{2,18},{10... | collective-permute-start | bytes 3145736 | tf_op jit(solution)/shard_map/ppermute | solution.py:102
  1243.3 70.5 %collective-permute-start.249 = (bf16[4,1,512,256]{3,2,0,1:T(8,128)(2,1)}, bf16[4,1,512,256]{3,2,0,1:T(8,128)(2,1)}, u32[]{:S(2)}, u32[]{:S(2)}) collective-permute-start(bf16[4,1,512,256]{3,2,0,1:T(8,128)(2,1)} %slice.1605), channel_id=1, source_target_pairs={{0,16},{8,24},{16,0},{24,8},{1,17},{9,25},{17,1},{25,9},{2,18},{10... | collective-permute-start | bytes 3145736 | tf_op jit(solution)/shard_map/ppermute | solution.py:102
  1243.9 71.2 %collective-permute-start.119 = (bf16[4,48,1024]{2,0,1:T(4,128)(2,1)}, bf16[4,48,1024]{2,0,1:T(4,128)(2,1)S(1)}, u32[]{:S(2)}, u32[]{:S(2)}) collective-permute-start(bf16[4,48,1024]{2,0,1:T(4,128)(2,1)} %multiply_convert_fusion.4), channel_id=1, source_target_pairs={{0,2},{2,4},{4,6},{1,3},{3,5},{5,7},{8,10},{10,12},{12,14},{9,11},... | collective-permute-start | bytes 1179656 | tf_op jit(solution)/shard_map/ppermute | solution.py:42
  1248.5 71.9 %collective-permute-start.120 = (bf16[4,48,1024]{2,0,1:T(4,128)(2,1)}, bf16[4,48,1024]{2,0,1:T(4,128)(2,1)}, u32[]{:S(2)}, u32[]{:S(2)}) collective-permute-start(bf16[4,48,1024]{2,0,1:T(4,128)(2,1)} %multiply_convert_fusion.4), channel_id=1, source_target_pairs={{2,0},{4,2},{6,4},{3,1},{5,3},{7,5},{10,8},{12,10},{14,12},{11,9},... | collective-permute-start | bytes 1179656 | tf_op jit(solution)/shard_map/ppermute | solution.py:43
  1271.3 49.8 %collective-permute-start.148 = (bf16[4,48,1024]{2,0,1:T(4,128)(2,1)S(1)}, bf16[4,48,1024]{2,0,1:T(4,128)(2,1)S(1)}, u32[]{:S(2)}, u32[]{:S(2)}) collective-permute-start(bf16[4,48,1024]{2,0,1:T(4,128)(2,1)S(1)} %get-tuple-element.233), channel_id=1, source_target_pairs={{2,0},{4,2},{6,4},{3,1},{5,3},{7,5},{10,8},{12,10},{14,12},{11,9},... | collective-permute-start | bytes 1179656 | tf_op jit(solution)/shard_map/ppermute | solution.py:43
  1322.7 69.0 %collective-permute-start.244 = (bf16[4,2,2,256,512]{4,3,2,0,1:T(8,128)(2,1)S(1)}, bf16[4,2,2,256,512]{4,3,2,0,1:T(8,128)(2,1)}, u32[]{:S(2)}, u32[]{:S(2)}) collective-permute-start(bf16[4,2,2,256,512]{4,3,2,0,1:T(8,128)(2,1)S(1)} %copy.293), channel_id=1, source_target_pairs={{0,8},{8,0},{16,24},{24,16},{1,9},{9,1},{17,25},{25,17},{2,10},{10... | collective-permute-start | bytes 12582920 | tf_op jit(solution)/shard_map/ppermute | solution.py:102
  1344.0 111.1 %collective-permute-start.240 = (bf16[4,2,2,256,512]{4,3,2,0,1:T(8,128)(2,1)}, bf16[4,2,2,256,512]{4,3,2,0,1:T(8,128)(2,1)}, u32[]{:S(2)}, u32[]{:S(2)}) collective-permute-start(bf16[4,2,2,256,512]{4,3,2,0,1:T(8,128)(2,1)} %copy.289), channel_id=1, source_target_pairs={{0,8},{8,0},{16,24},{24,16},{1,9},{9,1},{17,25},{25,17},{2,10},{10... | collective-permute-start | bytes 12582920 | tf_op jit(solution)/shard_map/ppermute | solution.py:102
  1387.3 75.0 %collective-permute-start.153 = (bf16[4,4,48,1024]{3,0,2,1:T(4,128)(2,1)}, bf16[4,4,48,1024]{3,0,2,1:T(4,128)(2,1)}, u32[]{:S(2)}, u32[]{:S(2)}) collective-permute-start(bf16[4,4,48,1024]{3,0,2,1:T(4,128)(2,1)} %pad_maximum_fusion.30), channel_id=1, source_target_pairs={{0,1},{2,3},{4,5},{6,7},{1,0},{3,2},{5,4},{7,6},{8,9},{10,11},{12,... | collective-permute-start | bytes 4718600 | tf_op jit(solution)/shard_map/ppermute | solution.py:39
  1387.9 93.8 %collective-permute-start.181 = (bf16[4,4,48,1024]{3,0,2,1:T(4,128)(2,1)}, bf16[4,4,48,1024]{3,0,2,1:T(4,128)(2,1)}, u32[]{:S(2)}, u32[]{:S(2)}) collective-permute-start(bf16[4,4,48,1024]{3,0,2,1:T(4,128)(2,1)} %pad_maximum_fusion.32), channel_id=1, source_target_pairs={{0,1},{2,3},{4,5},{6,7},{1,0},{3,2},{5,4},{7,6},{8,9},{10,11},{12,... | collective-permute-start | bytes 4718600 | tf_op jit(solution)/shard_map/ppermute | solution.py:39
  1455.0 55.7 %collective-permute-start.182 = (bf16[4,4,48,1024]{3,0,2,1:T(4,128)(2,1)}, bf16[4,4,48,1024]{3,0,2,1:T(4,128)(2,1)}, u32[]{:S(2)}, u32[]{:S(2)}) collective-permute-start(bf16[4,4,48,1024]{3,0,2,1:T(4,128)(2,1)} %copy.245), channel_id=1, source_target_pairs={{0,1},{2,3},{4,5},{6,7},{1,0},{3,2},{5,4},{7,6},{8,9},{10,11},{12,... | collective-permute-start | bytes 4718600 | tf_op jit(solution)/shard_map/ppermute | solution.py:78
  1462.3 85.6 %collective-permute-start.245 = (bf16[4,1,2,256,512]{4,3,2,0,1:T(8,128)(2,1)}, bf16[4,1,2,256,512]{4,3,2,0,1:T(8,128)(2,1)}, u32[]{:S(2)}, u32[]{:S(2)}) collective-permute-start(bf16[4,1,2,256,512]{4,3,2,0,1:T(8,128)(2,1)} %slice.1599), channel_id=1, source_target_pairs={{0,16},{8,24},{16,0},{24,8},{1,17},{9,25},{17,1},{25,9},{2,18},{10... | collective-permute-start | bytes 6291464 | tf_op jit(solution)/shard_map/ppermute | solution.py:102
  1559.5 65.5 %collective-permute-start.246 = (bf16[4,2,2,256,512]{4,3,2,1,0:T(8,128)(2,1)}, bf16[4,2,2,256,512]{4,3,2,1,0:T(8,128)(2,1)}, u32[]{:S(2)}, u32[]{:S(2)}) collective-permute-start(bf16[4,2,2,256,512]{4,3,2,1,0:T(8,128)(2,1)} %get-tuple-element.190), channel_id=1, source_target_pairs={{0,8},{8,0},{16,24},{24,16},{1,9},{9,1},{17,25},{25,17},{2,10},{10... | collective-permute-start | bytes 12582920 | tf_op jit(solution)/shard_map/ppermute | solution.py:102
  1630.2 257.0 %collective-permute-start.247 = (bf16[4,1,2,256,512]{4,3,2,1,0:T(8,128)(2,1)}, bf16[4,1,2,256,512]{4,3,2,1,0:T(8,128)(2,1)}, u32[]{:S(2)}, u32[]{:S(2)}) collective-permute-start(bf16[4,1,2,256,512]{4,3,2,1,0:T(8,128)(2,1)} %slice.1598), channel_id=1, source_target_pairs={{0,16},{8,24},{16,0},{24,8},{1,17},{9,25},{17,1},{25,9},{2,18},{10... | collective-permute-start | bytes 6291464 | tf_op jit(solution)/shard_map/ppermute | solution.py:102
  1690.3 190.9 %collective-permute-start.238 = (bf16[4,2,128,256]{3,2,0,1:T(8,128)(2,1)}, bf16[4,2,128,256]{3,2,0,1:T(8,128)(2,1)}, u32[]{:S(2)}, u32[]{:S(2)}) collective-permute-start(bf16[4,2,128,256]{3,2,0,1:T(8,128)(2,1)} %copy.287), channel_id=1, source_target_pairs={{0,8},{8,0},{16,24},{24,16},{1,9},{9,1},{17,25},{25,17},{2,10},{10... | collective-permute-start | bytes 1572872 | tf_op jit(solution)/shard_map/ppermute | solution.py:102
  1697.9 202.6 %collective-permute-start.220 = (bf16[4,2,48,1024]{3,0,2,1:T(4,128)(2,1)}, bf16[4,2,48,1024]{3,0,2,1:T(4,128)(2,1)}, u32[]{:S(2)}, u32[]{:S(2)}) collective-permute-start(bf16[4,2,48,1024]{3,0,2,1:T(4,128)(2,1)} %copy_dynamic-update-slice_fusion.2), channel_id=1, source_target_pairs={{6,4},{7,5},{14,12},{15,13},{22,20},{23,21},{30,28},{31,29}} | collective-permute-start | bytes 2359304 | tf_op jit(solution)/shard_map/ppermute | solution.py:57
  1883.9 51.9 %collective-permute-start.230 = (bf16[4,2,3,256,128]{4,3,2,0,1:T(8,128)(2,1)}, bf16[4,2,3,256,128]{4,3,2,0,1:T(8,128)(2,1)}, u32[]{:S(2)}, u32[]{:S(2)}) collective-permute-start(bf16[4,2,3,256,128]{4,3,2,0,1:T(8,128)(2,1)} %copy.281), channel_id=1, source_target_pairs={{0,8},{8,0},{16,24},{24,16},{1,9},{9,1},{17,25},{25,17},{2,10},{10... | collective-permute-start | bytes 4718600 | tf_op jit(solution)/shard_map/ppermute | solution.py:102
  1932.5 63.0 %collective-permute-start.196 = (bf16[4,4,48,1024]{3,0,2,1:T(4,128)(2,1)S(1)}, bf16[4,4,48,1024]{3,0,2,1:T(4,128)(2,1)S(1)}, u32[]{:S(2)}, u32[]{:S(2)}) collective-permute-start(bf16[4,4,48,1024]{3,0,2,1:T(4,128)(2,1)S(1)} %copy-done.61), channel_id=1, source_target_pairs={{0,1},{2,3},{4,5},{6,7},{1,0},{3,2},{5,4},{7,6},{8,9},{10,11},{12,... | collective-permute-start | bytes 4718600 | tf_op jit(solution)/shard_map/ppermute | solution.py:78
  1936.5 64.1 %collective-permute-start.224 = (bf16[4,2,3,256,128]{4,3,2,1,0:T(8,128)(2,1)S(1)}, bf16[4,2,3,256,128]{4,3,2,1,0:T(8,128)(2,1)S(1)}, u32[]{:S(2)}, u32[]{:S(2)}) collective-permute-start(bf16[4,2,3,256,128]{4,3,2,1,0:T(8,128)(2,1)S(1)} %copy-done.179), channel_id=1, source_target_pairs={{0,8},{8,0},{16,24},{24,16},{1,9},{9,1},{17,25},{25,17},{2,10},{10... | collective-permute-start | bytes 4718600 | tf_op jit(solution)/shard_map/ppermute | solution.py:102
  1938.9 62.7 %collective-permute-start.218 = (bf16[4,2,48,1024]{3,0,2,1:T(4,128)(2,1)S(1)}, bf16[4,2,48,1024]{3,0,2,1:T(4,128)(2,1)S(1)}, u32[]{:S(2)}, u32[]{:S(2)}) collective-permute-start(bf16[4,2,48,1024]{3,0,2,1:T(4,128)(2,1)S(1)} %get-tuple-element.420), channel_id=1, source_target_pairs={{0,2},{2,4},{1,3},{3,5},{8,10},{10,12},{9,11},{11,13},{16,18},{18,... | collective-permute-start | bytes 2359304 | tf_op jit(solution)/shard_map/ppermute | solution.py:56
  1943.6 61.0 %collective-permute-start.204 = (bf16[4,2,48,1024]{3,0,2,1:T(4,128)(2,1)S(1)}, bf16[4,2,48,1024]{3,0,2,1:T(4,128)(2,1)S(1)}, u32[]{:S(2)}, u32[]{:S(2)}) collective-permute-start(bf16[4,2,48,1024]{3,0,2,1:T(4,128)(2,1)S(1)} %get-tuple-element.414), channel_id=1, source_target_pairs={{0,2},{2,4},{1,3},{3,5},{8,10},{10,12},{9,11},{11,13},{16,18},{18,... | collective-permute-start | bytes 2359304 | tf_op jit(solution)/shard_map/ppermute | solution.py:56
  1966.0 52.8 %collective-permute-start.207 = (bf16[4,2,48,1024]{3,0,2,1:T(4,128)(2,1)S(1)}, bf16[4,2,48,1024]{3,0,2,1:T(4,128)(2,1)S(1)}, u32[]{:S(2)}, u32[]{:S(2)}) collective-permute-start(bf16[4,2,48,1024]{3,0,2,1:T(4,128)(2,1)S(1)} %get-tuple-element.415), channel_id=1, source_target_pairs={{4,2},{6,4},{5,3},{7,5},{12,10},{14,12},{13,11},{15,13},{20,18},{2... | collective-permute-start | bytes 2359304 | tf_op jit(solution)/shard_map/ppermute | solution.py:57
  2008.9 63.8 %collective-permute-start.231 = (bf16[4,1,3,256,128]{4,3,2,0,1:T(8,128)(2,1)S(1)}, bf16[4,1,3,256,128]{4,3,2,0,1:T(8,128)(2,1)S(1)}, u32[]{:S(2)}, u32[]{:S(2)}) collective-permute-start(bf16[4,1,3,256,128]{4,3,2,0,1:T(8,128)(2,1)S(1)} %slice.1606), channel_id=1, source_target_pairs={{0,16},{8,24},{16,0},{24,8},{1,17},{9,25},{17,1},{25,9},{2,18},{10... | collective-permute-start | bytes 2359304 | tf_op jit(solution)/shard_map/ppermute | solution.py:102
  2037.8 74.0 %collective-permute-start.219 = (bf16[4,2,48,1024]{3,0,2,1:T(4,128)(2,1)S(1)}, bf16[4,2,48,1024]{3,0,2,1:T(4,128)(2,1)S(1)}, u32[]{:S(2)}, u32[]{:S(2)}) collective-permute-start(bf16[4,2,48,1024]{3,0,2,1:T(4,128)(2,1)S(1)} %add_convert_fusion.1), channel_id=1, source_target_pairs={{0,2},{2,4},{4,6},{1,3},{3,5},{5,7},{8,10},{10,12},{12,14},{9,11},... | collective-permute-start | bytes 2359304 | tf_op jit(solution)/shard_map/ppermute | solution.py:56
  (399 other events, 6893.6 us)
Sparse Core Ops, SparseCore 0:
  1819.6 22.6 reduce-scatter.3

commit v2 on v1

--- a/solution.py
+++ b/solution.py
@@ -14,6 +14,7 @@
 FRAME_BLOCK = 16
 CHUNKS = 4
 VMEM_BYTES = 56 * 1024 * 1024
+KERNEL_VMEM_BYTES = 63 * 1024 * 1024
 
 f32 = jnp.float32
 bf16 = jnp.bfloat16
@@ -560,6 +561,978 @@
     )
 
 
+MESH = pl.DeviceIdType.MESH
+ZN, YN = 4, 2
+
+
+def fits(frames, group_size, local, positions, depth, width, hidden):
+    return (
+        frames == 4
+        and group_size == ZN * YN
+        and local % 16 == 0
+        and positions == 16
+        and width % 128 == 0
+        and (depth // frames) % 128 == 0
+        and hidden % 128 == 0
+    )
+
+
+class Place:
+    def __init__(self):
+        self.m = lax.axis_index("mp")
+        self.f = lax.axis_index("frames")
+        self.z = self.m // YN
+        self.ids = {
+            "y": ("mp", self.m ^ 1),
+            "up": ("mp", self.m + YN),
+            "down": ("mp", self.m - YN),
+            "core": ("frames", self.f ^ 1),
+            "x": ("frames", self.f ^ 2),
+        }
+
+    def device(self, way):
+        axis, index = self.ids[way]
+        return {axis: index}
+
+    def copy(self, src, dst, send, recv, way):
+        return pltpu.make_async_remote_copy(
+            src_ref=src, dst_ref=dst, send_sem=send, recv_sem=recv, device_id=self.device(way), device_id_type=MESH
+        )
+
+
+def when(condition, run):
+    pl.when(condition)(run)
+
+
+def wait_got(dst, send, recv, place):
+    place.copy(dst, dst, send, recv, "y").wait_recv()
+
+
+class GatherZ:
+    def __init__(self, place, g, send, recv):
+        self.place, self.g, self.send, self.recv = place, g, send, recv
+
+    def site(self, number, way, src, dst):
+        return self.place.copy(
+            self.g.at[src[0], src[1]],
+            self.g.at[dst[0], dst[1]],
+            self.send.at[number],
+            self.recv.at[dst[0] * 2 + dst[1]],
+            way,
+        )
+
+    def up(self, k):
+        return self.site(k - 1, "up", (k - 1, 0), (k, 0))
+
+    def down(self, k):
+        return self.site(2 + k, "down", ((5 - k) % 4, 0), (4 - k, 0))
+
+    def across(self, k):
+        return self.site(6 + k, "y", (k, 0), (k, 1))
+
+    def got(self, k, y):
+        wait_got(self.g.at[k, y], self.send.at[0], self.recv.at[k * 2 + y], self.place)
+
+    def t1(self):
+        z = self.place.z
+        when(z < 3, lambda: self.up(1).start())
+        when(z > 0, lambda: self.down(1).start())
+        self.across(0).start()
+
+    def t2(self):
+        z = self.place.z
+
+        def low():
+            self.got(1, 0)
+            when(z < 3, lambda: self.up(2).start())
+            self.across(1).start()
+
+        def high():
+            self.got(3, 0)
+            when(z > 0, lambda: self.down(2).start())
+            self.across(3).start()
+
+        when(z >= 1, low)
+        when(z <= 2, high)
+        when(z < 3, lambda: self.up(1).wait_send())
+        when(z > 0, lambda: self.down(1).wait_send())
+        self.across(0).wait_send()
+
+    def t3(self):
+        z = self.place.z
+        self.got(2, 0)
+        when(z == 2, lambda: self.up(3).start())
+        when(z == 1, lambda: self.down(3).start())
+        self.across(2).start()
+        when((z >= 1) & (z < 3), lambda: self.up(2).wait_send())
+        when((z <= 2) & (z > 0), lambda: self.down(2).wait_send())
+        when(z >= 1, lambda: self.across(1).wait_send())
+        when(z <= 2, lambda: self.across(3).wait_send())
+
+    def t4(self):
+        z = self.place.z
+
+        def bottom():
+            self.got(1, 0)
+            self.across(1).start()
+
+        def top():
+            self.got(3, 0)
+            self.across(3).start()
+
+        when(z == 0, bottom)
+        when(z == 3, top)
+        when(z == 2, lambda: self.up(3).wait_send())
+        when(z == 1, lambda: self.down(3).wait_send())
+        self.across(2).wait_send()
+
+    def done(self):
+        z = self.place.z
+        for k in range(4):
+            self.got(k, 1)
+        when(z == 0, lambda: self.across(1).wait_send())
+        when(z == 3, lambda: self.across(3).wait_send())
+
+
+class GatherY:
+    def __init__(self, place, g, send, recv):
+        self.place, self.g, self.send, self.recv = place, g, send, recv
+
+    def site(self, number, way, src, dst):
+        return self.place.copy(self.g.at[src], self.g.at[dst], self.send.at[number], self.recv.at[dst], way)
+
+    def up(self, k):
+        return self.site(k - 1, "up", k - 1, k)
+
+    def down(self, k):
+        return self.site(2 + k, "down", (5 - k) % 4, 4 - k)
+
+    def across(self):
+        return self.place.copy(self.g.at[0, 0], self.g.at[0, 1], self.send.at[6], self.recv.at[4], "y")
+
+    def got(self, k):
+        wait_got(self.g.at[k], self.send.at[0], self.recv.at[k], self.place)
+
+    def t1(self):
+        self.across().start()
+
+    def t2(self):
+        z = self.place.z
+        wait_got(self.g.at[0, 1], self.send.at[0], self.recv.at[4], self.place)
+        when(z < 3, lambda: self.up(1).start())
+        when(z > 0, lambda: self.down(1).start())
+        self.across().wait_send()
+
+    def t3(self):
+        z = self.place.z
+
+        def low():
+            self.got(1)
+            when(z < 3, lambda: self.up(2).start())
+
+        def high():
+            self.got(3)
+            when(z > 0, lambda: self.down(2).start())
+
+        when(z >= 1, low)
+        when(z <= 2, high)
+        when(z < 3, lambda: self.up(1).wait_send())
+        when(z > 0, lambda: self.down(1).wait_send())
+
+    def t4(self):
+        z = self.place.z
+        self.got(2)
+        when(z == 2, lambda: self.up(3).start())
+        when(z == 1, lambda: self.down(3).start())
+        when((z >= 1) & (z < 3), lambda: self.up(2).wait_send())
+        when((z <= 2) & (z > 0), lambda: self.down(2).wait_send())
+
+    def done(self):
+        z = self.place.z
+        when(z == 0, lambda: self.got(1))
+        when(z == 3, lambda: self.got(3))
+        when(z == 2, lambda: self.up(3).wait_send())
+        when(z == 1, lambda: self.down(3).wait_send())
+
+
+def up_to_f32(condition, ref):
+    return jnp.where(condition, ref[...].astype(f32), 0.0)
+
+
+class ReduceY:
+    def __init__(self, place, part, over, ups, downs, send, recv):
+        self.place, self.part, self.over, self.ups, self.downs = place, part, over, ups, downs
+        self.send, self.recv = send, recv
+
+    def across(self):
+        return self.place.copy(self.part.at[:, 1], self.over, self.send.at[0], self.recv.at[0], "y")
+
+    def up(self, s):
+        return self.place.copy(
+            self.part.at[s, 0], self.ups.at[s - 1], self.send.at[2 * s - 1], self.recv.at[s], "up"
+        )
+
+    def down(self, s):
+        return self.place.copy(
+            self.part.at[4 - s, 0], self.downs.at[s - 1], self.send.at[2 * s], self.recv.at[3 + s], "down"
+        )
+
+    def got_up(self, s):
+        wait_got(self.ups.at[s - 1], self.send.at[0], self.recv.at[s], self.place)
+
+    def got_down(self, s):
+        wait_got(self.downs.at[s - 1], self.send.at[0], self.recv.at[3 + s], self.place)
+
+    def local(self, k):
+        return self.part[k, 0].astype(f32) + self.over[k].astype(f32)
+
+    def store(self, k, value):
+        self.part[k, 0] = value.astype(bf16)
+
+    def t1(self):
+        self.across().start()
+
+    def t2(self):
+        z = self.place.z
+        wait_got(self.over, self.send.at[0], self.recv.at[0], self.place)
+
+        def bottom():
+            self.store(1, self.local(1))
+            self.up(1).start()
+
+        def top():
+            self.store(3, self.local(3))
+            self.down(1).start()
+
+        when(z == 0, bottom)
+        when(z == 3, top)
+        self.across().wait_send()
+
+    def t3(self):
+        z = self.place.z
+        when(z == 1, lambda: self.got_up(1))
+        when(z == 2, lambda: self.got_down(1))
+        self.store(
+            2, self.local(2) + up_to_f32(z == 1, self.ups.at[0]) + up_to_f32(z == 2, self.downs.at[0])
+        )
+        when(z <= 1, lambda: self.up(2).start())
+        when(z >= 2, lambda: self.down(2).start())
+        when(z == 0, lambda: self.up(1).wait_send())
+        when(z == 3, lambda: self.down(1).wait_send())
+
+    def t4(self):
+        z = self.place.z
+
+        def low():
+            when(z >= 1, lambda: self.got_up(2))
+            self.store(3, self.local(3) + up_to_f32(z >= 1, self.ups.at[1]))
+            self.up(3).start()
+
+        def high():
+            when(z <= 2, lambda: self.got_down(2))
+            self.store(1, self.local(1) + up_to_f32(z <= 2, self.downs.at[1]))
+            self.down(3).start()
+
+        when(z <= 2, low)
+        when(z >= 1, high)
+        when(z <= 1, lambda: self.up(2).wait_send())
+        when(z >= 2, lambda: self.down(2).wait_send())
+
+    def done(self):
+        z = self.place.z
+        when(z >= 1, lambda: self.got_up(3))
+        when(z <= 2, lambda: self.got_down(3))
+        when(z <= 2, lambda: self.up(3).wait_send())
+        when(z >= 1, lambda: self.down(3).wait_send())
+
+    def total(self):
+        z = self.place.z
+        return self.local(0) + up_to_f32(z >= 1, self.ups.at[2]) + up_to_f32(z <= 2, self.downs.at[2])
+
+
+class ReduceZ:
+    def __init__(self, place, part, over, ups, downs, send, recv):
+        self.place, self.part, self.over, self.ups, self.downs = place, part, over, ups, downs
+        self.send, self.recv = send, recv
+
+    def across(self):
+        return self.place.copy(self.part.at[0, 1], self.over, self.send.at[0], self.recv.at[0], "y")
+
+    def up(self, s):
+        return self.place.copy(self.part.at[s], self.ups.at[s - 1], self.send.at[2 * s - 1], self.recv.at[s], "up")
+
+    def down(self, s):
+        return self.place.copy(
+            self.part.at[4 - s], self.downs.at[s - 1], self.send.at[2 * s], self.recv.at[3 + s], "down"
+        )
+
+    got_up = ReduceY.got_up
+    got_down = ReduceY.got_down
+
+    def add(self, k, *more):
+        value = self.part[k].astype(f32)
+        for term in more:
+            value = value + term
+        self.part[k] = value.astype(bf16)
+
+    def t1(self):
+        z = self.place.z
+        when(z == 0, lambda: self.up(1).start())
+        when(z == 3, lambda: self.down(1).start())
+
+    def t2(self):
+        z = self.place.z
+
+        def low():
+            self.got_up(1)
+            self.add(2, self.ups[0].astype(f32))
+
+        def high():
+            self.got_down(1)
+            self.add(2, self.downs[0].astype(f32))
+
+        when(z == 1, low)
+        when(z == 2, high)
+        when(z <= 1, lambda: self.up(2).start())
+        when(z >= 2, lambda: self.down(2).start())
+        when(z == 0, lambda: self.up(1).wait_send())
+        when(z == 3, lambda: self.down(1).wait_send())
+
+    def t3(self):
+        z = self.place.z
+
+        def low():
+            self.got_up(2)
+            self.add(3, self.ups[1].astype(f32))
+
+        def high():
+            self.got_down(2)
+            self.add(1, self.downs[1].astype(f32))
+
+        when((z >= 1) & (z <= 2), low)
+        when((z >= 1) & (z <= 2), high)
+        when(z <= 2, lambda: self.up(3).start())
+        when(z >= 1, lambda: self.down(3).start())
+        when(z <= 1, lambda: self.up(2).wait_send())
+        when(z >= 2, lambda: self.down(2).wait_send())
+
+    def t4(self):
+        z = self.place.z
+        when(z >= 1, lambda: self.got_up(3))
+        when(z <= 2, lambda: self.got_down(3))
+        value = self.part[0, 1].astype(f32)
+        value = value + up_to_f32(z >= 1, self.ups.at[2, 1]) + up_to_f32(z <= 2, self.downs.at[2, 1])
+        self.part[0, 1] = value.astype(bf16)
+        self.across().start()
+        when(z <= 2, lambda: self.up(3).wait_send())
+        when(z >= 1, lambda: self.down(3).wait_send())
+
+    def done(self):
+        wait_got(self.over, self.send.at[0], self.recv.at[0], self.place)
+        self.across().wait_send()
+
+    def total(self):
+        z = self.place.z
+        value = self.part[0, 0].astype(f32) + self.over[...].astype(f32)
+        return value + up_to_f32(z >= 1, self.ups.at[2, 0]) + up_to_f32(z <= 2, self.downs.at[2, 0])
+
+
+class FramesSum:
+    def __init__(self, place, sent, kept, from_core, from_x, sems, free, number):
+        self.place, self.sent, self.kept, self.from_core, self.from_x = place, sent, kept, from_core, from_x
+        self.sems, self.free, self.number = sems, free, number
+
+    def core(self, j):
+        return self.place.copy(self.sent[j], self.from_core[j], self.sems.at[0, j], self.sems.at[1, j], "core")
+
+    def x(self, j):
+        return self.place.copy(self.kept[j].at[1], self.from_x[j], self.sems.at[2, j], self.sems.at[3, j], "x")
+
+    def out(self, j, outs, p):
+        return pltpu.make_async_copy(self.kept[j].at[0], outs[j].at[p], self.sems.at[4, j])
+
+    def start(self, later):
+        def credit():
+            pl.semaphore_wait(self.free.at[2 * self.number], 1)
+
+        when(later, credit)
+        for j in range(2):
+            self.core(j).start()
+
+    def middle(self, later):
+        for j in range(2):
+            self.core(j).wait_recv()
+
+        def credit():
+            pl.semaphore_wait(self.free.at[2 * self.number + 1], 1)
+
+        when(later, credit)
+        for j in range(2):
+            kept, got = self.kept[j], self.from_core[j]
+            kept[1] = (kept[1].astype(f32) + got[1].astype(f32)).astype(bf16)
+            self.x(j).start()
+        for j in range(2):
+            self.core(j).wait_send()
+
+    def finish(self, outs, p, more):
+        for j in range(2):
+            self.x(j).wait_recv()
+            kept = self.kept[j]
+            total = kept[0].astype(f32) + self.from_core[j][0].astype(f32) + self.from_x[j][...].astype(f32)
+            kept[0] = total.astype(bf16)
+            self.out(j, outs, p).start()
+
+        def credit():
+            for k, way in enumerate(("core", "x")):
+                pl.semaphore_signal(
+                    self.free.at[2 * self.number + k], inc=1, device_id=self.place.device(way), device_id_type=MESH
+                )
+
+        when(more, credit)
+        for j in range(2):
+            self.x(j).wait_send()
+
+    def drained(self, outs, p):
+        for j in range(2):
+            self.out(j, outs, p).wait()
+
+
+def layer_kernel(
+    x_ref, cot_ref, mask_ref, gains_ref, in_w, out_w, gu_w, dn_w,
+    out_hbm, ingrad_hbm, gu_hbm, dn_hbm, iw_hbm, ow_hbm, gain_ref, rows_hbm,
+    g_ffn, g_cot, g_att, p_attn, p_gin, p_ffn, p_back,
+    over_attn, over_gin, over_ffn, over_back, ups_attn, ups_gin, ups_ffn, ups_back,
+    downs_attn, downs_gin, downs_ffn, downs_back,
+    q_s, k_s, v_s, mixed_s, dk_s, dv_s, sc, dp,
+    gu_v, dn_v, owa_v, owe_v, iw_v, xb,
+    act_s, gg_s, gup_s, gmixed_s, gproj_s, hmid_s, ghmid_s, stage,
+    gu_sent, gu_kept, gu_core, gu_x, dn_sent, dn_kept, dn_core, dn_x,
+    iw_sent, iw_kept, iw_core, iw_x, ow_sent, ow_kept, ow_core, ow_x,
+    sem_first, sem_first_got, sem_gather, sem_gather_got, sem_reduce, sem_reduce_got,
+    sem_grad_ffn, sem_grad_att, sem_local, credits, free,
+):
+    place = Place()
+    z, f = place.z, place.f
+    positions, local, depth = x_ref.shape
+    rows = ZN * YN * local
+    last = positions - 1
+    width = q_s.shape[-1]
+    hidden = dn_v.shape[0]
+    half = rows // 2
+    quarter = depth // 4
+    mask = mask_ref[...]
+    scale = HDIM ** (-0.5)
+
+    barrier = pltpu.get_barrier_semaphore()
+
+    def greet(way):
+        pl.semaphore_signal(barrier, inc=1, device_id=place.device(way), device_id_type=MESH)
+
+    for way in ("y", "core", "x"):
+        greet(way)
+    when(z < 3, lambda: greet("up"))
+    when(z > 0, lambda: greet("down"))
+    pl.semaphore_wait(barrier, 3 + (z < 3).astype(jnp.int32) + (z > 0).astype(jnp.int32))
+
+    def load(src, dst, number):
+        return pltpu.make_async_copy(src, dst, sem_local.at[number])
+
+    def load_owa(p):
+        return load(out_w.at[p], owa_v, 0)
+
+    def load_owe(p):
+        return load(out_w.at[p], owe_v, 1)
+
+    def load_iw(p, slot):
+        return load(in_w.at[p], iw_v.at[slot], 2 + slot)
+
+    def load_gu(p):
+        return load(gu_w.at[p], gu_v, 4)
+
+    def load_dn(p):
+        return load(dn_w.at[p], dn_v, 5)
+
+    def load_rows(p, dst, number):
+        return load(rows_hbm.at[p // 4, :, :, (p % 4) // 2, p % 2], dst, number)
+
+    groups = positions // 4
+
+    def normalise(p, c):
+        residual = x_ref[p].astype(f32)
+        value = residual * inverse_rms(residual) * gains_ref[0, p]
+        g_att[p // 8, (p % 8) // 2, p % 2] = value.astype(bf16)
+        return c
+
+    def own_rows(g):
+        return load(g_att.at[g // 2, pl.ds((g % 2) * 2, 2)], rows_hbm.at[g, 0, 0], 10 + g)
+
+    firsts = [
+        GatherZ(place, rows_hbm.at[g], sem_first.at[g], sem_first_got.at[g]) for g in range(groups)
+    ]
+    for g in range(groups):
+        lax.fori_loop(4 * g, 4 * g + 4, normalise, 0)
+        own_rows(g).start()
+        own_rows(g).wait()
+        firsts[g].t1()
+    load_owa(last).start()
+    load_gu(last).start()
+    load_dn(last).start()
+    load_iw(0, 0).start()
+    dk_s[...] = jnp.zeros_like(dk_s)
+    dv_s[...] = jnp.zeros_like(dv_s)
+
+    def project(p, c):
+        slot = lax.rem(p, 2)
+        load_rows(p, g_ffn.at[slot], 6 + slot).wait()
+        load_iw(p, slot).wait()
+
+        @pl.when(lax.rem(p, 4) < 3)
+        def _():
+            load_rows(p + 1, g_ffn.at[1 - slot], 7 - slot).start()
+
+        @pl.when(p < last)
+        def _():
+            load_iw(p + 1, 1 - slot).start()
+
+        block = g_ffn[slot].reshape(rows, depth)
+        q_s[p] = (dot(block, iw_v[slot, 0], NN).astype(bf16) * scale).astype(bf16)
+        k_s[p] = dot(block, iw_v[slot, 1], NN).astype(bf16)
+        v_s[p] = dot(block, iw_v[slot, 2], NN).astype(bf16)
+        return c
+
+    for g in range(groups):
+        firsts[g].t2()
+    for g in range(groups):
+        firsts[g].t3()
+    for g in range(groups):
+        firsts[g].t4()
+    for g in range(groups):
+        firsts[g].done()
+        load_rows(4 * g, g_ffn.at[0], 6).start()
+        lax.fori_loop(4 * g, 4 * g + 4, project, 0)
+    load_owe(last).start()
+    load_iw(last, 0).start()
+    load_rows(last, xb, 8).start()
+
+    row = lax.broadcasted_iota(jnp.int32, (2 * width, width), 0)
+    column = lax.broadcasted_iota(jnp.int32, (2 * width, width), 1)
+    ones = jnp.where((row % width) // HDIM == column // HDIM, 1.0, 0.0).astype(bf16)
+
+    def per_head(product):
+        high = product.astype(bf16)
+        low = (product - high.astype(f32)).astype(bf16)
+        return dot(jnp.concatenate([high, low], axis=1), ones, NN)
+
+    def scores_of(p, q, at):
+        def two(jj, top):
+            first = per_head(q * k_s[2 * jj, at].astype(f32))
+            second = per_head(q * k_s[2 * jj + 1, at].astype(f32))
+            second = jnp.where(2 * jj + 1 <= p, second, -1e30)
+            sc[2 * jj], sc[2 * jj + 1] = first, second
+            return jnp.maximum(top, jnp.maximum(first, second))
+
+        return lax.fori_loop(0, p // 2 + 1, two, jnp.full((half, width), -1e30, f32))
+
+    def attend_one(p):
+        pairs = p // 2 + 1
+        for part in range(2):
+            at = pl.ds(part * half, half)
+            q = q_s[p, at].astype(f32)
+            top = scores_of(p, q, at)
+
+            def raise_two(jj, total):
+                for t in range(2):
+                    raised = jnp.exp(sc[2 * jj + t] - top)
+                    sc[2 * jj + t] = raised
+                    total = total + raised
+                return total
+
+            total = lax.fori_loop(0, pairs, raise_two, jnp.zeros((half, width), f32))
+            factor = 1.0 / total
+
+            def mix_two(jj, out):
+                for t in range(2):
+                    probs = (sc[2 * jj + t] * factor).astype(bf16).astype(f32)
+                    out = out + probs * v_s[2 * jj + t, at].astype(f32)
+                return out
+
+            out = lax.fori_loop(0, pairs, mix_two, jnp.zeros((half, width), f32))
+            mixed_s[p, at] = out.astype(bf16)
+
+    def attend_back_one(p):
+        pairs = p // 2 + 1
+        for part in range(2):
+            at = pl.ds(part * half, half)
+            q = q_s[p, at].astype(f32)
+            g = gmixed_s[at].astype(f32)
+            top = scores_of(p, q, at)
+
+            def raise_two(jj, carry):
+                total, weighted = carry
+                for t in range(2):
+                    raised = jnp.exp(sc[2 * jj + t] - top)
+                    sc[2 * jj + t] = raised
+                    grad_probs = per_head(g * v_s[2 * jj + t, at].astype(f32))
+                    dp[2 * jj + t] = grad_probs
+                    total = total + raised
+                    weighted = weighted + raised * grad_probs
+                return total, weighted
+
+            zero = jnp.zeros((half, width), f32)
+            total, weighted = lax.fori_loop(0, pairs, raise_two, (zero, zero))
+            factor = 1.0 / total
+            centre = weighted * factor
+
+            def back_two(jj, dq):
+                for t in range(2):
+                    j = 2 * jj + t
+                    probs = sc[j] * factor
+                    grad = (probs * (dp[j] - centre)).astype(bf16).astype(f32)
+                    dq = dq + grad * k_s[j, at].astype(f32)
+                    dk_s[j, at] = dk_s[j, at] + grad * q
+                    dv_s[j, at] = dv_s[j, at] + probs.astype(bf16).astype(f32) * g
+                return dq
+
+            dq = lax.fori_loop(0, pairs, back_two, zero)
+            gproj_s[0, at] = (dq * scale).astype(bf16)
+        gproj_s[1] = dk_s[p].astype(bf16)
+        gproj_s[2] = dv_s[p].astype(bf16)
+
+    blocks = (ZN, YN, local, depth)
+    grad_ffn = FramesSum(
+        place, (gu_sent, dn_sent), (gu_kept, dn_kept), (gu_core, dn_core), (gu_x, dn_x), sem_grad_ffn, free, 0
+    )
+    grad_att = FramesSum(
+        place, (iw_sent, ow_sent), (iw_kept, ow_kept), (iw_core, ow_core), (iw_x, ow_x), sem_grad_att, free, 1
+    )
+    ffn_outs, att_outs = (gu_hbm, dn_hbm), (iw_hbm, ow_hbm)
+
+    def step(s, c):
+        now = lax.rem(s, 2)
+        then = 1 - now
+
+        def valid(delay):
+            return (s >= delay) & (s <= last + delay)
+
+        def pos(delay):
+            return last - (s - delay)
+
+        def ring(delay):
+            return lax.rem(s - delay + 8, 4)
+
+        gather_ffn = GatherZ(place, g_ffn.at[now], sem_gather.at[0], sem_gather_got.at[0, now])
+        gather_cot = GatherY(place, g_cot.at[now], sem_gather.at[1], sem_gather_got.at[1, now])
+        gather_att = GatherY(place, g_att.at[now], sem_gather.at[2], sem_gather_got.at[2, now])
+
+        def reducing(kind, part, over, ups, downs, number, which):
+            return kind(
+                place, part, over.at[which], ups.at[which], downs.at[which],
+                sem_reduce.at[number], sem_reduce_got.at[number, which],
+            )
+
+        attn_now = reducing(ReduceY, p_attn, over_attn, ups_attn, downs_attn, 0, now)
+        attn_then = reducing(ReduceY, p_attn, over_attn, ups_attn, downs_attn, 0, then)
+        gin_now = reducing(ReduceY, p_gin, over_gin, ups_gin, downs_gin, 1, now)
+        gin_then = reducing(ReduceY, p_gin, over_gin, ups_gin, downs_gin, 1, then)
+        ffn_now = reducing(ReduceZ, p_ffn.at[now], over_ffn, ups_ffn, downs_ffn, 2, now)
+        ffn_then = reducing(ReduceZ, p_ffn.at[then], over_ffn, ups_ffn, downs_ffn, 2, then)
+        back_now = reducing(ReduceY, p_back.at[now], over_back, ups_back, downs_back, 3, now)
+        back_then = reducing(ReduceY, p_back.at[then], over_back, ups_back, downs_back, 3, then)
+
+        @pl.when(s >= 1)
+        def _():
+            pl.semaphore_wait(credits.at[0], 1)
+            when(z > 0, lambda: pl.semaphore_wait(credits.at[1], 1))
+            when(z < 3, lambda: pl.semaphore_wait(credits.at[2], 1))
+
+        @pl.when(valid(1))
+        def _():
+            p = pos(1)
+            g_cot[now, 0, 0] = (mask * cot_ref[p].astype(f32)).astype(bf16)
+            gather_cot.t1()
+            attn_then.done()
+            hmid = x_ref[p].astype(f32) + mask * attn_then.total()
+            hmid_s[ring(1)] = hmid
+            g_ffn[now, 0, 0] = (hmid * inverse_rms(hmid) * gains_ref[1, p]).astype(bf16)
+            gather_ffn.t1()
+
+        @pl.when(valid(3))
+        def _():
+            p = pos(3)
+            gin_then.done()
+            hmid = hmid_s[ring(3)]
+            factor = inverse_rms(hmid)
+            grad = cot_ref[p].astype(f32) + norm_back(gin_then.total(), hmid * factor, factor, gains_ref[1, p])
+            ghmid_s[ring(3)] = grad
+            g_att[now, 0, 0] = (mask * grad).astype(bf16)
+            gather_att.t1()
+
+        @pl.when(valid(0))
+        def _():
+            p = pos(0)
+            attend_one(p)
+            load_owa(p).wait()
+            p_attn[...] = dot(mixed_s[p], owa_v[...], NN).astype(bf16).reshape(blocks)
+            attn_now.t1()
+            when(s < last, lambda: load_owa(p - 1).start())
+
+        when(valid(1), gather_cot.t2)
+        when(valid(1), gather_ffn.t2)
+        when(valid(3), gather_att.t2)
+        when(valid(3), ffn_then.t3)
+        when(valid(5), back_then.t2)
+
+        @pl.when(valid(2))
+        def _():
+            p = pos(2)
+            load_gu(p).wait()
+            load_dn(p).wait()
+            x = g_ffn[then].reshape(rows, depth)
+            g = g_cot[then].reshape(rows, depth)
+            for h in range(2):
+                at = slice(h * hidden // 2, (h + 1) * hidden // 2)
+                gate = dot(x, gu_v[0, :, at], NN)
+                up = dot(x, gu_v[1, :, at], NN)
+                grad_act = dot(g, dn_v[at], NT)
+                sigma = 1.0 / (1.0 + jnp.exp(-gate))
+                silu = gate * sigma
+                act_s[:, at] = (silu * up).astype(bf16)
+                gg_s[:, at] = (grad_act * up * sigma * (1.0 + gate * (1.0 - sigma))).astype(bf16)
+                gup_s[:, at] = (grad_act * silu).astype(bf16)
+            back = dot(gg_s[...], gu_v[0], NT) + dot(gup_s[...], gu_v[1], NT)
+            p_gin[...] = back.astype(bf16).reshape(blocks)
+            gin_now.t1()
+            gain_ref[1, p] = jnp.sum(back * x.astype(f32), axis=0, keepdims=True)
+            p_ffn[now] = dot(act_s[...], dn_v[...], NN).astype(bf16).reshape(blocks)
+            ffn_now.t1()
+
+            @pl.when(s < last + 2)
+            def _():
+                load_gu(p - 1).start()
+                load_dn(p - 1).start()
+
+        when(valid(1), gather_cot.t3)
+        when(valid(1), gather_ffn.t3)
+        when(valid(3), gather_att.t3)
+        when(valid(0), attn_now.t2)
+        when(valid(3), ffn_then.t4)
+        when(valid(5), back_then.t3)
+        when(valid(3), lambda: grad_ffn.finish(ffn_outs, pos(3), s < last + 3))
+
+        @pl.when(valid(4))
+        def _():
+            p = pos(4)
+            load_owe(p).wait()
+            load_iw(p, 0).wait()
+            load_rows(p, xb, 8).wait()
+            gmixed_s[...] = dot(g_att[then].reshape(rows, depth), owe_v[...], NT).astype(bf16)
+            attend_back_one(p)
+            back = dot(gproj_s[0], iw_v[0, 0], NT)
+            back = back + dot(gproj_s[1], iw_v[0, 1], NT)
+            back = back + dot(gproj_s[2], iw_v[0, 2], NT)
+            p_back[now] = back.astype(bf16).reshape(blocks)
+            back_now.t1()
+            gain_ref[0, p] = jnp.sum(back * xb[...].reshape(rows, depth).astype(f32), axis=0, keepdims=True)
+
+        when(valid(1), gather_cot.t4)
+        when(valid(1), gather_ffn.t4)
+        when(valid(3), gather_att.t4)
+        when(valid(0), attn_now.t3)
+        when(valid(2), gin_now.t2)
+        when(valid(2), ffn_now.t2)
+        when(valid(5), back_then.t4)
+
+        def out_copy(p):
+            return pltpu.make_async_copy(stage.at[0], out_hbm.at[p], sem_local.at[14])
+
+        def ingrad_copy(p):
+            return pltpu.make_async_copy(stage.at[1], ingrad_hbm.at[p], sem_local.at[15])
+
+        @pl.when(valid(3))
+        def _():
+            ffn_then.done()
+            stage[0] = (hmid_s[ring(3)] + mask * ffn_then.total()).astype(bf16)
+            out_copy(pos(3)).start()
+
+        @pl.when(valid(3))
+        def _():
+            grad_ffn.drained(ffn_outs, pos(3))
+
+        @pl.when(valid(2))
+        def _():
+            for r in range(4):
+                at = piece_at(r, f, quarter)
+                gu_to, dn_to = (gu_kept, dn_kept) if r % 2 == 0 else (gu_sent, dn_sent)
+                columns = g_ffn[then, :, :, :, at].reshape(rows, quarter)
+                gu_to[r // 2, 0] = dot(columns, gg_s[...], TN).astype(bf16)
+                gu_to[r // 2, 1] = dot(columns, gup_s[...], TN).astype(bf16)
+                dn_to[r // 2] = dot(act_s[...], g_cot[then, :, :, :, at].reshape(rows, quarter), TN).astype(bf16)
+            grad_ffn.start(s > 2)
+
+        when(valid(0), attn_now.t4)
+        when(valid(2), gin_now.t3)
+
+        @pl.when(valid(5))
+        def _():
+            p = pos(5)
+            back_then.done()
+            residual = x_ref[p].astype(f32)
+            factor = inverse_rms(residual)
+            grad = norm_back(back_then.total(), residual * factor, factor, gains_ref[0, p])
+            stage[1] = (ghmid_s[ring(5)] + grad).astype(bf16)
+            ingrad_copy(p).start()
+            grad_att.finish(att_outs, p, s < last + 5)
+            grad_att.drained(att_outs, p)
+
+        @pl.when(valid(4))
+        def _():
+            p = pos(4)
+            for r in range(4):
+                at = piece_at(r, f, quarter)
+                iw_to, ow_to = (iw_kept, ow_kept) if r % 2 == 0 else (iw_sent, ow_sent)
+                columns = xb[:, :, :, at].reshape(rows, quarter)
+                for j in range(3):
+                    iw_to[r // 2, j] = dot(columns, gproj_s[j], TN).astype(bf16)
+                ow_to[r // 2] = dot(mixed_s[p], g_att[then, :, :, :, at].reshape(rows, quarter), TN).astype(bf16)
+            grad_att.start(s > 4)
+
+            @pl.when(s < last + 4)
+            def _():
+                load_owe(p - 1).start()
+                load_iw(p - 1, 0).start()
+                load_rows(p - 1, xb, 8).start()
+
+        @pl.when(s < last + 5)
+        def _():
+            def tell(number, way):
+                pl.semaphore_signal(credits.at[number], inc=1, device_id=place.device(way), device_id_type=MESH)
+
+            tell(0, "y")
+            when(z < 3, lambda: tell(1, "up"))
+            when(z > 0, lambda: tell(2, "down"))
+
+        when(valid(2), lambda: grad_ffn.middle(s > 2))
+        when(valid(2), gin_now.t4)
+        when(valid(1), gather_cot.done)
+        when(valid(1), gather_ffn.done)
+        when(valid(3), gather_att.done)
+        when(valid(4), lambda: grad_att.middle(s > 4))
+        when(valid(3), lambda: out_copy(pos(3)).wait())
+        when(valid(5), lambda: ingrad_copy(pos(5)).wait())
+        return c
+
+    lax.fori_loop(0, positions + 5, step, 0)
+
+
+def layer(x, cot, mask, gains, in_weight, out_weight, gate_up, down):
+    positions, local, depth = x.shape
+    width, hidden = out_weight.shape[1], down.shape[1]
+    rows = ZN * YN * local
+    quarter = depth // 4
+    block = (local, depth)
+    groups = positions // 4
+
+    def vm(*shape, dtype=bf16):
+        return pltpu.VMEM(shape, dtype)
+
+    def hbm(*shape, dtype=bf16):
+        return jax.ShapeDtypeStruct(shape, dtype)
+
+    everything = (ZN, YN) + block
+    scratch = (
+        [vm(2, *everything)] * 3
+        + [vm(*everything)] * 2
+        + [vm(2, *everything)] * 2
+        + [vm(2, ZN, *block)] * 2
+        + [vm(2, *block), vm(2, ZN, *block)]
+        + [vm(2, 3, *block), vm(2, 3, *block), vm(2, 3, YN, *block), vm(2, 3, *block)] * 2
+        + [vm(positions, rows, width)] * 4
+        + [vm(positions, rows, width, dtype=f32)] * 2
+        + [vm(positions, rows // 2, width, dtype=f32)] * 2
+        + [vm(2, depth, hidden), vm(hidden, depth), vm(width, depth), vm(width, depth)]
+        + [vm(2, 3, depth, width), vm(*everything)]
+        + [vm(rows, hidden)] * 3
+        + [vm(rows, width), vm(3, rows, width)]
+        + [vm(4, *block, dtype=f32)] * 2
+        + [vm(2, *block)]
+        + [vm(2, 2, quarter, hidden)] * 3
+        + [vm(2, quarter, hidden)]
+        + [vm(2, hidden, quarter)] * 3
+        + [vm(hidden, quarter)]
+        + [vm(2, 3, quarter, width)] * 3
+        + [vm(3, quarter, width)]
+        + [vm(2, width, quarter)] * 3
+        + [vm(width, quarter)]
+        + [
+            pltpu.SemaphoreType.DMA((groups, 10)),
+            pltpu.SemaphoreType.DMA((groups, 8)),
+            pltpu.SemaphoreType.DMA((3, 10)),
+            pltpu.SemaphoreType.DMA((3, 2, 8)),
+            pltpu.SemaphoreType.DMA((4, 7)),
+            pltpu.SemaphoreType.DMA((4, 2, 7)),
+            pltpu.SemaphoreType.DMA((5, 2)),
+            pltpu.SemaphoreType.DMA((5, 2)),
+            pltpu.SemaphoreType.DMA((16,)),
+            pltpu.SemaphoreType.REGULAR((3,)),
+            pltpu.SemaphoreType.REGULAR((4,)),
+        ]
+    )
+    in_vmem = pl.BlockSpec(memory_space=pltpu.VMEM)
+    anywhere = pl.BlockSpec(memory_space=pl.ANY)
+    return pl.pallas_call(
+        layer_kernel,
+        in_specs=[in_vmem] * 4 + [anywhere] * 4,
+        out_specs=[anywhere] * 6 + [in_vmem, anywhere],
+        out_shape=[
+            hbm(positions, *block),
+            hbm(positions, *block),
+            hbm(positions, 2, quarter, hidden),
+            hbm(positions, hidden, quarter),
+            hbm(positions, 3, quarter, width),
+            hbm(positions, width, quarter),
+            hbm(2, positions, 1, depth, dtype=f32),
+            hbm(groups, ZN, YN, 2, 2, *block),
+        ],
+        scratch_shapes=scratch,
+        compiler_params=pltpu.CompilerParams(
+            collective_id=0, has_side_effects=True, vmem_limit_bytes=KERNEL_VMEM_BYTES
+        ),
+        name="layer",
+    )(x, cot, mask, gains, in_weight, out_weight, gate_up, down)
+
+
+def body_in_one(inputs, counts, norm_gains, in_weight, out_weight, gate_up, down_weight, cotangent):
+    group_size = lax.axis_size("mp")
+    local = inputs.shape[0]
+    ids = lax.axis_index("mp") * local + jnp.arange(local)
+    mask = (ids < counts[0]).astype(f32)[:, None]
+    output, input_grad, g_gu, g_dn, g_in, g_out, gain_sums, _ = layer(
+        jnp.swapaxes(inputs, 0, 1),
+        jnp.swapaxes(cotangent, 0, 1),
+        mask,
+        norm_gains[:, :, None, :],
+        in_weight,
+        out_weight,
+        gate_up,
+        down_weight,
+    )
+    terms = gain_sums[:, :, 0] / norm_gains
+    terms = lax.psum_scatter(terms, "frames", scatter_dimension=2, tiled=True)
+    step = 1
+    while step < group_size:
+        terms = terms + lax.ppermute(terms, "mp", [(i, i ^ step) for i in range(group_size)])
+        step *= 2
+    return (
+        jnp.swapaxes(output, 0, 1),
+        jnp.swapaxes(input_grad, 0, 1),
+        g_in.astype(f32),
+        g_out.astype(f32),
+        g_gu.astype(f32),
+        g_dn.astype(f32),
+        terms,
+    )
+
+
 def solution(mesh):
     placed = (
         P(("frames", "mp"), None, None),
@@ -571,8 +1544,15 @@
         P(None, "mp", None),
         P(("frames", "mp"), None, None),
     )
+    def local_body(*args):
+        frames, group_size = lax.axis_size("frames"), lax.axis_size("mp")
+        local, positions, depth = args[0].shape
+        width, hidden = args[4].shape[1], args[6].shape[1]
+        one = fits(frames, group_size, local, positions, depth, width, hidden)
+        return (body_in_one if one else body)(*args)
+
     return jax.shard_map(
-        body,
+        local_body,
         mesh=mesh,
         in_specs=placed,
         out_specs=(

time: 2160 us -> 1100 us (0.51)
  waiting for transfers between devices: 761 us -> 23.9 us
  Pallas kernels: 330 us -> 1020 us
  starting transfers between devices: 548 us -> 5.71 us
  other arithmetic: 309 us -> 24.9 us
  local copies, waits for them, and re-layouts: 175 us -> 11.4 us
    ppermute x259 -> x3, waiting for transfers between devices: 742 us -> 5.11 us  [body_in_one(): lax.ppermute(terms, 'mp', [(i, i ^ step) for i in range(group_size)])]
    pallas_call x16 -> x1, Pallas kernels: 330 us -> 1020 us  [layer(): pl.pallas_call(layer_kernel, in_specs=[in_vmem] * 4 + [anywhere] * 4, out...]
    ppermute x259 -> x3, starting transfers between devices: 548 us -> 5.67 us  [body_in_one(): lax.ppermute(terms, 'mp', [(i, i ^ step) for i in range(group_size)])]
    another operation x99 -> x0, other arithmetic: 133 us -> none  [the longest x28 64.9 us: gather(): return jnp.stack(self.y.gather(column), axis=1)]
    convert_element_type x83 -> x5, other arithmetic: 88.8 us -> 21.9 us  [the longest x1 12 us: body_in_one(): g_gu.astype(f32)]
    another operation x28 -> x0, local copies, waits for them, and re-layouts: 50.2 us -> none  [the longest x14 37.6 us: gather(): return jnp.stack(self.y.gather(column), axis=1)]
    unnamed x415 -> x14, local copies, waits for them, and re-layouts: 53.5 us -> 4.46 us
    slice x39 -> x0, local copies, waits for them, and re-layouts: 33.4 us -> none  [the longest x12 14.6 us: row(): return jnp.stack([part[:, k] for part in parts], axis=1).astype(f32)]
  transfers between devices with their start and end apart: 260 -> 4, of which waited for: 92 -> 3; matrix products, arithmetic and copies ran while one was open for 21% -> 2% of each run, Pallas kernels for 14% -> 0%
where the time goes in v2:
time: 1100 us
  Pallas kernels  1020 us (93%)
  other arithmetic  24.9 us (2%)
  waiting for transfers between devices  23.9 us (2%)
  between operations  14.7 us (1%)
  local copies, waits for them, and re-layouts  11.4 us (1%)
    pallas_call x1, Pallas kernels, layer(): pl.pallas_call(layer_kernel, in_specs=[in_vmem] * 4 + [anywhere] * 4, out...  1020 us
  transfers between devices with their start and end apart: 4, of which 3 were waited for; matrix products, arithmetic and copies ran while one was open for 2% of the time, Pallas kernels for 0%

profile of v2, /device:TPU:0, one launch (start us, length us, event | category | flops | bytes accessed | tf_op | source)
XLA Modules:
  0.0 1099.2 jit_solution(7508858967033353807)
XLA Ops:
  7.2 0.0 reduce-scatter.2.cloned.1.call-start
  7.2 1.7 broadcast_in_dim.4.gains_ref
  9.5 5.3 copy_bitcast_fusion
  14.8 0.6 fusion.mask_ref
  15.4 0.0 copy-start.5
  15.4 1018.6 %layer.1 = (bf16[16,48,1024]{2,1,0:T(8,128)(2,1)}, bf16[16,48,1024]{2,1,0:T(8,128)(2,1)}, bf16[16,2,256,512]{3,2,1,0:T(8,128)(2,1)}, bf16[16,512,256]{2,1,0:T(8,...) custom-call(bf16[16,48,1024]{2,1,0:T(8,128)(2,1)} %get-tuple-element, ...), custom_call_target="tpu_custom_call" | custom-call | tf_op jit(solution)/shard_map/layer/pallas_call | solution.py:1482
  1034.0 0.0 copy-done.5
  1034.0 1.6 bitcast_divide_fusion
  1035.6 0.0 reduce-scatter.2.cloned.1.call-update
  1035.6 18.8 %reduce-scatter.2.cloned.1.call-done = f32[2,16,256]{2,1,0:T(8,128)} async-done(((f32[2,16,1024]{2,1,0:T(8,128)}), f32[2,16,256]{2,1,0:T(8,128)}) %reduce-scatter.2.cloned.1.call-update) | async-done | bytes 32784 | tf_op jit(solution)/shard_map/reduce_scatter | solution.py:1520
  1054.4 1.5 collective-permute-start
  1055.9 2.7 collective-permute-done
  1058.6 0.8 add.26
  1059.3 1.5 collective-permute-start.1
  1060.8 2.4 collective-permute-done.1
  1063.2 2.7 collective-permute-start.2
  1066.0 0.0 copy-start
  1066.0 12.0 %convert_element_type.25 = f32[16,2,256,512]{3,2,1,0:T(8,128)} convert(bf16[16,2,256,512]{3,2,1,0:T(8,128)(2,1)} %get-tuple-element.18) | non-fusion elementwise | flops 4194304 | bytes 25165824 | tf_op jit(solution)/shard_map/convert_element_type | solution.py:1530
  1078.0 0.0 copy-done
  1078.0 0.0 copy-start.1
  1078.0 4.3 convert_element_type.26
  1082.3 0.0 copy-done.1
  1082.3 0.0 copy-start.4
  1082.3 3.5 convert_element_type.23
  1085.7 0.0 copy-start.3
  1085.7 0.0 copy-done.4
  1085.8 1.5 convert_element_type.24
  1087.3 0.0 copy-start.2
  1087.3 0.4 copy-done.3
  1087.7 2.0 copy.22
  1089.7 0.0 copy-done.2
  1089.7 2.0 copy.23
  1091.7 0.0 collective-permute-done.2
  1091.7 0.6 add.28
  (1 shorter events, 0.0 us)
Async XLA Ops:
  7.2 1047.3 %reduce-scatter.2.cloned.1.call-start = ((), (), s32[]{:S(2)}) async-start(), calls=%async_computation.1 | async-start | bytes 163840 | tf_op jit(solution)/shard_map/reduce_scatter | solution.py:1520
  15.4 1018.6 %copy-start.5 = (f32[2,16,1024]{2,1,0:T(8,128)S(1)}, f32[2,16,1024]{2,1,0:T(8,128)}, u32[]{:S(2)}) copy-start(f32[2,16,1024]{2,1,0:T(8,128)} %param.10) | copy-start | bytes 393220
  1054.4 4.1 collective-permute-start
  1059.3 3.9 collective-permute-start.1
  1063.2 28.5 %collective-permute-start.2 = (f32[2,16,256]{2,1,0:T(8,128)S(1)}, f32[2,16,256]{2,1,0:T(8,128)S(1)}, u32[]{:S(2)}, u32[]{:S(2)}) collective-permute-start(f32[2,16,256]{2,1,0:T(8,128)S(1)} %add.27), channel_id=1, source_target_pairs={{0,4},{1,5},{2,6},{3,7},{4,0},{5,1},{6,2},{7,3},{8,12},{9,13},{10,... | collective-permute-start | bytes 98312 | tf_op jit(solution)/shard_map/ppermute | solution.py:1523
  1066.0 12.0 %copy-start = (bf16[16,512,256]{2,1,0:T(8,128)(2,1)S(1)}, bf16[16,512,256]{2,1,0:T(8,128)(2,1)}, u32[]{:S(2)}) copy-start(bf16[16,512,256]{2,1,0:T(8,128)(2,1)} %get-tuple-element.19) | copy-start | bytes 12582916
  1078.0 4.3 copy-start.1
  1082.3 3.5 copy-start.4
  1085.7 2.0 copy-start.3
  1087.3 2.4 copy-start.2
Sparse Core Ops, SparseCore 0:
  1035.8 18.6 reduce-scatter.1

commit v3 on v2

--- a/solution.py
+++ b/solution.py
@@ -588,6 +588,8 @@
             "down": ("mp", self.m - YN),
             "core": ("frames", self.f ^ 1),
             "x": ("frames", self.f ^ 2),
+            "pair": ("mp", self.m ^ YN),
+            "far": ("mp", self.m ^ (2 * YN)),
         }
 
     def device(self, way):
@@ -654,9 +656,6 @@
 
         when(z >= 1, low)
         when(z <= 2, high)
-        when(z < 3, lambda: self.up(1).wait_send())
-        when(z > 0, lambda: self.down(1).wait_send())
-        self.across(0).wait_send()
 
     def t3(self):
         z = self.place.z
@@ -664,10 +663,6 @@
         when(z == 2, lambda: self.up(3).start())
         when(z == 1, lambda: self.down(3).start())
         self.across(2).start()
-        when((z >= 1) & (z < 3), lambda: self.up(2).wait_send())
-        when((z <= 2) & (z > 0), lambda: self.down(2).wait_send())
-        when(z >= 1, lambda: self.across(1).wait_send())
-        when(z <= 2, lambda: self.across(3).wait_send())
 
     def t4(self):
         z = self.place.z
@@ -682,16 +677,19 @@
 
         when(z == 0, bottom)
         when(z == 3, top)
+
+    def done(self):
+        z = self.place.z
+        for k in range(4):
+            self.got(k, 1)
+        when(z < 3, lambda: self.up(1).wait_send())
+        when(z > 0, lambda: self.down(1).wait_send())
+        when((z >= 1) & (z < 3), lambda: self.up(2).wait_send())
+        when((z >= 1) & (z < 3), lambda: self.down(2).wait_send())
         when(z == 2, lambda: self.up(3).wait_send())
         when(z == 1, lambda: self.down(3).wait_send())
-        self.across(2).wait_send()
-
-    def done(self):
-        z = self.place.z
         for k in range(4):
-            self.got(k, 1)
-        when(z == 0, lambda: self.across(1).wait_send())
-        when(z == 3, lambda: self.across(3).wait_send())
+            self.across(k).wait_send()
 
 
 class GatherY:
@@ -721,7 +719,6 @@
         wait_got(self.g.at[0, 1], self.send.at[0], self.recv.at[4], self.place)
         when(z < 3, lambda: self.up(1).start())
         when(z > 0, lambda: self.down(1).start())
-        self.across().wait_send()
 
     def t3(self):
         z = self.place.z
@@ -736,23 +733,24 @@
 
         when(z >= 1, low)
         when(z <= 2, high)
-        when(z < 3, lambda: self.up(1).wait_send())
-        when(z > 0, lambda: self.down(1).wait_send())
 
     def t4(self):
         z = self.place.z
         self.got(2)
         when(z == 2, lambda: self.up(3).start())
         when(z == 1, lambda: self.down(3).start())
-        when((z >= 1) & (z < 3), lambda: self.up(2).wait_send())
-        when((z <= 2) & (z > 0), lambda: self.down(2).wait_send())
 
     def done(self):
         z = self.place.z
         when(z == 0, lambda: self.got(1))
         when(z == 3, lambda: self.got(3))
+        when(z < 3, lambda: self.up(1).wait_send())
+        when(z > 0, lambda: self.down(1).wait_send())
+        when((z >= 1) & (z < 3), lambda: self.up(2).wait_send())
+        when((z >= 1) & (z < 3), lambda: self.down(2).wait_send())
         when(z == 2, lambda: self.up(3).wait_send())
         when(z == 1, lambda: self.down(3).wait_send())
+        self.across().wait_send()
 
 
 def up_to_f32(condition, ref):
@@ -764,18 +762,21 @@
         self.place, self.part, self.over, self.ups, self.downs = place, part, over, ups, downs
         self.send, self.recv = send, recv
 
-    def across(self):
-        return self.place.copy(self.part.at[:, 1], self.over, self.send.at[0], self.recv.at[0], "y")
+    def across(self, k):
+        return self.place.copy(self.part.at[k, 1], self.over.at[k], self.send.at[6 + k], self.recv.at[7 + k], "y")
 
     def up(self, s):
         return self.place.copy(
-            self.part.at[s, 0], self.ups.at[s - 1], self.send.at[2 * s - 1], self.recv.at[s], "up"
+            self.part.at[s, 0], self.ups.at[s - 1], self.send.at[2 * s - 2], self.recv.at[s], "up"
         )
 
     def down(self, s):
         return self.place.copy(
-            self.part.at[4 - s, 0], self.downs.at[s - 1], self.send.at[2 * s], self.recv.at[3 + s], "down"
+            self.part.at[4 - s, 0], self.downs.at[s - 1], self.send.at[2 * s - 1], self.recv.at[3 + s], "down"
         )
+
+    def got_over(self, k):
+        wait_got(self.over.at[k], self.send.at[0], self.recv.at[7 + k], self.place)
 
     def got_up(self, s):
         wait_got(self.ups.at[s - 1], self.send.at[0], self.recv.at[s], self.place)
@@ -790,26 +791,28 @@
         self.part[k, 0] = value.astype(bf16)
 
     def t1(self):
-        self.across().start()
+        for k in (1, 3, 2, 0):
+            self.across(k).start()
 
     def t2(self):
         z = self.place.z
-        wait_got(self.over, self.send.at[0], self.recv.at[0], self.place)
 
         def bottom():
+            self.got_over(1)
             self.store(1, self.local(1))
             self.up(1).start()
 
         def top():
+            self.got_over(3)
             self.store(3, self.local(3))
             self.down(1).start()
 
         when(z == 0, bottom)
         when(z == 3, top)
-        self.across().wait_send()
 
     def t3(self):
         z = self.place.z
+        self.got_over(2)
         when(z == 1, lambda: self.got_up(1))
         when(z == 2, lambda: self.got_down(1))
         self.store(
@@ -817,33 +820,38 @@
         )
         when(z <= 1, lambda: self.up(2).start())
         when(z >= 2, lambda: self.down(2).start())
-        when(z == 0, lambda: self.up(1).wait_send())
-        when(z == 3, lambda: self.down(1).wait_send())
 
     def t4(self):
         z = self.place.z
 
         def low():
+            self.got_over(3)
             when(z >= 1, lambda: self.got_up(2))
             self.store(3, self.local(3) + up_to_f32(z >= 1, self.ups.at[1]))
             self.up(3).start()
 
         def high():
+            self.got_over(1)
             when(z <= 2, lambda: self.got_down(2))
             self.store(1, self.local(1) + up_to_f32(z <= 2, self.downs.at[1]))
             self.down(3).start()
 
         when(z <= 2, low)
         when(z >= 1, high)
+
+    def done(self):
+        z = self.place.z
+        self.got_over(0)
+        when(z >= 1, lambda: self.got_up(3))
+        when(z <= 2, lambda: self.got_down(3))
+        when(z == 0, lambda: self.up(1).wait_send())
+        when(z == 3, lambda: self.down(1).wait_send())
         when(z <= 1, lambda: self.up(2).wait_send())
         when(z >= 2, lambda: self.down(2).wait_send())
-
-    def done(self):
-        z = self.place.z
-        when(z >= 1, lambda: self.got_up(3))
-        when(z <= 2, lambda: self.got_down(3))
         when(z <= 2, lambda: self.up(3).wait_send())
         when(z >= 1, lambda: self.down(3).wait_send())
+        for k in range(4):
+            self.across(k).wait_send()
 
     def total(self):
         z = self.place.z
@@ -895,8 +903,6 @@
         when(z == 2, high)
         when(z <= 1, lambda: self.up(2).start())
         when(z >= 2, lambda: self.down(2).start())
-        when(z == 0, lambda: self.up(1).wait_send())
-        when(z == 3, lambda: self.down(1).wait_send())
 
     def t3(self):
         z = self.place.z
@@ -913,8 +919,6 @@
         when((z >= 1) & (z <= 2), high)
         when(z <= 2, lambda: self.up(3).start())
         when(z >= 1, lambda: self.down(3).start())
-        when(z <= 1, lambda: self.up(2).wait_send())
-        when(z >= 2, lambda: self.down(2).wait_send())
 
     def t4(self):
         z = self.place.z
@@ -924,11 +928,16 @@
         value = value + up_to_f32(z >= 1, self.ups.at[2, 1]) + up_to_f32(z <= 2, self.downs.at[2, 1])
         self.part[0, 1] = value.astype(bf16)
         self.across().start()
+
+    def done(self):
+        wait_got(self.over, self.send.at[0], self.recv.at[0], self.place)
+        z = self.place.z
+        when(z == 0, lambda: self.up(1).wait_send())
+        when(z == 3, lambda: self.down(1).wait_send())
+        when(z <= 1, lambda: self.up(2).wait_send())
+        when(z >= 2, lambda: self.down(2).wait_send())
         when(z <= 2, lambda: self.up(3).wait_send())
         when(z >= 1, lambda: self.down(3).wait_send())
-
-    def done(self):
-        wait_got(self.over, self.send.at[0], self.recv.at[0], self.place)
         self.across().wait_send()
 
     def total(self):
@@ -997,19 +1006,63 @@
             self.out(j, outs, p).wait()
 
 
+COT_GATHER = GatherZ
+FFN_GATHER = GatherY
+ATT_GATHER = GatherY
+ATTN_REDUCE = ReduceY
+GIN_REDUCE = ReduceY
+FFN_REDUCE = ReduceZ
+BACK_REDUCE = ReduceY
+
+SCHEDULE = (
+    ("Fm", 3), ("RF3", 3), ("RA5", 1), ("RG5", 3), ("AC1", 0), ("RB4", 5), ("A", 0), ("AF2", 1),
+    ("C", 2), ("AG2", 3), ("Ef", 5), ("AC2", 0), ("RA2", 0), ("RF4", 3), ("AF3", 1), ("E", 4),
+    ("AC3", 0), ("RA3", 0), ("AG3", 3), ("RA4", 0), ("RG2", 2), ("Eg", 4), ("AC5", 1), ("Ff", 3),
+    ("AF4", 1), ("RG3", 2), ("Em", 4), ("RF2", 2), ("Cg", 2), ("RB2", 4), ("RG4", 2), ("AG4", 3),
+    ("AC4", 0), ("RB5", 5), ("RF5", 3), ("K", 0), ("RB3", 4),
+)
+
+
+class GainSum:
+    def __init__(self, place, pieces, got, send, recv):
+        self.place, self.pieces, self.got, self.send, self.recv = place, pieces, got, send, recv
+
+    def hop(self, k):
+        ways = ("core", "x", "y", "pair", "far")
+        sources = (self.pieces.at[1], self.pieces.at[0].at[1], self.pieces.at[0].at[0])
+        src = sources[min(k, 2)]
+        if k == 0:
+            dst = self.got.at[pl.ds(0, 2)]
+        else:
+            dst = self.got.at[k + 1]
+        return self.place.copy(src, dst, self.send.at[k], self.recv.at[k], ways[k])
+
+    def start(self):
+        self.hop(0).start()
+
+    def next(self, k):
+        self.hop(k).wait()
+        if k == 0:
+            self.pieces[0] = self.pieces[0] + self.got[0:2]
+        else:
+            self.pieces[0, 0] = self.pieces[0, 0] + self.got[k + 1]
+        if k < 4:
+            self.hop(k + 1).start()
+
+
 def layer_kernel(
-    x_ref, cot_ref, mask_ref, gains_ref, in_w, out_w, gu_w, dn_w,
-    out_hbm, ingrad_hbm, gu_hbm, dn_hbm, iw_hbm, ow_hbm, gain_ref, rows_hbm,
-    g_ffn, g_cot, g_att, p_attn, p_gin, p_ffn, p_back,
+    x_ref, cot_ref, mask_ref, gains_ref, masked_cot, in_w, out_w, gu_w, dn_w,
+    out_hbm, ingrad_hbm, gu_hbm, dn_hbm, iw_hbm, ow_hbm, gain_out, rows_hbm, cot_hbm,
+    g_ffn, g_att, cot_v, p_attn, p_gin, p_ffn, p_back,
     over_attn, over_gin, over_ffn, over_back, ups_attn, ups_gin, ups_ffn, ups_back,
     downs_attn, downs_gin, downs_ffn, downs_back,
     q_s, k_s, v_s, mixed_s, dk_s, dv_s, sc, dp,
     gu_v, dn_v, owa_v, owe_v, iw_v, xb,
-    act_s, gg_s, gup_s, gmixed_s, gproj_s, hmid_s, ghmid_s, stage,
+    act_s, gg_s, gup_s, gmixed_s, gproj_s, hmid_s, ghmid_s, stage, gain_s, gain_pieces, gain_got,
     gu_sent, gu_kept, gu_core, gu_x, dn_sent, dn_kept, dn_core, dn_x,
     iw_sent, iw_kept, iw_core, iw_x, ow_sent, ow_kept, ow_core, ow_x,
     sem_first, sem_first_got, sem_gather, sem_gather_got, sem_reduce, sem_reduce_got,
-    sem_grad_ffn, sem_grad_att, sem_local, credits, free,
+    sem_grad_ffn, sem_grad_att, sem_gain, sem_local, credits, free,
 ):
     place = Place()
     z, f = place.z, place.f
@@ -1022,58 +1075,82 @@
     quarter = depth // 4
     mask = mask_ref[...]
     scale = HDIM ** (-0.5)
+    pairs_of = positions // 2
+
+    def load(src, dst, number):
+        return pltpu.make_async_copy(src, dst, sem_local.at[number])
+
+    def load_owa(p):
+        return load(out_w.at[p], owa_v, 0)
+
+    def load_owe(p):
+        return load(out_w.at[p], owe_v, 1)
+
+    def load_iw(p, slot):
+        return load(in_w.at[p], iw_v.at[slot], 2 + slot)
+
+    def load_gu(p):
+        return load(gu_w.at[p], gu_v, 4)
+
+    def load_dn(p):
+        return load(dn_w.at[p], dn_v, 5)
+
+    def load_rows(p, dst, number):
+        return load(rows_hbm.at[p // 4, :, :, (p % 4) // 2, p % 2], dst, number)
+
+    def load_cot(p):
+        return load(cot_hbm.at[p // 2, :, :, p % 2], cot_v, 9)
+
+    def own_cot(j):
+        return load(masked_cot.at[j], cot_hbm.at[j, 0, 0], 16 + j)
+
+    for j in range(pairs_of):
+        own_cot(j).start()
 
     barrier = pltpu.get_barrier_semaphore()
 
     def greet(way):
         pl.semaphore_signal(barrier, inc=1, device_id=place.device(way), device_id_type=MESH)
 
-    for way in ("y", "core", "x"):
+    for way in ("y", "core", "x", "far"):
         greet(way)
     when(z < 3, lambda: greet("up"))
     when(z > 0, lambda: greet("down"))
-    pl.semaphore_wait(barrier, 3 + (z < 3).astype(jnp.int32) + (z > 0).astype(jnp.int32))
-
-    def load(src, dst, number):
-        return pltpu.make_async_copy(src, dst, sem_local.at[number])
-
-    def load_owa(p):
-        return load(out_w.at[p], owa_v, 0)
-
-    def load_owe(p):
-        return load(out_w.at[p], owe_v, 1)
-
-    def load_iw(p, slot):
-        return load(in_w.at[p], iw_v.at[slot], 2 + slot)
-
-    def load_gu(p):
-        return load(gu_w.at[p], gu_v, 4)
-
-    def load_dn(p):
-        return load(dn_w.at[p], dn_v, 5)
-
-    def load_rows(p, dst, number):
-        return load(rows_hbm.at[p // 4, :, :, (p % 4) // 2, p % 2], dst, number)
+    pl.semaphore_wait(barrier, 4 + (z < 3).astype(jnp.int32) + (z > 0).astype(jnp.int32))
 
     groups = positions // 4
+
+    def gain_of(which, p):
+        return gains_ref[which, pl.ds(p, 1), :]
 
     def normalise(p, c):
         residual = x_ref[p].astype(f32)
-        value = residual * inverse_rms(residual) * gains_ref[0, p]
+        value = residual * inverse_rms(residual) * gain_of(0, p)
         g_att[p // 8, (p % 8) // 2, p % 2] = value.astype(bf16)
         return c
 
     def own_rows(g):
         return load(g_att.at[g // 2, pl.ds((g % 2) * 2, 2)], rows_hbm.at[g, 0, 0], 10 + g)
 
+    def first_kind(g):
+        return GatherY if g == groups - 1 else GatherZ
+
     firsts = [
-        GatherZ(place, rows_hbm.at[g], sem_first.at[g], sem_first_got.at[g]) for g in range(groups)
+        first_kind(g)(place, rows_hbm.at[g], sem_first.at[g], sem_first_got.at[g]) for g in range(groups)
     ]
+
+    def cot_gather(j, which):
+        return COT_GATHER(place, cot_hbm.at[pairs_of - 1 - j], sem_gather.at[2, which], sem_gather_got.at[2, which])
+
+    first_cot = cot_gather(0, 0)
     for g in range(groups):
         lax.fori_loop(4 * g, 4 * g + 4, normalise, 0)
         own_rows(g).start()
         own_rows(g).wait()
         firsts[g].t1()
+    for j in range(pairs_of):
+        own_cot(j).wait()
+    first_cot.t1()
     load_owa(last).start()
     load_gu(last).start()
     load_dn(last).start()
@@ -1102,14 +1179,19 @@
 
     for g in range(groups):
         firsts[g].t2()
+    first_cot.t2()
     for g in range(groups):
         firsts[g].t3()
+    first_cot.t3()
     for g in range(groups):
         firsts[g].t4()
+    first_cot.t4()
     for g in range(groups):
         firsts[g].done()
         load_rows(4 * g, g_ffn.at[0], 6).start()
         lax.fori_loop(4 * g, 4 * g + 4, project, 0)
+    first_cot.done()
+    load_cot(last).start()
     load_owe(last).start()
     load_iw(last, 0).start()
     load_rows(last, xb, 8).start()
@@ -1206,89 +1288,74 @@
         place, (iw_sent, ow_sent), (iw_kept, ow_kept), (iw_core, ow_core), (iw_x, ow_x), sem_grad_att, free, 1
     )
     ffn_outs, att_outs = (gu_hbm, dn_hbm), (iw_hbm, ow_hbm)
-
-    def step(s, c):
-        now = lax.rem(s, 2)
-        then = 1 - now
-
-        def valid(delay):
-            return (s >= delay) & (s <= last + delay)
-
-        def pos(delay):
-            return last - (s - delay)
-
-        def ring(delay):
-            return lax.rem(s - delay + 8, 4)
-
-        gather_ffn = GatherZ(place, g_ffn.at[now], sem_gather.at[0], sem_gather_got.at[0, now])
-        gather_cot = GatherY(place, g_cot.at[now], sem_gather.at[1], sem_gather_got.at[1, now])
-        gather_att = GatherY(place, g_att.at[now], sem_gather.at[2], sem_gather_got.at[2, now])
-
-        def reducing(kind, part, over, ups, downs, number, which):
+    gain_sum = GainSum(place, gain_pieces, gain_got, sem_gain.at[0], sem_gain.at[1])
+
+    def out_copy(p):
+        return pltpu.make_async_copy(stage.at[0], out_hbm.at[p], sem_local.at[14])
+
+    def ingrad_copy(p):
+        return pltpu.make_async_copy(stage.at[1], ingrad_hbm.at[p], sem_local.at[15])
+
+    class Position:
+        def __init__(self, i):
+            self.i = i
+            self.p = last - i
+            self.par = lax.rem(i + 16, 2)
+            self.ring = lax.rem(i + 16, 4)
+
+        def gather(self, kind, g, number):
+            par = self.par
+            return kind(place, g.at[par], sem_gather.at[number, par], sem_gather_got.at[number, par])
+
+        def reduce(self, kind, part, over, ups, downs, number):
+            par = self.par
             return kind(
-                place, part, over.at[which], ups.at[which], downs.at[which],
-                sem_reduce.at[number], sem_reduce_got.at[number, which],
+                place, part, over.at[par], ups.at[par], downs.at[par],
+                sem_reduce.at[number, par], sem_reduce_got.at[number, par],
             )
 
-        attn_now = reducing(ReduceY, p_attn, over_attn, ups_attn, downs_attn, 0, now)
-        attn_then = reducing(ReduceY, p_attn, over_attn, ups_attn, downs_attn, 0, then)
-        gin_now = reducing(ReduceY, p_gin, over_gin, ups_gin, downs_gin, 1, now)
-        gin_then = reducing(ReduceY, p_gin, over_gin, ups_gin, downs_gin, 1, then)
-        ffn_now = reducing(ReduceZ, p_ffn.at[now], over_ffn, ups_ffn, downs_ffn, 2, now)
-        ffn_then = reducing(ReduceZ, p_ffn.at[then], over_ffn, ups_ffn, downs_ffn, 2, then)
-        back_now = reducing(ReduceY, p_back.at[now], over_back, ups_back, downs_back, 3, now)
-        back_then = reducing(ReduceY, p_back.at[then], over_back, ups_back, downs_back, 3, then)
-
-        @pl.when(s >= 1)
-        def _():
-            pl.semaphore_wait(credits.at[0], 1)
-            when(z > 0, lambda: pl.semaphore_wait(credits.at[1], 1))
-            when(z < 3, lambda: pl.semaphore_wait(credits.at[2], 1))
-
-        @pl.when(valid(1))
-        def _():
-            p = pos(1)
-            g_cot[now, 0, 0] = (mask * cot_ref[p].astype(f32)).astype(bf16)
-            gather_cot.t1()
-            attn_then.done()
-            hmid = x_ref[p].astype(f32) + mask * attn_then.total()
-            hmid_s[ring(1)] = hmid
-            g_ffn[now, 0, 0] = (hmid * inverse_rms(hmid) * gains_ref[1, p]).astype(bf16)
-            gather_ffn.t1()
-
-        @pl.when(valid(3))
-        def _():
-            p = pos(3)
-            gin_then.done()
-            hmid = hmid_s[ring(3)]
-            factor = inverse_rms(hmid)
-            grad = cot_ref[p].astype(f32) + norm_back(gin_then.total(), hmid * factor, factor, gains_ref[1, p])
-            ghmid_s[ring(3)] = grad
-            g_att[now, 0, 0] = (mask * grad).astype(bf16)
-            gather_att.t1()
-
-        @pl.when(valid(0))
-        def _():
-            p = pos(0)
+        def AF(self):
+            return self.gather(FFN_GATHER, g_ffn, 0)
+
+        def AG(self):
+            return self.gather(ATT_GATHER, g_att, 1)
+
+        def RA(self):
+            return self.reduce(ATTN_REDUCE, p_attn, over_attn, ups_attn, downs_attn, 0)
+
+        def RG(self):
+            return self.reduce(GIN_REDUCE, p_gin, over_gin, ups_gin, downs_gin, 1)
+
+        def RF(self):
+            return self.reduce(FFN_REDUCE, p_ffn.at[self.par], over_ffn, ups_ffn, downs_ffn, 2)
+
+        def RB(self):
+            return self.reduce(BACK_REDUCE, p_back.at[self.par], over_back, ups_back, downs_back, 3)
+
+        def do_A(self):
+            p = self.p
             attend_one(p)
             load_owa(p).wait()
             p_attn[...] = dot(mixed_s[p], owa_v[...], NN).astype(bf16).reshape(blocks)
-            attn_now.t1()
-            when(s < last, lambda: load_owa(p - 1).start())
-
-        when(valid(1), gather_cot.t2)
-        when(valid(1), gather_ffn.t2)
-        when(valid(3), gather_att.t2)
-        when(valid(3), ffn_then.t3)
-        when(valid(5), back_then.t2)
-
-        @pl.when(valid(2))
-        def _():
-            p = pos(2)
+            self.RA().t1()
+            when(p > 0, lambda: load_owa(p - 1).start())
+
+        def do_RA5(self):
+            p, total = self.p, self.RA()
+            total.done()
+            hmid = x_ref[p].astype(f32) + mask * total.total()
+            hmid_s[self.ring] = hmid
+            g_ffn[self.par, 0, 0] = (hmid * inverse_rms(hmid) * gain_of(1, p)).astype(bf16)
+            self.AF().t1()
+
+        def do_C(self):
+            p, par = self.p, self.par
+            self.AF().done()
             load_gu(p).wait()
             load_dn(p).wait()
-            x = g_ffn[then].reshape(rows, depth)
-            g = g_cot[then].reshape(rows, depth)
+            load_cot(p).wait()
+            x = g_ffn[par].reshape(rows, depth)
+            g = cot_v[...].reshape(rows, depth)
             for h in range(2):
                 at = slice(h * hidden // 2, (h + 1) * hidden // 2)
                 gate = dot(x, gu_v[0, :, at], NN)
@@ -1301,130 +1368,190 @@
                 gup_s[:, at] = (grad_act * silu).astype(bf16)
             back = dot(gg_s[...], gu_v[0], NT) + dot(gup_s[...], gu_v[1], NT)
             p_gin[...] = back.astype(bf16).reshape(blocks)
-            gin_now.t1()
-            gain_ref[1, p] = jnp.sum(back * x.astype(f32), axis=0, keepdims=True)
-            p_ffn[now] = dot(act_s[...], dn_v[...], NN).astype(bf16).reshape(blocks)
-            ffn_now.t1()
-
-            @pl.when(s < last + 2)
+            self.RG().t1()
+            gain_s[1, pl.ds(p, 1), :] = jnp.sum(back * x.astype(f32), axis=0, keepdims=True)
+            p_ffn[par] = dot(act_s[...], dn_v[...], NN).astype(bf16).reshape(blocks)
+            self.RF().t1()
+
+            @pl.when(p > 0)
             def _():
                 load_gu(p - 1).start()
                 load_dn(p - 1).start()
 
-        when(valid(1), gather_cot.t3)
-        when(valid(1), gather_ffn.t3)
-        when(valid(3), gather_att.t3)
-        when(valid(0), attn_now.t2)
-        when(valid(3), ffn_then.t4)
-        when(valid(5), back_then.t3)
-        when(valid(3), lambda: grad_ffn.finish(ffn_outs, pos(3), s < last + 3))
-
-        @pl.when(valid(4))
-        def _():
-            p = pos(4)
+        def do_Cg(self):
+            p, par = self.p, self.par
+
+            @pl.when(p < last)
+            def _():
+                grad_ffn.drained(ffn_outs, p + 1)
+
+            for r in range(4):
+                at = piece_at(r, f, quarter)
+                gu_to, dn_to = (gu_kept, dn_kept) if r % 2 == 0 else (gu_sent, dn_sent)
+                columns = g_ffn[par, :, :, :, at].reshape(rows, quarter)
+                gu_to[r // 2, 0] = dot(columns, gg_s[...], TN).astype(bf16)
+                gu_to[r // 2, 1] = dot(columns, gup_s[...], TN).astype(bf16)
+                dn_to[r // 2] = dot(act_s[...], cot_v[:, :, :, at].reshape(rows, quarter), TN).astype(bf16)
+            grad_ffn.start(p < last)
+            when(p > 0, lambda: load_cot(p - 1).start())
+
+        def do_Fm(self):
+            grad_ffn.middle(self.p < last)
+
+        def do_Ff(self):
+            grad_ffn.finish(ffn_outs, self.p, self.p > 0)
+
+        def do_RG5(self):
+            p, total = self.p, self.RG()
+            total.done()
+            hmid = hmid_s[self.ring]
+            factor = inverse_rms(hmid)
+            grad = cot_ref[p].astype(f32) + norm_back(total.total(), hmid * factor, factor, gain_of(1, p))
+            ghmid_s[self.ring] = grad
+            g_att[self.par, 0, 0] = (mask * grad).astype(bf16)
+            self.AG().t1()
+
+        def do_RF5(self):
+            p, total = self.p, self.RF()
+            total.done()
+
+            @pl.when(p < last)
+            def _():
+                out_copy(p + 1).wait()
+
+            stage[0] = (hmid_s[self.ring] + mask * total.total()).astype(bf16)
+            out_copy(p).start()
+
+        def do_E(self):
+            p, par = self.p, self.par
+            self.AG().done()
             load_owe(p).wait()
             load_iw(p, 0).wait()
             load_rows(p, xb, 8).wait()
-            gmixed_s[...] = dot(g_att[then].reshape(rows, depth), owe_v[...], NT).astype(bf16)
+            gmixed_s[...] = dot(g_att[par].reshape(rows, depth), owe_v[...], NT).astype(bf16)
             attend_back_one(p)
             back = dot(gproj_s[0], iw_v[0, 0], NT)
             back = back + dot(gproj_s[1], iw_v[0, 1], NT)
             back = back + dot(gproj_s[2], iw_v[0, 2], NT)
-            p_back[now] = back.astype(bf16).reshape(blocks)
-            back_now.t1()
-            gain_ref[0, p] = jnp.sum(back * xb[...].reshape(rows, depth).astype(f32), axis=0, keepdims=True)
-
-        when(valid(1), gather_cot.t4)
-        when(valid(1), gather_ffn.t4)
-        when(valid(3), gather_att.t4)
-        when(valid(0), attn_now.t3)
-        when(valid(2), gin_now.t2)
-        when(valid(2), ffn_now.t2)
-        when(valid(5), back_then.t4)
-
-        def out_copy(p):
-            return pltpu.make_async_copy(stage.at[0], out_hbm.at[p], sem_local.at[14])
-
-        def ingrad_copy(p):
-            return pltpu.make_async_copy(stage.at[1], ingrad_hbm.at[p], sem_local.at[15])
-
-        @pl.when(valid(3))
-        def _():
-            ffn_then.done()
-            stage[0] = (hmid_s[ring(3)] + mask * ffn_then.total()).astype(bf16)
-            out_copy(pos(3)).start()
-
-        @pl.when(valid(3))
-        def _():
-            grad_ffn.drained(ffn_outs, pos(3))
-
-        @pl.when(valid(2))
-        def _():
-            for r in range(4):
-                at = piece_at(r, f, quarter)
-                gu_to, dn_to = (gu_kept, dn_kept) if r % 2 == 0 else (gu_sent, dn_sent)
-                columns = g_ffn[then, :, :, :, at].reshape(rows, quarter)
-                gu_to[r // 2, 0] = dot(columns, gg_s[...], TN).astype(bf16)
-                gu_to[r // 2, 1] = dot(columns, gup_s[...], TN).astype(bf16)
-                dn_to[r // 2] = dot(act_s[...], g_cot[then, :, :, :, at].reshape(rows, quarter), TN).astype(bf16)
-            grad_ffn.start(s > 2)
-
-        when(valid(0), attn_now.t4)
-        when(valid(2), gin_now.t3)
-
-        @pl.when(valid(5))
-        def _():
-            p = pos(5)
-            back_then.done()
-            residual = x_ref[p].astype(f32)
-            factor = inverse_rms(residual)
-            grad = norm_back(back_then.total(), residual * factor, factor, gains_ref[0, p])
-            stage[1] = (ghmid_s[ring(5)] + grad).astype(bf16)
-            ingrad_copy(p).start()
-            grad_att.finish(att_outs, p, s < last + 5)
-            grad_att.drained(att_outs, p)
-
-        @pl.when(valid(4))
-        def _():
-            p = pos(4)
+            p_back[par] = back.astype(bf16).reshape(blocks)
+            self.RB().t1()
+            gain_s[0, pl.ds(p, 1), :] = jnp.sum(back * xb[...].reshape(rows, depth).astype(f32), axis=0, keepdims=True)
+
+            @pl.when(p == 0)
+            def _():
+                for r in range(4):
+                    gain_pieces[r % 2, r // 2] = gain_s[:, :, piece_at(r, f, quarter)]
+                gain_sum.start()
+
+            @pl.when(p > 0)
+            def _():
+                load_owe(p - 1).start()
+                load_iw(p - 1, 0).start()
+
+        def do_Eg(self):
+            p, par = self.p, self.par
+
+            @pl.when(p < last)
+            def _():
+                grad_att.drained(att_outs, p + 1)
+
             for r in range(4):
                 at = piece_at(r, f, quarter)
                 iw_to, ow_to = (iw_kept, ow_kept) if r % 2 == 0 else (iw_sent, ow_sent)
                 columns = xb[:, :, :, at].reshape(rows, quarter)
                 for j in range(3):
                     iw_to[r // 2, j] = dot(columns, gproj_s[j], TN).astype(bf16)
-                ow_to[r // 2] = dot(mixed_s[p], g_att[then, :, :, :, at].reshape(rows, quarter), TN).astype(bf16)
-            grad_att.start(s > 4)
-
-            @pl.when(s < last + 4)
+                ow_to[r // 2] = dot(mixed_s[p], g_att[par, :, :, :, at].reshape(rows, quarter), TN).astype(bf16)
+            grad_att.start(p < last)
+            when(p > 0, lambda: load_rows(p - 1, xb, 8).start())
+
+        def do_Em(self):
+            grad_att.middle(self.p < last)
+
+        def do_Ef(self):
+            grad_att.finish(att_outs, self.p, self.p > 0)
+
+        def do_RB5(self):
+            p, total = self.p, self.RB()
+            total.done()
+            when(p == 0, lambda: gain_sum.next(3))
+
+            @pl.when(p < last)
             def _():
-                load_owe(p - 1).start()
-                load_iw(p - 1, 0).start()
-                load_rows(p - 1, xb, 8).start()
-
-        @pl.when(s < last + 5)
-        def _():
-            def tell(number, way):
-                pl.semaphore_signal(credits.at[number], inc=1, device_id=place.device(way), device_id_type=MESH)
-
-            tell(0, "y")
-            when(z < 3, lambda: tell(1, "up"))
-            when(z > 0, lambda: tell(2, "down"))
-
-        when(valid(2), lambda: grad_ffn.middle(s > 2))
-        when(valid(2), gin_now.t4)
-        when(valid(1), gather_cot.done)
-        when(valid(1), gather_ffn.done)
-        when(valid(3), gather_att.done)
-        when(valid(4), lambda: grad_att.middle(s > 4))
-        when(valid(3), lambda: out_copy(pos(3)).wait())
-        when(valid(5), lambda: ingrad_copy(pos(5)).wait())
+                ingrad_copy(p + 1).wait()
+
+            residual = x_ref[p].astype(f32)
+            factor = inverse_rms(residual)
+            grad = norm_back(total.total(), residual * factor, factor, gain_of(0, p))
+            stage[1] = (ghmid_s[self.ring] + grad).astype(bf16)
+            ingrad_copy(p).start()
+
+        def do_RB2(self):
+            self.RB().t2()
+            when(self.p == 0, lambda: gain_sum.next(0))
+
+        def do_RB3(self):
+            self.RB().t3()
+            when(self.p == 0, lambda: gain_sum.next(1))
+
+        def do_RB4(self):
+            self.RB().t4()
+            when(self.p == 0, lambda: gain_sum.next(2))
+
+        def runs(self):
+            ticks = {}
+            for name, event in (
+                ("RA", self.RA), ("RG", self.RG), ("RF", self.RF), ("AF", self.AF), ("AG", self.AG),
+            ):
+                ticks[name + "2"] = lambda event=event: event().t2()
+                ticks[name + "3"] = lambda event=event: event().t3()
+                ticks[name + "4"] = lambda event=event: event().t4()
+            return ticks | {
+                "A": self.do_A, "RA5": self.do_RA5, "C": self.do_C, "Cg": self.do_Cg, "Fm": self.do_Fm,
+                "Ff": self.do_Ff, "RG5": self.do_RG5, "RF5": self.do_RF5, "E": self.do_E, "Eg": self.do_Eg,
+                "Em": self.do_Em, "Ef": self.do_Ef, "RB2": self.do_RB2, "RB3": self.do_RB3, "RB4": self.do_RB4,
+                "RB5": self.do_RB5,
+            }
+
+    def cot_runs(j):
+        event = cot_gather(j, lax.rem(j + 16, 2))
+        return {"AC1": event.t1, "AC2": event.t2, "AC3": event.t3, "AC4": event.t4, "AC5": event.done}
+
+    def tell(number, way):
+        pl.semaphore_signal(credits.at[number], inc=1, device_id=place.device(way), device_id_type=MESH)
+
+    def tell_all():
+        tell(0, "y")
+        when(z < 3, lambda: tell(1, "up"))
+        when(z > 0, lambda: tell(2, "down"))
+
+    steps = positions + max(delay for name, delay in SCHEDULE if name[:2] != "AC")
+    tell_all()
+
+    def step(s, c):
+        pl.semaphore_wait(credits.at[0], 1)
+        when(z > 0, lambda: pl.semaphore_wait(credits.at[1], 1))
+        when(z < 3, lambda: pl.semaphore_wait(credits.at[2], 1))
+        for name, delay in SCHEDULE:
+            if name == "K":
+                when(s < steps - 1, tell_all)
+            elif name[:2] == "AC":
+                j = s + 1 - delay
+                when((j >= 1) & (j < pairs_of), cot_runs(j)[name])
+            else:
+                when((s >= delay) & (s <= last + delay), Position(s - delay).runs()[name])
         return c
 
-    lax.fori_loop(0, positions + 5, step, 0)
-
-
-def layer(x, cot, mask, gains, in_weight, out_weight, gate_up, down):
+    lax.fori_loop(0, steps, step, 0)
+    gain_sum.next(4)
+    gain_out[...] = gain_pieces[0, 0] / gains_ref[:, :, piece_at(0, f, quarter)]
+    grad_ffn.drained(ffn_outs, 0)
+    grad_att.drained(att_outs, 0)
+    out_copy(0).wait()
+    ingrad_copy(0).wait()
+
+
+def layer(x, cot, mask, gains, masked_cot, in_weight, out_weight, gate_up, down):
     positions, local, depth = x.shape
     width, hidden = out_weight.shape[1], down.shape[1]
     rows = ZN * YN * local
@@ -1440,11 +1567,10 @@
 
     everything = (ZN, YN) + block
     scratch = (
-        [vm(2, *everything)] * 3
-        + [vm(*everything)] * 2
+        [vm(2, *everything)] * 2
+        + [vm(*everything)] * 3
         + [vm(2, *everything)] * 2
-        + [vm(2, ZN, *block)] * 2
-        + [vm(2, *block), vm(2, ZN, *block)]
+        + [vm(2, ZN, *block), vm(2, ZN, *block), vm(2, *block), vm(2, ZN, *block)]
         + [vm(2, 3, *block), vm(2, 3, *block), vm(2, 3, YN, *block), vm(2, 3, *block)] * 2
         + [vm(positions, rows, width)] * 4
         + [vm(positions, rows, width, dtype=f32)] * 2
@@ -1455,6 +1581,8 @@
         + [vm(rows, width), vm(3, rows, width)]
         + [vm(4, *block, dtype=f32)] * 2
         + [vm(2, *block)]
+        + [vm(2, positions, depth, dtype=f32)]
+        + [vm(2, 2, 2, positions, quarter, dtype=f32), vm(6, 2, positions, quarter, dtype=f32)]
         + [vm(2, 2, quarter, hidden)] * 3
         + [vm(2, quarter, hidden)]
         + [vm(2, hidden, quarter)] * 3
@@ -1466,13 +1594,14 @@
         + [
             pltpu.SemaphoreType.DMA((groups, 10)),
             pltpu.SemaphoreType.DMA((groups, 8)),
-            pltpu.SemaphoreType.DMA((3, 10)),
+            pltpu.SemaphoreType.DMA((3, 2, 10)),
             pltpu.SemaphoreType.DMA((3, 2, 8)),
-            pltpu.SemaphoreType.DMA((4, 7)),
-            pltpu.SemaphoreType.DMA((4, 2, 7)),
+            pltpu.SemaphoreType.DMA((4, 2, 10)),
+            pltpu.SemaphoreType.DMA((4, 2, 11)),
             pltpu.SemaphoreType.DMA((5, 2)),
             pltpu.SemaphoreType.DMA((5, 2)),
-            pltpu.SemaphoreType.DMA((16,)),
+            pltpu.SemaphoreType.DMA((2, 5)),
+            pltpu.SemaphoreType.DMA((16 + positions // 2,)),
             pltpu.SemaphoreType.REGULAR((3,)),
             pltpu.SemaphoreType.REGULAR((4,)),
         ]
@@ -1481,8 +1610,8 @@
     anywhere = pl.BlockSpec(memory_space=pl.ANY)
     return pl.pallas_call(
         layer_kernel,
-        in_specs=[in_vmem] * 4 + [anywhere] * 4,
-        out_specs=[anywhere] * 6 + [in_vmem, anywhere],
+        in_specs=[in_vmem] * 4 + [anywhere] * 5,
+        out_specs=[anywhere] * 6 + [in_vmem, anywhere, anywhere],
         out_shape=[
             hbm(positions, *block),
             hbm(positions, *block),
@@ -1490,38 +1619,34 @@
             hbm(positions, hidden, quarter),
             hbm(positions, 3, quarter, width),
             hbm(positions, width, quarter),
-            hbm(2, positions, 1, depth, dtype=f32),
+            hbm(2, positions, quarter, dtype=f32),
             hbm(groups, ZN, YN, 2, 2, *block),
+            hbm(positions // 2, ZN, YN, 2, *block),
         ],
         scratch_shapes=scratch,
         compiler_params=pltpu.CompilerParams(
             collective_id=0, has_side_effects=True, vmem_limit_bytes=KERNEL_VMEM_BYTES
         ),
         name="layer",
-    )(x, cot, mask, gains, in_weight, out_weight, gate_up, down)
+    )(x, cot, mask, gains, masked_cot, in_weight, out_weight, gate_up, down)
 
 
 def body_in_one(inputs, counts, norm_gains, in_weight, out_weight, gate_up, down_weight, cotangent):
-    group_size = lax.axis_size("mp")
-    local = inputs.shape[0]
+    local, positions, depth = inputs.shape
     ids = lax.axis_index("mp") * local + jnp.arange(local)
-    mask = (ids < counts[0]).astype(f32)[:, None]
-    output, input_grad, g_gu, g_dn, g_in, g_out, gain_sums, _ = layer(
+    valid = ids < counts[0]
+    masked = jnp.where(valid[:, None, None], cotangent, jnp.zeros_like(cotangent))
+    output, input_grad, g_gu, g_dn, g_in, g_out, gain_sums, _, _ = layer(
         jnp.swapaxes(inputs, 0, 1),
         jnp.swapaxes(cotangent, 0, 1),
-        mask,
-        norm_gains[:, :, None, :],
+        valid.astype(f32)[:, None],
+        norm_gains,
+        jnp.swapaxes(masked, 0, 1).reshape(positions // 2, 2, local, depth),
         in_weight,
         out_weight,
         gate_up,
         down_weight,
     )
-    terms = gain_sums[:, :, 0] / norm_gains
-    terms = lax.psum_scatter(terms, "frames", scatter_dimension=2, tiled=True)
-    step = 1
-    while step < group_size:
-        terms = terms + lax.ppermute(terms, "mp", [(i, i ^ step) for i in range(group_size)])
-        step *= 2
     return (
         jnp.swapaxes(output, 0, 1),
         jnp.swapaxes(input_grad, 0, 1),
@@ -1529,7 +1654,7 @@
         g_out.astype(f32),
         g_gu.astype(f32),
         g_dn.astype(f32),
-        terms,
+        gain_sums,
     )
 
 

time: 1100 us -> 969 us (0.88)
  Pallas kernels: 1020 us -> 931 us
  waiting for transfers between devices: 23.9 us -> 0 us
  between operations: 14.7 us -> 1.34 us
    pallas_call x1, Pallas kernels: 1020 us -> 931 us  [layer(): pl.pallas_call(layer_kernel, in_specs=[in_vmem] * 4 + [anywhere] * 5, out...]
    reduce_scatter x1 -> x0, waiting for transfers between devices: 18.8 us -> none  [body_in_one(): terms = lax.psum_scatter(terms, 'frames', scatter_dimension=2, tiled=True)]
  transfers between devices with their start and end apart: 4 -> 0, of which waited for: 3 -> 0; matrix products, arithmetic and copies ran while one was open for 2% -> 0% of each run, Pallas kernels for 0% -> 0%
where the time goes in v3:
time: 969 us; the launch traced here: 968 us
  Pallas kernels  931 us (96%)
  other arithmetic  23.4 us (2%)
  local copies, waits for them, and re-layouts  12.7 us (1%)
    pallas_call x1, Pallas kernels, layer(): pl.pallas_call(layer_kernel, in_specs=[in_vmem] * 4 + [anywhere] * 5, out...  931 us

profile of v3, /device:TPU:0, one launch (start us, length us, event | category | flops | bytes accessed | tf_op | source)
XLA Modules:
  0.0 968.0 jit_solution(13629404168392622458)
XLA Ops:
  1.3 0.6 fusion.mask_ref
  1.9 1.6 select_bitcast_fusion
  3.5 0.0 copy-start
  3.5 0.0 copy-start.4
  3.5 2.0 copy.23
  5.5 0.0 copy-done
  5.5 0.0 copy-done.4
  5.5 3.4 copy_bitcast_fusion
  8.9 930.6 %layer.1 = (bf16[16,48,1024]{2,1,0:T(8,128)(2,1)}, bf16[16,48,1024]{2,1,0:T(8,128)(2,1)}, bf16[16,2,256,512]{3,2,1,0:T(8,128)(2,1)}, bf16[16,512,256]{2,1,0:T(8,...) custom-call(bf16[16,48,1024]{2,1,0:T(8,128)(2,1)} %get-tuple-element, ...), custom_call_target="tpu_custom_call" | custom-call | tf_op jit(solution)/shard_map/layer/pallas_call | solution.py:1611
  939.6 0.0 copy-start.3
  939.6 3.5 copy.24
  943.1 0.0 copy-done.3
  943.1 0.0 copy-start.5
  943.1 2.0 copy.25
  945.1 0.0 copy-done.5
  945.1 0.0 copy-start.2
  945.1 1.5 convert_element_type.24
  946.7 1.1 copy-done.2
  947.8 0.0 copy-start.1
  947.8 3.5 convert_element_type.23
  951.2 0.0 copy-done.1
  951.2 4.3 convert_element_type.26
  955.5 0.0 copy-start.6
  955.6 11.8 %convert_element_type.25 = f32[16,2,256,512]{3,2,1,0:T(8,128)} convert(bf16[16,2,256,512]{3,2,1,0:T(8,128)(2,1)} %get-tuple-element.18) | non-fusion elementwise | flops 4194304 | bytes 25165824 | tf_op jit(solution)/shard_map/convert_element_type | solution.py:1655
  967.4 0.0 copy-done.6
  967.4 0.6 copy.30
  (1 shorter events, 0.0 us)
Async XLA Ops:
  3.5 2.0 copy-start
  3.5 2.0 copy-start.4
  939.6 3.5 copy-start.3
  943.1 2.0 copy-start.5
  945.1 2.6 copy-start.2
  947.8 3.5 copy-start.1
  955.5 11.8 %copy-start.6 = (f32[2,16,256]{2,1,0:T(8,128)S(1)}, f32[2,16,256]{2,1,0:T(8,128)}, u32[]{:S(2)}) copy-start(f32[2,16,256]{2,1,0:T(8,128)} %get-tuple-element.50) | copy-start | bytes 98308

commit v4 on v3

--- a/solution.py
+++ b/solution.py
@@ -1007,20 +1007,87 @@
 
 
 COT_GATHER = GatherZ
-FFN_GATHER = GatherY
-ATT_GATHER = GatherY
 ATTN_REDUCE = ReduceY
 GIN_REDUCE = ReduceY
-FFN_REDUCE = ReduceZ
 BACK_REDUCE = ReduceY
+Z_FIRST = (0, 1, 2, 3, 4, 5, 6)
+FFN_Y_FIRST = (0, 1, 2, 3, 4, 5, 6, 7, 8, 9, 10, 11, 12, 13, 14, 15)
+ATT_Y_FIRST = (0, 1, 2, 3, 4, 5, 6, 7, 8, 9, 10, 11, 12, 13, 14, 15)
 
 SCHEDULE = (
-    ("Fm", 3), ("RF3", 3), ("RA5", 1), ("RG5", 3), ("AC1", 0), ("RB4", 5), ("A", 0), ("AF2", 1),
-    ("C", 2), ("AG2", 3), ("Ef", 5), ("AC2", 0), ("RA2", 0), ("RF4", 3), ("AF3", 1), ("E", 4),
-    ("AC3", 0), ("RA3", 0), ("AG3", 3), ("RA4", 0), ("RG2", 2), ("Eg", 4), ("AC5", 1), ("Ff", 3),
-    ("AF4", 1), ("RG3", 2), ("Em", 4), ("RF2", 2), ("Cg", 2), ("RB2", 4), ("RG4", 2), ("AG4", 3),
-    ("AC4", 0), ("RB5", 5), ("RF5", 3), ("K", 0), ("RB3", 4),
+    ("RA5", 1), ("RG5", 3), ("RB3", 5), ("AC1", 0), ("A", 0), ("RF3", 3), ("Ef", 5), ("AF2", 1),
+    ("C", 2), ("RF4", 3), ("RB4", 5), ("RA2", 0), ("AC2", 0), ("AG2", 3), ("E", 4), ("AF3", 1),
+    ("Eg", 4), ("RA3", 0), ("AC5", 1), ("AC3", 0), ("Ff", 3), ("RG2", 2), ("AG3", 3), ("Cg", 2),
+    ("RG3", 2), ("RA4", 0), ("RB5", 5), ("Em", 4), ("AC4", 0), ("RF5", 3), ("K", 0), ("RG4", 2),
+    ("RB2", 4), ("AF4", 1), ("AG4", 3), ("Fm", 2), ("RF2", 2),
 )
+
+
+class EitherGather:
+    def __init__(self, place, g, send, recv):
+        self.along_y = GatherY(place, g, send, recv)
+        self.along_z = GatherZ(place, g, send, recv)
+
+    def choose(self, i, y_first):
+        self.y_first = i < 0
+        for k in y_first:
+            self.y_first = self.y_first | (i == k)
+        return self
+
+    def both(self, along_y, along_z):
+        when(self.y_first, along_y)
+        when(jnp.logical_not(self.y_first), along_z)
+
+    def t1(self):
+        self.both(self.along_y.t1, self.along_z.t1)
+
+    def t2(self):
+        self.both(self.along_y.t2, self.along_z.t2)
+
+    def t3(self):
+        self.both(self.along_y.t3, self.along_z.t3)
+
+    def t4(self):
+        self.both(self.along_y.t4, self.along_z.t4)
+
+    def done(self):
+        self.both(self.along_y.done, self.along_z.done)
+
+
+class EitherReduce:
+    def __init__(self, place, part, over, ups, downs, send, recv):
+        self.along_z = ReduceZ(place, part, over.at[0], ups, downs, send, recv)
+        self.along_y = ReduceY(place, part, over, ups.at[:, 0], downs.at[:, 0], send, recv)
+
+    def choose(self, i):
+        self.z_first = i < 0
+        for k in Z_FIRST:
+            self.z_first = self.z_first | (i == k)
+        return self
+
+    def both(self, along_z, along_y):
+        when(self.z_first, along_z)
+        when(jnp.logical_not(self.z_first), along_y)
+
+    def t1(self):
+        self.both(self.along_z.t1, self.along_y.t1)
+
+    def t2(self):
+        self.both(self.along_z.t2, self.along_y.t2)
+
+    def t3(self):
+        self.both(self.along_z.t3, self.along_y.t3)
+
+    def t4(self):
+        self.both(self.along_z.t4, self.along_y.t4)
+
+    def done(self):
+        self.both(self.along_z.done, self.along_y.done)
+
+    def total(self):
+        z = self.along_z.place.z
+        value = self.along_y.local(0)
+        return value + up_to_f32(z >= 1, self.along_y.ups.at[2]) + up_to_f32(z <= 2, self.along_y.downs.at[2])
 
 
 class GainSum:
@@ -1096,13 +1163,16 @@
         return load(dn_w.at[p], dn_v, 5)
 
     def load_rows(p, dst, number):
-        return load(rows_hbm.at[p // 4, :, :, (p % 4) // 2, p % 2], dst, number)
+        return load(rows_hbm.at[p // 2, :, :, p % 2], dst, number)
 
     def load_cot(p):
         return load(cot_hbm.at[p // 2, :, :, p % 2], cot_v, 9)
 
     def own_cot(j):
         return load(masked_cot.at[j], cot_hbm.at[j, 0, 0], 16 + j)
+
+    def own_rows(j):
+        return load(g_att.at[j // 4, j % 4], rows_hbm.at[j, 0, 0], 16 + pairs_of + j)
 
     for j in range(pairs_of):
         own_cot(j).start()
@@ -1118,7 +1188,7 @@
     when(z > 0, lambda: greet("down"))
     pl.semaphore_wait(barrier, 4 + (z < 3).astype(jnp.int32) + (z > 0).astype(jnp.int32))
 
-    groups = positions // 4
+    groups = pairs_of
 
     def gain_of(which, p):
         return gains_ref[which, pl.ds(p, 1), :]
@@ -1129,9 +1199,6 @@
         g_att[p // 8, (p % 8) // 2, p % 2] = value.astype(bf16)
         return c
 
-    def own_rows(g):
-        return load(g_att.at[g // 2, pl.ds((g % 2) * 2, 2)], rows_hbm.at[g, 0, 0], 10 + g)
-
     def first_kind(g):
         return GatherY if g == groups - 1 else GatherZ
 
@@ -1142,15 +1209,13 @@
     def cot_gather(j, which):
         return COT_GATHER(place, cot_hbm.at[pairs_of - 1 - j], sem_gather.at[2, which], sem_gather_got.at[2, which])
 
-    first_cot = cot_gather(0, 0)
     for g in range(groups):
-        lax.fori_loop(4 * g, 4 * g + 4, normalise, 0)
+        lax.fori_loop(2 * g, 2 * g + 2, normalise, 0)
         own_rows(g).start()
         own_rows(g).wait()
         firsts[g].t1()
     for j in range(pairs_of):
         own_cot(j).wait()
-    first_cot.t1()
     load_owa(last).start()
     load_gu(last).start()
     load_dn(last).start()
@@ -1163,10 +1228,6 @@
         load_rows(p, g_ffn.at[slot], 6 + slot).wait()
         load_iw(p, slot).wait()
 
-        @pl.when(lax.rem(p, 4) < 3)
-        def _():
-            load_rows(p + 1, g_ffn.at[1 - slot], 7 - slot).start()
-
         @pl.when(p < last)
         def _():
             load_iw(p + 1, 1 - slot).start()
@@ -1179,19 +1240,15 @@
 
     for g in range(groups):
         firsts[g].t2()
-    first_cot.t2()
     for g in range(groups):
         firsts[g].t3()
-    first_cot.t3()
     for g in range(groups):
         firsts[g].t4()
-    first_cot.t4()
     for g in range(groups):
         firsts[g].done()
-        load_rows(4 * g, g_ffn.at[0], 6).start()
-        lax.fori_loop(4 * g, 4 * g + 4, project, 0)
-    first_cot.done()
-    load_cot(last).start()
+        load_rows(2 * g, g_ffn.at[0], 6).start()
+        load_rows(2 * g + 1, g_ffn.at[1], 7).start()
+        lax.fori_loop(2 * g, 2 * g + 2, project, 0)
     load_owe(last).start()
     load_iw(last, 0).start()
     load_rows(last, xb, 8).start()
@@ -1315,10 +1372,10 @@
             )
 
         def AF(self):
-            return self.gather(FFN_GATHER, g_ffn, 0)
+            return self.gather(EitherGather, g_ffn, 0).choose(self.i, FFN_Y_FIRST)
 
         def AG(self):
-            return self.gather(ATT_GATHER, g_att, 1)
+            return self.gather(EitherGather, g_att, 1).choose(self.i, ATT_Y_FIRST)
 
         def RA(self):
             return self.reduce(ATTN_REDUCE, p_attn, over_attn, ups_attn, downs_attn, 0)
@@ -1327,7 +1384,7 @@
             return self.reduce(GIN_REDUCE, p_gin, over_gin, ups_gin, downs_gin, 1)
 
         def RF(self):
-            return self.reduce(FFN_REDUCE, p_ffn.at[self.par], over_ffn, ups_ffn, downs_ffn, 2)
+            return self.reduce(EitherReduce, p_ffn.at[self.par], over_ffn, ups_ffn, downs_ffn, 2).choose(self.i)
 
         def RB(self):
             return self.reduce(BACK_REDUCE, p_back.at[self.par], over_back, ups_back, downs_back, 3)
@@ -1515,7 +1572,12 @@
 
     def cot_runs(j):
         event = cot_gather(j, lax.rem(j + 16, 2))
-        return {"AC1": event.t1, "AC2": event.t2, "AC3": event.t3, "AC4": event.t4, "AC5": event.done}
+
+        def done():
+            event.done()
+            when(j == 0, lambda: load_cot(last).start())
+
+        return {"AC1": event.t1, "AC2": event.t2, "AC3": event.t3, "AC4": event.t4, "AC5": done}
 
     def tell(number, way):
         pl.semaphore_signal(credits.at[number], inc=1, device_id=place.device(way), device_id_type=MESH)
@@ -1536,8 +1598,8 @@
             if name == "K":
                 when(s < steps - 1, tell_all)
             elif name[:2] == "AC":
-                j = s + 1 - delay
-                when((j >= 1) & (j < pairs_of), cot_runs(j)[name])
+                j = s - delay
+                when((j >= 0) & (j < pairs_of), cot_runs(j)[name])
             else:
                 when((s >= delay) & (s <= last + delay), Position(s - delay).runs()[name])
         return c
@@ -1557,7 +1619,7 @@
     rows = ZN * YN * local
     quarter = depth // 4
     block = (local, depth)
-    groups = positions // 4
+    groups = positions // 2
 
     def vm(*shape, dtype=bf16):
         return pltpu.VMEM(shape, dtype)
@@ -1570,7 +1632,7 @@
         [vm(2, *everything)] * 2
         + [vm(*everything)] * 3
         + [vm(2, *everything)] * 2
-        + [vm(2, ZN, *block), vm(2, ZN, *block), vm(2, *block), vm(2, ZN, *block)]
+        + [vm(2, ZN, *block), vm(2, ZN, *block), vm(2, ZN, *block), vm(2, ZN, *block)]
         + [vm(2, 3, *block), vm(2, 3, *block), vm(2, 3, YN, *block), vm(2, 3, *block)] * 2
         + [vm(positions, rows, width)] * 4
         + [vm(positions, rows, width, dtype=f32)] * 2
@@ -1601,7 +1663,7 @@
             pltpu.SemaphoreType.DMA((5, 2)),
             pltpu.SemaphoreType.DMA((5, 2)),
             pltpu.SemaphoreType.DMA((2, 5)),
-            pltpu.SemaphoreType.DMA((16 + positions // 2,)),
+            pltpu.SemaphoreType.DMA((16 + positions,)),
             pltpu.SemaphoreType.REGULAR((3,)),
             pltpu.SemaphoreType.REGULAR((4,)),
         ]
@@ -1620,7 +1682,7 @@
             hbm(positions, 3, quarter, width),
             hbm(positions, width, quarter),
             hbm(2, positions, quarter, dtype=f32),
-            hbm(groups, ZN, YN, 2, 2, *block),
+            hbm(positions // 2, ZN, YN, 2, *block),
             hbm(positions // 2, ZN, YN, 2, *block),
         ],
         scratch_shapes=scratch,

time: 969 us -> 935 us (0.965)
  Pallas kernels: 931 us -> 897 us
    pallas_call x1, Pallas kernels: 931 us -> 897 us  [layer(): pl.pallas_call(layer_kernel, in_specs=[in_vmem] * 4 + [anywhere] * 5, out...]
where the time goes in v4:
time: 935 us; the launch traced here: 934 us
  Pallas kernels  897 us (96%)
  other arithmetic  23.4 us (3%)
  local copies, waits for them, and re-layouts  12.7 us (1%)
    pallas_call x1, Pallas kernels, layer(): pl.pallas_call(layer_kernel, in_specs=[in_vmem] * 4 + [anywhere] * 5, out...  897 us

profile of v4, /device:TPU:0, one launch (start us, length us, event | category | flops | bytes accessed | tf_op | source)
XLA Modules:
  0.0 934.3 jit_solution(1218194688602840634)
XLA Ops:
  1.3 0.6 fusion.mask_ref
  1.9 1.6 select_bitcast_fusion
  3.5 0.0 copy-start
  3.5 0.0 copy-start.4
  3.5 2.0 copy.23
  5.5 0.0 copy-done
  5.5 0.0 copy-done.4
  5.5 3.4 copy_bitcast_fusion
  8.9 896.9 %layer.1 = (bf16[16,48,1024]{2,1,0:T(8,128)(2,1)}, bf16[16,48,1024]{2,1,0:T(8,128)(2,1)}, bf16[16,2,256,512]{3,2,1,0:T(8,128)(2,1)}, bf16[16,512,256]{2,1,0:T(8,...) custom-call(bf16[16,48,1024]{2,1,0:T(8,128)(2,1)} %get-tuple-element, ...), custom_call_target="tpu_custom_call" | custom-call | tf_op jit(solution)/shard_map/layer/pallas_call | solution.py:1673
  905.9 0.0 copy-start.3
  905.9 3.5 copy.24
  909.4 0.0 copy-done.3
  909.4 0.0 copy-start.5
  909.4 2.0 copy.25
  911.4 0.0 copy-done.5
  911.4 0.0 copy-start.2
  911.4 1.5 convert_element_type.24
  913.0 1.1 copy-done.2
  914.1 0.0 copy-start.1
  914.1 3.5 convert_element_type.23
  917.6 0.0 copy-done.1
  917.6 4.3 convert_element_type.26
  921.9 0.0 copy-start.6
  921.9 11.8 %convert_element_type.25 = f32[16,2,256,512]{3,2,1,0:T(8,128)} convert(bf16[16,2,256,512]{3,2,1,0:T(8,128)(2,1)} %get-tuple-element.18) | non-fusion elementwise | flops 4194304 | bytes 25165824 | tf_op jit(solution)/shard_map/convert_element_type | solution.py:1717
  933.7 0.0 copy-done.6
  933.7 0.6 copy.30
  (1 shorter events, 0.0 us)
Async XLA Ops:
  3.5 2.0 copy-start
  3.5 2.0 copy-start.4
  905.9 3.5 copy-start.3
  909.4 2.0 copy-start.5
  911.4 2.6 copy-start.2
  914.1 3.5 copy-start.1
  921.9 11.8 %copy-start.6 = (f32[2,16,256]{2,1,0:T(8,128)S(1)}, f32[2,16,256]{2,1,0:T(8,128)}, u32[]{:S(2)}) copy-start(f32[2,16,256]{2,1,0:T(8,128)} %get-tuple-element.50) | copy-start | bytes 98308

commit v5 on v4

--- a/solution.py
+++ b/solution.py
@@ -569,7 +569,7 @@
     return (
         frames == 4
         and group_size == ZN * YN
-        and local % 16 == 0
+        and local == 48
         and positions == 16
         and width % 128 == 0
         and (depth // frames) % 128 == 0
@@ -1006,21 +1006,25 @@
             self.out(j, outs, p).wait()
 
 
-COT_GATHER = GatherZ
 ATTN_REDUCE = ReduceY
 GIN_REDUCE = ReduceY
 BACK_REDUCE = ReduceY
-Z_FIRST = (0, 1, 2, 3, 4, 5, 6)
-FFN_Y_FIRST = (0, 1, 2, 3, 4, 5, 6, 7, 8, 9, 10, 11, 12, 13, 14, 15)
-ATT_Y_FIRST = (0, 1, 2, 3, 4, 5, 6, 7, 8, 9, 10, 11, 12, 13, 14, 15)
-
-SCHEDULE = (
-    ("RA5", 1), ("RG5", 3), ("RB3", 5), ("AC1", 0), ("A", 0), ("RF3", 3), ("Ef", 5), ("AF2", 1),
-    ("C", 2), ("RF4", 3), ("RB4", 5), ("RA2", 0), ("AC2", 0), ("AG2", 3), ("E", 4), ("AF3", 1),
-    ("Eg", 4), ("RA3", 0), ("AC5", 1), ("AC3", 0), ("Ff", 3), ("RG2", 2), ("AG3", 3), ("Cg", 2),
-    ("RG3", 2), ("RA4", 0), ("RB5", 5), ("Em", 4), ("AC4", 0), ("RF5", 3), ("K", 0), ("RG4", 2),
-    ("RB2", 4), ("AF4", 1), ("AG4", 3), ("Fm", 2), ("RF2", 2),
+FIRST_Y_FIRST = (6,)
+COT_Y_FIRST = (1, 4)
+FFN_Y_FIRST = (1, 2, 4, 5, 6, 7, 8, 9, 10, 11, 12, 13, 14, 15)
+ATT_Y_FIRST = (0, 2, 3, 4, 5, 6, 7, 8, 9, 10, 11, 12, 13, 14)
+Z_ROWS = (48, 48, 48, 48, 48, 48, 16, 16, 16, 16, 16, 16, 16, 16, 0, 0)
+
+SCHEDULES = (
+    (
+        ("AC1", 0), ("RA5", 1), ("RF3", 3), ("A", 0), ("Fm", 3), ("AG4", 4), ("RB3", 5), ("AC4", 1),
+        ("RG5", 3), ("AF2", 1), ("AC2", 0), ("RA2", 0), ("C", 2), ("RB4", 5), ("Ef", 5), ("RF4", 3),
+        ("RA3", 0), ("AG2", 3), ("E", 4), ("AF3", 1), ("Eg", 4), ("AC5", 1), ("RG2", 2), ("RA4", 0),
+        ("Ff", 3), ("RB5", 5), ("Em", 4), ("AC3", 0), ("RG3", 2), ("RF2", 2), ("AG3", 3), ("Cg", 2),
+        ("RF5", 3), ("K", 0), ("RG4", 2), ("AF4", 1), ("RB2", 4),
+    ),
 )
+CHANGES = ()
 
 
 class EitherGather:
@@ -1054,40 +1058,70 @@
         self.both(self.along_y.done, self.along_z.done)
 
 
-class EitherReduce:
+class SplitReduce:
     def __init__(self, place, part, over, ups, downs, send, recv):
-        self.along_z = ReduceZ(place, part, over.at[0], ups, downs, send, recv)
-        self.along_y = ReduceY(place, part, over, ups.at[:, 0], downs.at[:, 0], send, recv)
+        self.place, self.part, self.over, self.ups, self.downs = place, part, over, ups, downs
+        local = part.shape[2]
+
+        def pair(count):
+            first, rest = pl.ds(0, count), pl.ds(count, local - count)
+            runs = []
+            if count > 0:
+                runs.append(
+                    ReduceZ(
+                        place, part.at[:, :, first], over.at[0, first], ups.at[:, :, first], downs.at[:, :, first],
+                        send.at[0], recv.at[0],
+                    )
+                )
+            if count < local:
+                runs.append(
+                    ReduceY(
+                        place, part.at[:, :, rest], over.at[:, rest], ups.at[:, 0, rest], downs.at[:, 0, rest],
+                        send.at[1], recv.at[1],
+                    )
+                )
+            return runs
+
+        self.pairs = {count: pair(count * local // 48) for count in sorted(set(Z_ROWS))}
 
     def choose(self, i):
-        self.z_first = i < 0
-        for k in Z_FIRST:
-            self.z_first = self.z_first | (i == k)
+        self.chosen = {}
+        for count in self.pairs:
+            chosen = i < 0
+            for k in range(len(Z_ROWS)):
+                if Z_ROWS[k] == count:
+                    chosen = chosen | (i == k)
+            self.chosen[count] = chosen
         return self
 
-    def both(self, along_z, along_y):
-        when(self.z_first, along_z)
-        when(jnp.logical_not(self.z_first), along_y)
+    def both(self, run):
+        for count, pair in self.pairs.items():
+
+            def each(pair=pair):
+                for part in pair:
+                    run(part)
+
+            when(self.chosen[count], each)
 
     def t1(self):
-        self.both(self.along_z.t1, self.along_y.t1)
+        self.both(lambda part: part.t1())
 
     def t2(self):
-        self.both(self.along_z.t2, self.along_y.t2)
+        self.both(lambda part: part.t2())
 
     def t3(self):
-        self.both(self.along_z.t3, self.along_y.t3)
+        self.both(lambda part: part.t3())
 
     def t4(self):
-        self.both(self.along_z.t4, self.along_y.t4)
+        self.both(lambda part: part.t4())
 
     def done(self):
-        self.both(self.along_z.done, self.along_y.done)
+        self.both(lambda part: part.done())
 
     def total(self):
-        z = self.along_z.place.z
-        value = self.along_y.local(0)
-        return value + up_to_f32(z >= 1, self.along_y.ups.at[2]) + up_to_f32(z <= 2, self.along_y.downs.at[2])
+        z = self.place.z
+        value = self.part[0, 0].astype(f32) + self.over[0].astype(f32)
+        return value + up_to_f32(z >= 1, self.ups.at[2, 0]) + up_to_f32(z <= 2, self.downs.at[2, 0])
 
 
 class GainSum:
@@ -1118,7 +1152,7 @@
 
 
 def layer_kernel(
-    x_ref, cot_ref, mask_ref, gains_ref, masked_cot, in_w, out_w, gu_w, dn_w,
+    x_ref, cot_ref, mask_ref, gains_ref, in_w, out_w, gu_w, dn_w,
     out_hbm, ingrad_hbm, gu_hbm, dn_hbm, iw_hbm, ow_hbm, gain_out, rows_hbm, cot_hbm,
     g_ffn, g_att, cot_v, p_attn, p_gin, p_ffn, p_back,
     over_attn, over_gin, over_ffn, over_back, ups_attn, ups_gin, ups_ffn, ups_back,
@@ -1128,7 +1162,7 @@
     act_s, gg_s, gup_s, gmixed_s, gproj_s, hmid_s, ghmid_s, stage, gain_s, gain_pieces, gain_got,
     gu_sent, gu_kept, gu_core, gu_x, dn_sent, dn_kept, dn_core, dn_x,
     iw_sent, iw_kept, iw_core, iw_x, ow_sent, ow_kept, ow_core, ow_x,
-    sem_first, sem_first_got, sem_gather, sem_gather_got, sem_reduce, sem_reduce_got,
+    sem_first, sem_first_got, sem_gather, sem_gather_got, sem_reduce, sem_reduce_got, sem_split, sem_split_got,
     sem_grad_ffn, sem_grad_att, sem_gain, sem_local, credits, free,
 ):
     place = Place()
@@ -1169,13 +1203,10 @@
         return load(cot_hbm.at[p // 2, :, :, p % 2], cot_v, 9)
 
     def own_cot(j):
-        return load(masked_cot.at[j], cot_hbm.at[j, 0, 0], 16 + j)
+        return load(g_ffn.at[j // 4, j % 4], cot_hbm.at[j, 0, 0], 16 + j)
 
     def own_rows(j):
         return load(g_att.at[j // 4, j % 4], rows_hbm.at[j, 0, 0], 16 + pairs_of + j)
-
-    for j in range(pairs_of):
-        own_cot(j).start()
 
     barrier = pltpu.get_barrier_semaphore()
 
@@ -1200,22 +1231,29 @@
         return c
 
     def first_kind(g):
-        return GatherY if g == groups - 1 else GatherZ
+        return GatherY if g in FIRST_Y_FIRST else GatherZ
 
     firsts = [
         first_kind(g)(place, rows_hbm.at[g], sem_first.at[g], sem_first_got.at[g]) for g in range(groups)
     ]
 
     def cot_gather(j, which):
-        return COT_GATHER(place, cot_hbm.at[pairs_of - 1 - j], sem_gather.at[2, which], sem_gather_got.at[2, which])
+        sems = sem_gather.at[2, which], sem_gather_got.at[2, which]
+        return EitherGather(place, cot_hbm.at[pairs_of - 1 - j], *sems).choose(j, COT_Y_FIRST)
 
     for g in range(groups):
         lax.fori_loop(2 * g, 2 * g + 2, normalise, 0)
         own_rows(g).start()
         own_rows(g).wait()
         firsts[g].t1()
+
+    def masked(p, c):
+        g_ffn[p // 8, (p % 8) // 2, p % 2] = (mask * cot_ref[p].astype(f32)).astype(bf16)
+        return c
+
+    lax.fori_loop(0, positions, masked, 0)
     for j in range(pairs_of):
-        own_cot(j).wait()
+        own_cot(j).start()
     load_owa(last).start()
     load_gu(last).start()
     load_dn(last).start()
@@ -1244,6 +1282,8 @@
         firsts[g].t3()
     for g in range(groups):
         firsts[g].t4()
+    for j in range(pairs_of):
+        own_cot(j).wait()
     for g in range(groups):
         firsts[g].done()
         load_rows(2 * g, g_ffn.at[0], 6).start()
@@ -1384,7 +1424,11 @@
             return self.reduce(GIN_REDUCE, p_gin, over_gin, ups_gin, downs_gin, 1)
 
         def RF(self):
-            return self.reduce(EitherReduce, p_ffn.at[self.par], over_ffn, ups_ffn, downs_ffn, 2).choose(self.i)
+            par = self.par
+            return SplitReduce(
+                place, p_ffn.at[par], over_ffn.at[par], ups_ffn.at[par], downs_ffn.at[par],
+                sem_split.at[par], sem_split_got.at[par],
+            ).choose(self.i)
 
         def RB(self):
             return self.reduce(BACK_REDUCE, p_back.at[self.par], over_back, ups_back, downs_back, 3)
@@ -1587,16 +1631,18 @@
         when(z < 3, lambda: tell(1, "up"))
         when(z > 0, lambda: tell(2, "down"))
 
-    steps = positions + max(delay for name, delay in SCHEDULE if name[:2] != "AC")
+    steps = positions + max(delay for name, delay in SCHEDULES[0] if name[:2] != "AC")
     tell_all()
 
-    def step(s, c):
+    def step(low, high, schedule, s, c):
         pl.semaphore_wait(credits.at[0], 1)
         when(z > 0, lambda: pl.semaphore_wait(credits.at[1], 1))
         when(z < 3, lambda: pl.semaphore_wait(credits.at[2], 1))
-        for name, delay in SCHEDULE:
+        for name, delay in schedule:
             if name == "K":
                 when(s < steps - 1, tell_all)
+            elif high <= delay or low >= delay + (pairs_of if name[:2] == "AC" else positions):
+                continue
             elif name[:2] == "AC":
                 j = s - delay
                 when((j >= 0) & (j < pairs_of), cot_runs(j)[name])
@@ -1604,7 +1650,9 @@
                 when((s >= delay) & (s <= last + delay), Position(s - delay).runs()[name])
         return c
 
-    lax.fori_loop(0, steps, step, 0)
+    bounds = (0,) + CHANGES + (steps,)
+    for low, high, schedule in zip(bounds, bounds[1:], SCHEDULES):
+        lax.fori_loop(low, high, functools.partial(step, low, high, schedule), 0)
     gain_sum.next(4)
     gain_out[...] = gain_pieces[0, 0] / gains_ref[:, :, piece_at(0, f, quarter)]
     grad_ffn.drained(ffn_outs, 0)
@@ -1613,7 +1661,7 @@
     ingrad_copy(0).wait()
 
 
-def layer(x, cot, mask, gains, masked_cot, in_weight, out_weight, gate_up, down):
+def layer(x, cot, mask, gains, in_weight, out_weight, gate_up, down):
     positions, local, depth = x.shape
     width, hidden = out_weight.shape[1], down.shape[1]
     rows = ZN * YN * local
@@ -1632,7 +1680,7 @@
         [vm(2, *everything)] * 2
         + [vm(*everything)] * 3
         + [vm(2, *everything)] * 2
-        + [vm(2, ZN, *block), vm(2, ZN, *block), vm(2, ZN, *block), vm(2, ZN, *block)]
+        + [vm(2, ZN, *block)] * 4
         + [vm(2, 3, *block), vm(2, 3, *block), vm(2, 3, YN, *block), vm(2, 3, *block)] * 2
         + [vm(positions, rows, width)] * 4
         + [vm(positions, rows, width, dtype=f32)] * 2
@@ -1660,6 +1708,8 @@
             pltpu.SemaphoreType.DMA((3, 2, 8)),
             pltpu.SemaphoreType.DMA((4, 2, 10)),
             pltpu.SemaphoreType.DMA((4, 2, 11)),
+            pltpu.SemaphoreType.DMA((2, 2, 10)),
+            pltpu.SemaphoreType.DMA((2, 2, 11)),
             pltpu.SemaphoreType.DMA((5, 2)),
             pltpu.SemaphoreType.DMA((5, 2)),
             pltpu.SemaphoreType.DMA((2, 5)),
@@ -1672,7 +1722,7 @@
     anywhere = pl.BlockSpec(memory_space=pl.ANY)
     return pl.pallas_call(
         layer_kernel,
-        in_specs=[in_vmem] * 4 + [anywhere] * 5,
+        in_specs=[in_vmem] * 4 + [anywhere] * 4,
         out_specs=[anywhere] * 6 + [in_vmem, anywhere, anywhere],
         out_shape=[
             hbm(positions, *block),
@@ -1690,20 +1740,40 @@
             collective_id=0, has_side_effects=True, vmem_limit_bytes=KERNEL_VMEM_BYTES
         ),
         name="layer",
-    )(x, cot, mask, gains, masked_cot, in_weight, out_weight, gate_up, down)
+    )(x, cot, mask, gains, in_weight, out_weight, gate_up, down)
+
+
+def widen_kernel(*refs):
+    half = len(refs) // 2
+    for narrow, wide in zip(refs[:half], refs[half:]):
+        wide[...] = narrow[...].astype(f32)
+
+
+def widened(*arrays):
+    def spec(a):
+        rank = a.ndim
+        return pl.BlockSpec((1,) + a.shape[1:], lambda i: (i,) + (0,) * (rank - 1))
+
+    return pl.pallas_call(
+        widen_kernel,
+        grid=(arrays[0].shape[0],),
+        in_specs=[spec(a) for a in arrays],
+        out_specs=[spec(a) for a in arrays],
+        out_shape=[jax.ShapeDtypeStruct(a.shape, f32) for a in arrays],
+        compiler_params=pltpu.CompilerParams(vmem_limit_bytes=32 * 1024 * 1024),
+        name="widen",
+    )(*arrays)
 
 
 def body_in_one(inputs, counts, norm_gains, in_weight, out_weight, gate_up, down_weight, cotangent):
-    local, positions, depth = inputs.shape
+    local = inputs.shape[0]
     ids = lax.axis_index("mp") * local + jnp.arange(local)
     valid = ids < counts[0]
-    masked = jnp.where(valid[:, None, None], cotangent, jnp.zeros_like(cotangent))
     output, input_grad, g_gu, g_dn, g_in, g_out, gain_sums, _, _ = layer(
         jnp.swapaxes(inputs, 0, 1),
         jnp.swapaxes(cotangent, 0, 1),
         valid.astype(f32)[:, None],
         norm_gains,
-        jnp.swapaxes(masked, 0, 1).reshape(positions // 2, 2, local, depth),
         in_weight,
         out_weight,
         gate_up,
@@ -1712,10 +1782,7 @@
     return (
         jnp.swapaxes(output, 0, 1),
         jnp.swapaxes(input_grad, 0, 1),
-        g_in.astype(f32),
-        g_out.astype(f32),
-        g_gu.astype(f32),
-        g_dn.astype(f32),
+        *widened(g_in, g_out, g_gu, g_dn),
         gain_sums,
     )
 

time: 935 us -> 899 us (0.961)
  other arithmetic: 23.4 us -> 0.62 us
  Pallas kernels: 897 us -> 878 us
    convert_element_type x4 -> x0, other arithmetic: 21.2 us -> none  [the longest x1 11.8 us: body_in_one(): g_gu.astype(f32)]
    pallas_call x1 -> x2, Pallas kernels: 897 us -> 878 us  [the longest x1 867 us: layer(): pl.pallas_call(layer_kernel, in_specs=[in_vmem] * 4 + [anywhere] * 4, out...]
where the time goes in v5:
time: 899 us; the launch traced here: 898 us
  Pallas kernels  878 us (98%)
  local copies, waits for them, and re-layouts  18.2 us (2%)
    pallas_call x1, Pallas kernels, layer(): pl.pallas_call(layer_kernel, in_specs=[in_vmem] * 4 + [anywhere] * 4, out...  867 us

profile of v5, /device:TPU:0, one launch (start us, length us, event | category | flops | bytes accessed | tf_op | source)
XLA Modules:
  0.0 898.5 jit_solution(74722759424858604)
XLA Ops:
  1.3 0.6 fusion.mask_ref
  1.9 5.3 copy_bitcast_fusion
  7.2 866.7 %layer.1 = (bf16[16,48,1024]{2,1,0:T(8,128)(2,1)}, bf16[16,48,1024]{2,1,0:T(8,128)(2,1)}, bf16[16,2,256,512]{3,2,1,0:T(8,128)(2,1)}, bf16[16,512,256]{2,1,0:T(8,...) custom-call(bf16[16,48,1024]{2,1,0:T(8,128)(2,1)} %get-tuple-element, ...), custom_call_target="tpu_custom_call" | custom-call | tf_op jit(solution)/shard_map/layer/pallas_call | solution.py:1723
  873.9 0.0 copy-start.1
  873.9 3.6 copy.22
  877.5 0.0 copy-start.3
  877.5 3.5 copy.23
  881.0 0.0 copy-done.1
  881.0 0.0 copy-done.3
  881.0 0.0 copy-start
  881.0 3.4 copy-done
  884.4 0.0 copy-start.2
  884.4 1.9 copy-done.2
  886.3 0.0 copy-start.4
  886.3 11.6 %widen.1 = (f32[16,3,256,128]{3,2,1,0:T(8,128)}, f32[16,128,256]{2,1,0:T(8,128)}, f32[16,2,256,512]{3,2,1,0:T(8,128)}, f32[16,512,256]{2,1,0:T(8,128)}) custom-call(bf16[16,3,256,128]{3,2,1,0:T(8,128)(2,1)S(1)} %copy-done.2, bf16[16,128,256]{2,1,0:T(8,128)(2,1)S(1)} %copy-done.3, bf16[16,2,256,512]{3,2,1,0:T(8,128)(2,1)S(1)} %copy-done, ...), custom_call_target="tpu_custom_call" | custom-call | tf_op jit(solution)/shard_map/widen/pallas_call | solution.py:1757
  897.9 0.0 copy-done.4
  897.9 0.6 copy.28
Async XLA Ops:
  873.9 7.1 copy-start.1
  877.5 3.5 copy-start.3
  881.0 3.4 copy-start
  884.4 1.9 copy-start.2
  886.3 11.6 %copy-start.4 = (f32[2,16,256]{2,1,0:T(8,128)S(1)}, f32[2,16,256]{2,1,0:T(8,128)}, u32[]{:S(2)}) copy-start(f32[2,16,256]{2,1,0:T(8,128)} %get-tuple-element.58) | copy-start | bytes 98308

commit v6 on v5

--- a/solution.py
+++ b/solution.py
@@ -1006,60 +1006,81 @@
             self.out(j, outs, p).wait()
 
 
-ATTN_REDUCE = ReduceY
 GIN_REDUCE = ReduceY
 BACK_REDUCE = ReduceY
-FIRST_Y_FIRST = (6,)
-COT_Y_FIRST = (1, 4)
-FFN_Y_FIRST = (1, 2, 4, 5, 6, 7, 8, 9, 10, 11, 12, 13, 14, 15)
-ATT_Y_FIRST = (0, 2, 3, 4, 5, 6, 7, 8, 9, 10, 11, 12, 13, 14)
-Z_ROWS = (48, 48, 48, 48, 48, 48, 16, 16, 16, 16, 16, 16, 16, 16, 0, 0)
+FIRST_Y_ROWS = (0, 0, 0, 0, 0, 0, 16, 16)
+COT_Y_ROWS = (16, 16, 0, 0, 0, 0, 0, 16)
+FFN_Y_ROWS = (0, 48, 32, 48, 32, 48, 32, 48, 48, 48, 48, 48, 48, 48, 48, 16)
+ATT_Y_ROWS = (48, 48, 32, 48, 48, 48, 48, 48, 48, 48, 48, 48, 48, 48, 0, 0)
+FFN_Z_ROWS = (32, 16, 16, 32, 16, 16, 16, 16, 16, 16, 16, 16, 16, 0, 16, 48)
+ATTN_Z_ROWS = (0, 0, 48, 48, 48, 48, 48, 48, 0, 0, 0, 0, 0, 0, 0, 0)
 
 SCHEDULES = (
     (
-        ("AC1", 0), ("RA5", 1), ("RF3", 3), ("A", 0), ("Fm", 3), ("AG4", 4), ("RB3", 5), ("AC4", 1),
-        ("RG5", 3), ("AF2", 1), ("AC2", 0), ("RA2", 0), ("C", 2), ("RB4", 5), ("Ef", 5), ("RF4", 3),
-        ("RA3", 0), ("AG2", 3), ("E", 4), ("AF3", 1), ("Eg", 4), ("AC5", 1), ("RG2", 2), ("RA4", 0),
-        ("Ff", 3), ("RB5", 5), ("Em", 4), ("AC3", 0), ("RG3", 2), ("RF2", 2), ("AG3", 3), ("Cg", 2),
-        ("RF5", 3), ("K", 0), ("RG4", 2), ("AF4", 1), ("RB2", 4),
+        ("AC1", 0), ("RA5", 1), ("A", 0), ("RF3", 3), ("AC4", 1), ("Fm", 3), ("AG4", 4), ("RB3", 5),
+        ("RG5", 3), ("AC2", 0), ("RA2", 0), ("AF2", 1), ("RF4", 3), ("C", 2), ("RB4", 5), ("Ef", 5),
+        ("RA3", 0), ("AG2", 3), ("E", 4), ("RG2", 2), ("AF3", 1), ("Eg", 4), ("RB5", 5), ("Ff", 3),
+        ("RA4", 0), ("AC5", 1), ("AC3", 0), ("RF5", 3), ("RG3", 2), ("RF2", 2), ("AG3", 3), ("Cg", 2),
+        ("K", 0), ("Em", 4), ("AF4", 1), ("RG4", 2), ("RB2", 4),
     ),
 )
 CHANGES = ()
 
 
-class EitherGather:
-    def __init__(self, place, g, send, recv):
-        self.along_y = GatherY(place, g, send, recv)
-        self.along_z = GatherZ(place, g, send, recv)
-
-    def choose(self, i, y_first):
-        self.y_first = i < 0
-        for k in y_first:
-            self.y_first = self.y_first | (i == k)
+class Split:
+    def choose(self, i, table):
+        self.chosen = {}
+        for count in self.pairs:
+            chosen = i < 0
+            for k in range(len(table)):
+                if table[k] == count:
+                    chosen = chosen | (i == k)
+            self.chosen[count] = chosen
         return self
 
-    def both(self, along_y, along_z):
-        when(self.y_first, along_y)
-        when(jnp.logical_not(self.y_first), along_z)
+    def both(self, run):
+        for count, pair in self.pairs.items():
+
+            def each(pair=pair):
+                for part in pair:
+                    run(part)
+
+            when(self.chosen[count], each)
 
     def t1(self):
-        self.both(self.along_y.t1, self.along_z.t1)
+        self.both(lambda part: part.t1())
 
     def t2(self):
-        self.both(self.along_y.t2, self.along_z.t2)
+        self.both(lambda part: part.t2())
 
     def t3(self):
-        self.both(self.along_y.t3, self.along_z.t3)
+        self.both(lambda part: part.t3())
 
     def t4(self):
-        self.both(self.along_y.t4, self.along_z.t4)
+        self.both(lambda part: part.t4())
 
     def done(self):
-        self.both(self.along_y.done, self.along_z.done)
-
-
-class SplitReduce:
-    def __init__(self, place, part, over, ups, downs, send, recv):
+        self.both(lambda part: part.done())
+
+
+class SplitGather(Split):
+    def __init__(self, place, g, send, recv, table, rows=0):
+        def cut(start, size):
+            return g.at[(slice(None), slice(None)) + (slice(None),) * rows + (pl.ds(start, size),)]
+
+        def pair(count, local):
+            runs = []
+            if count > 0:
+                runs.append(GatherY(place, cut(0, count), send.at[0], recv.at[0]))
+            if count < local:
+                runs.append(GatherZ(place, cut(count, local - count), send.at[1], recv.at[1]))
+            return runs
+
+        self.pairs = {count: pair(count, g.shape[2 + rows]) for count in sorted(set(table))}
+
+
+class SplitReduce(Split):
+    def __init__(self, place, part, over, ups, downs, send, recv, table):
         self.place, self.part, self.over, self.ups, self.downs = place, part, over, ups, downs
         local = part.shape[2]
 
@@ -1082,41 +1103,7 @@
                 )
             return runs
 
-        self.pairs = {count: pair(count * local // 48) for count in sorted(set(Z_ROWS))}
-
-    def choose(self, i):
-        self.chosen = {}
-        for count in self.pairs:
-            chosen = i < 0
-            for k in range(len(Z_ROWS)):
-                if Z_ROWS[k] == count:
-                    chosen = chosen | (i == k)
-            self.chosen[count] = chosen
-        return self
-
-    def both(self, run):
-        for count, pair in self.pairs.items():
-
-            def each(pair=pair):
-                for part in pair:
-                    run(part)
-
-            when(self.chosen[count], each)
-
-    def t1(self):
-        self.both(lambda part: part.t1())
-
-    def t2(self):
-        self.both(lambda part: part.t2())
-
-    def t3(self):
-        self.both(lambda part: part.t3())
-
-    def t4(self):
-        self.both(lambda part: part.t4())
-
-    def done(self):
-        self.both(lambda part: part.done())
+        self.pairs = {count: pair(count) for count in sorted(set(table))}
 
     def total(self):
         z = self.place.z
@@ -1230,16 +1217,16 @@
         g_att[p // 8, (p % 8) // 2, p % 2] = value.astype(bf16)
         return c
 
-    def first_kind(g):
-        return GatherY if g in FIRST_Y_FIRST else GatherZ
-
     firsts = [
-        first_kind(g)(place, rows_hbm.at[g], sem_first.at[g], sem_first_got.at[g]) for g in range(groups)
+        SplitGather(place, rows_hbm.at[g], sem_first.at[g], sem_first_got.at[g], FIRST_Y_ROWS[g : g + 1], 1).choose(
+            g, FIRST_Y_ROWS
+        )
+        for g in range(groups)
     ]
 
     def cot_gather(j, which):
         sems = sem_gather.at[2, which], sem_gather_got.at[2, which]
-        return EitherGather(place, cot_hbm.at[pairs_of - 1 - j], *sems).choose(j, COT_Y_FIRST)
+        return SplitGather(place, cot_hbm.at[pairs_of - 1 - j], *sems, COT_Y_ROWS, 1).choose(j, COT_Y_ROWS)
 
     for g in range(groups):
         lax.fori_loop(2 * g, 2 * g + 2, normalise, 0)
@@ -1400,9 +1387,10 @@
             self.par = lax.rem(i + 16, 2)
             self.ring = lax.rem(i + 16, 4)
 
-        def gather(self, kind, g, number):
+        def gather(self, g, number, table):
             par = self.par
-            return kind(place, g.at[par], sem_gather.at[number, par], sem_gather_got.at[number, par])
+            sems = sem_gather.at[number, par], sem_gather_got.at[number, par]
+            return SplitGather(place, g.at[par], *sems, table).choose(self.i, table)
 
         def reduce(self, kind, part, over, ups, downs, number):
             par = self.par
@@ -1412,23 +1400,27 @@
             )
 
         def AF(self):
-            return self.gather(EitherGather, g_ffn, 0).choose(self.i, FFN_Y_FIRST)
+            return self.gather(g_ffn, 0, FFN_Y_ROWS)
 
         def AG(self):
-            return self.gather(EitherGather, g_att, 1).choose(self.i, ATT_Y_FIRST)
+            return self.gather(g_att, 1, ATT_Y_ROWS)
+
+        def split(self, part, over, ups, downs, number, table):
+            par = self.par
+            event = SplitReduce(
+                place, part, over.at[par], ups.at[par], downs.at[par],
+                sem_split.at[number, par], sem_split_got.at[number, par], table,
+            )
+            return event.choose(self.i, table)
 
         def RA(self):
-            return self.reduce(ATTN_REDUCE, p_attn, over_attn, ups_attn, downs_attn, 0)
+            return self.split(p_attn, over_attn, ups_attn, downs_attn, 1, ATTN_Z_ROWS)
 
         def RG(self):
             return self.reduce(GIN_REDUCE, p_gin, over_gin, ups_gin, downs_gin, 1)
 
         def RF(self):
-            par = self.par
-            return SplitReduce(
-                place, p_ffn.at[par], over_ffn.at[par], ups_ffn.at[par], downs_ffn.at[par],
-                sem_split.at[par], sem_split_got.at[par],
-            ).choose(self.i)
+            return self.split(p_ffn.at[self.par], over_ffn, ups_ffn, downs_ffn, 0, FFN_Z_ROWS)
 
         def RB(self):
             return self.reduce(BACK_REDUCE, p_back.at[self.par], over_back, ups_back, downs_back, 3)
@@ -1681,7 +1673,7 @@
         + [vm(*everything)] * 3
         + [vm(2, *everything)] * 2
         + [vm(2, ZN, *block)] * 4
-        + [vm(2, 3, *block), vm(2, 3, *block), vm(2, 3, YN, *block), vm(2, 3, *block)] * 2
+        + [vm(2, 3, YN, *block), vm(2, 3, *block), vm(2, 3, YN, *block), vm(2, 3, *block)] * 2
         + [vm(positions, rows, width)] * 4
         + [vm(positions, rows, width, dtype=f32)] * 2
         + [vm(positions, rows // 2, width, dtype=f32)] * 2
@@ -1702,14 +1694,14 @@
         + [vm(2, width, quarter)] * 3
         + [vm(width, quarter)]
         + [
-            pltpu.SemaphoreType.DMA((groups, 10)),
-            pltpu.SemaphoreType.DMA((groups, 8)),
-            pltpu.SemaphoreType.DMA((3, 2, 10)),
-            pltpu.SemaphoreType.DMA((3, 2, 8)),
+            pltpu.SemaphoreType.DMA((groups, 2, 10)),
+            pltpu.SemaphoreType.DMA((groups, 2, 8)),
+            pltpu.SemaphoreType.DMA((3, 2, 2, 10)),
+            pltpu.SemaphoreType.DMA((3, 2, 2, 8)),
             pltpu.SemaphoreType.DMA((4, 2, 10)),
             pltpu.SemaphoreType.DMA((4, 2, 11)),
-            pltpu.SemaphoreType.DMA((2, 2, 10)),
-            pltpu.SemaphoreType.DMA((2, 2, 11)),
+            pltpu.SemaphoreType.DMA((2, 2, 2, 10)),
+            pltpu.SemaphoreType.DMA((2, 2, 2, 11)),
             pltpu.SemaphoreType.DMA((5, 2)),
             pltpu.SemaphoreType.DMA((5, 2)),
             pltpu.SemaphoreType.DMA((2, 5)),
@@ -1760,7 +1752,7 @@
         in_specs=[spec(a) for a in arrays],
         out_specs=[spec(a) for a in arrays],
         out_shape=[jax.ShapeDtypeStruct(a.shape, f32) for a in arrays],
-        compiler_params=pltpu.CompilerParams(vmem_limit_bytes=32 * 1024 * 1024),
+        compiler_params=pltpu.CompilerParams(vmem_limit_bytes=KERNEL_VMEM_BYTES),
         name="widen",
     )(*arrays)
 

time: 899 us -> 886 us (0.986)
    pallas_call x1, Pallas kernels: 867 us -> 853 us  [layer(): pl.pallas_call(layer_kernel, in_specs=[in_vmem] * 4 + [anywhere] * 4, out...]
where the time goes in v6:
time: 886 us; the launch traced here: 885 us
  Pallas kernels  872 us (98%)
  local copies, waits for them, and re-layouts  11.4 us (1%)
    pallas_call x1, Pallas kernels, layer(): pl.pallas_call(layer_kernel, in_specs=[in_vmem] * 4 + [anywhere] * 4, out...  853 us
    pallas_call x1, Pallas kernels, widened(): pl.pallas_call(widen_kernel, grid=(arrays[0].shape[0],), in_specs=[spec(a...  18.8 us

profile of v6, /device:TPU:0, one launch (start us, length us, event | category | flops | bytes accessed | tf_op | source)
XLA Modules:
  0.0 885.5 jit_solution(2904991658641650062)
XLA Ops:
  1.3 0.6 fusion.mask_ref
  1.9 5.3 copy_bitcast_fusion
  7.2 853.3 %layer.1 = (bf16[16,48,1024]{2,1,0:T(8,128)(2,1)}, bf16[16,48,1024]{2,1,0:T(8,128)(2,1)}, bf16[16,2,256,512]{3,2,1,0:T(8,128)(2,1)}, bf16[16,512,256]{2,1,0:T(8,...) custom-call(bf16[16,48,1024]{2,1,0:T(8,128)(2,1)} %get-tuple-element, ...), custom_call_target="tpu_custom_call" | custom-call | tf_op jit(solution)/shard_map/layer/pallas_call | solution.py:1715
  860.5 0.0 copy-start
  860.5 3.5 copy.22
  864.1 0.0 copy-done
  864.1 2.0 copy.23
  866.1 0.0 copy-start.1
  866.1 18.8 %widen.1 = (f32[16,3,256,128]{3,2,1,0:T(8,128)}, f32[16,128,256]{2,1,0:T(8,128)}, f32[16,2,256,512]{3,2,1,0:T(8,128)}, f32[16,512,256]{2,1,0:T(8,128)}) custom-call(bf16[16,3,256,128]{3,2,1,0:T(8,128)(2,1)} %get-tuple-element.20.refs_0_, bf16[16,128,256]{2,1,0:T(8,128)(2,1)} %get-tuple-element.21.refs_1_, ...), custom_call_target="tpu_custom_call" | custom-call | tf_op jit(solution)/shard_map/widen/pallas_call | solution.py:1749
  884.9 0.0 copy-done.1
  884.9 0.6 copy.28
Async XLA Ops:
  860.5 3.5 copy-start
  866.1 18.8 %copy-start.1 = (f32[2,16,256]{2,1,0:T(8,128)S(1)}, f32[2,16,256]{2,1,0:T(8,128)}, u32[]{:S(2)}) copy-start(f32[2,16,256]{2,1,0:T(8,128)} %get-tuple-element.58) | copy-start | bytes 98308

commit v7 on v6

--- a/solution.py
+++ b/solution.py
@@ -1008,23 +1008,37 @@
 
 GIN_REDUCE = ReduceY
 BACK_REDUCE = ReduceY
-FIRST_Y_ROWS = (0, 0, 0, 0, 0, 0, 16, 16)
-COT_Y_ROWS = (16, 16, 0, 0, 0, 0, 0, 16)
-FFN_Y_ROWS = (0, 48, 32, 48, 32, 48, 32, 48, 48, 48, 48, 48, 48, 48, 48, 16)
-ATT_Y_ROWS = (48, 48, 32, 48, 48, 48, 48, 48, 48, 48, 48, 48, 48, 48, 0, 0)
-FFN_Z_ROWS = (32, 16, 16, 32, 16, 16, 16, 16, 16, 16, 16, 16, 16, 0, 16, 48)
-ATTN_Z_ROWS = (0, 0, 48, 48, 48, 48, 48, 48, 0, 0, 0, 0, 0, 0, 0, 0)
+FIRST_Y_ROWS = (0, 0, 0, 16, 16, 0, 0, 0)
+COT_Y_ROWS = (16, 32, 16, 16, 16, 16, 16, 16)
+FFN_Y_ROWS = (0, 0, 16, 0, 0, 16, 0, 32, 48, 48, 48, 48, 48, 48, 48, 0)
+ATT_Y_ROWS = (16, 48, 48, 32, 48, 48, 48, 48, 48, 48, 48, 48, 48, 16, 0, 16)
+FFN_Z_ROWS = (32, 32, 32, 32, 32, 32, 16, 16, 16, 16, 16, 16, 16, 0, 48, 48)
+ATTN_Z_ROWS = (0, 0, 48, 48, 48, 48, 48, 48, 48, 0, 0, 0, 0, 0, 0, 0)
 
 SCHEDULES = (
     (
-        ("AC1", 0), ("RA5", 1), ("A", 0), ("RF3", 3), ("AC4", 1), ("Fm", 3), ("AG4", 4), ("RB3", 5),
-        ("RG5", 3), ("AC2", 0), ("RA2", 0), ("AF2", 1), ("RF4", 3), ("C", 2), ("RB4", 5), ("Ef", 5),
-        ("RA3", 0), ("AG2", 3), ("E", 4), ("RG2", 2), ("AF3", 1), ("Eg", 4), ("RB5", 5), ("Ff", 3),
-        ("RA4", 0), ("AC5", 1), ("AC3", 0), ("RF5", 3), ("RG3", 2), ("RF2", 2), ("AG3", 3), ("Cg", 2),
-        ("K", 0), ("Em", 4), ("AF4", 1), ("RG4", 2), ("RB2", 4),
+        ("AC1", 0), ("AC3", 1), ("Fm", 3), ("RF3", 3), ("RA5", 1), ("A", 0), ("AG4", 4), ("RG5", 3),
+        ("RB3", 5), ("AC2", 0), ("C", 2), ("RF4", 3), ("RA2", 0), ("AC4", 1), ("AG2", 3), ("AF2", 1),
+        ("E", 4), ("RG2", 2), ("Ef", 5), ("Ff", 3), ("RA3", 0), ("Eg", 4), ("RB4", 5), ("Cg", 2),
+        ("RG3", 2), ("RF5", 3), ("AF3", 1), ("RF2", 2), ("AG3", 3), ("RB2", 4), ("AC5", 1), ("Em", 4),
+        ("RA4", 0), ("RB5", 5), ("K", 0), ("RG4", 2), ("AF4", 1),
+    ),
+    (
+        ("RA5", 1), ("A", 0), ("AC3", 1), ("RF3", 3), ("Fm", 3), ("AF2", 1), ("Ef", 5), ("AG4", 4),
+        ("RG5", 3), ("AC4", 1), ("RA2", 0), ("RB3", 5), ("RF4", 3), ("C", 2), ("AF3", 1), ("RA3", 0),
+        ("AG2", 3), ("E", 4), ("RG2", 2), ("RB4", 5), ("AC1", 0), ("RA4", 0), ("AC5", 1), ("AC2", 0),
+        ("AF4", 1), ("Ff", 3), ("RF5", 3), ("Eg", 4), ("RG3", 2), ("RF2", 2), ("Cg", 2), ("Em", 4),
+        ("AG3", 3), ("RB5", 5), ("K", 0), ("RG4", 2), ("RB2", 4),
+    ),
+    (
+        ("Fm", 3), ("RF3", 3), ("RA5", 1), ("AC1", 0), ("AG4", 4), ("A", 0), ("RA2", 0), ("RG5", 3),
+        ("C", 2), ("RB3", 5), ("Ef", 5), ("RF4", 3), ("AF2", 1), ("E", 4), ("AC2", 0), ("Eg", 4),
+        ("AF3", 1), ("AC3", 1), ("RG2", 2), ("RB4", 5), ("AG2", 3), ("Em", 4), ("Ff", 3), ("AC4", 1),
+        ("RA3", 0), ("RG3", 2), ("RF2", 2), ("Cg", 2), ("AF4", 1), ("AG3", 3), ("RG4", 2), ("RA4", 0),
+        ("RF5", 3), ("RB2", 4), ("AC5", 1), ("RB5", 5), ("K", 0),
     ),
 )
-CHANGES = ()
+CHANGES = (9, 16)
 
 
 class Split:

time: 886 us -> 890 us (level)
  no operation moved by 1% of the time
where the time goes in v7:
time: 890 us; the launch traced here: 883 us
  Pallas kernels  869 us (98%)
  local copies, waits for them, and re-layouts  11.4 us (1%)
    pallas_call x1, Pallas kernels, layer(): pl.pallas_call(layer_kernel, in_specs=[in_vmem] * 4 + [anywhere] * 4, out...  850 us
    pallas_call x1, Pallas kernels, widened(): pl.pallas_call(widen_kernel, grid=(arrays[0].shape[0],), in_specs=[spec(a...  18.8 us

profile of v7, /device:TPU:0, one launch (start us, length us, event | category | flops | bytes accessed | tf_op | source)
XLA Modules:
  0.0 882.8 jit_solution(2812526415279234491)
XLA Ops:
  1.3 0.6 fusion.mask_ref
  1.9 5.3 copy_bitcast_fusion
  7.2 850.5 %layer.1 = (bf16[16,48,1024]{2,1,0:T(8,128)(2,1)}, bf16[16,48,1024]{2,1,0:T(8,128)(2,1)}, bf16[16,2,256,512]{3,2,1,0:T(8,128)(2,1)}, bf16[16,512,256]{2,1,0:T(8,...) custom-call(bf16[16,48,1024]{2,1,0:T(8,128)(2,1)} %get-tuple-element, ...), custom_call_target="tpu_custom_call" | custom-call | tf_op jit(solution)/shard_map/layer/pallas_call | solution.py:1729
  857.6 0.0 copy-start
  857.6 3.5 copy.22
  861.2 0.0 copy-done
  861.2 2.0 copy.23
  863.2 0.0 copy-start.1
  863.2 18.8 %widen.1 = (f32[16,3,256,128]{3,2,1,0:T(8,128)}, f32[16,128,256]{2,1,0:T(8,128)}, f32[16,2,256,512]{3,2,1,0:T(8,128)}, f32[16,512,256]{2,1,0:T(8,128)}) custom-call(bf16[16,3,256,128]{3,2,1,0:T(8,128)(2,1)} %get-tuple-element.20.refs_0_, bf16[16,128,256]{2,1,0:T(8,128)(2,1)} %get-tuple-element.21.refs_1_, ...), custom_call_target="tpu_custom_call" | custom-call | tf_op jit(solution)/shard_map/widen/pallas_call | solution.py:1763
  882.0 0.0 copy-done.1
  882.0 0.6 copy.28
Async XLA Ops:
  857.6 3.5 copy-start
  863.2 18.8 %copy-start.1 = (f32[2,16,256]{2,1,0:T(8,128)S(1)}, f32[2,16,256]{2,1,0:T(8,128)}, u32[]{:S(2)}) copy-start(f32[2,16,256]{2,1,0:T(8,128)} %get-tuple-element.58) | copy-start | bytes 98308

commit v8 on v6

--- a/solution.py
+++ b/solution.py
@@ -1008,20 +1008,20 @@
 
 GIN_REDUCE = ReduceY
 BACK_REDUCE = ReduceY
-FIRST_Y_ROWS = (0, 0, 0, 0, 0, 0, 16, 16)
+FIRST_Y_ROWS = (0, 16, 16, 0, 0, 0, 0, 0)
 COT_Y_ROWS = (16, 16, 0, 0, 0, 0, 0, 16)
-FFN_Y_ROWS = (0, 48, 32, 48, 32, 48, 32, 48, 48, 48, 48, 48, 48, 48, 48, 16)
-ATT_Y_ROWS = (48, 48, 32, 48, 48, 48, 48, 48, 48, 48, 48, 48, 48, 48, 0, 0)
-FFN_Z_ROWS = (32, 16, 16, 32, 16, 16, 16, 16, 16, 16, 16, 16, 16, 0, 16, 48)
-ATTN_Z_ROWS = (0, 0, 48, 48, 48, 48, 48, 48, 0, 0, 0, 0, 0, 0, 0, 0)
+FFN_Y_ROWS = (0, 48, 32, 48, 48, 48, 48, 48, 48, 48, 48, 48, 48, 48, 32, 0)
+ATT_Y_ROWS = (16, 48, 32, 32, 32, 48, 48, 48, 48, 48, 48, 48, 32, 16, 0, 0)
+FFN_Z_ROWS = (32, 32, 32, 32, 32, 48, 32, 16, 16, 16, 16, 16, 16, 16, 48, 48)
+ATTN_Z_ROWS = (0, 0, 48, 48, 48, 48, 48, 0, 0, 0, 0, 0, 0, 0, 0, 0)
 
 SCHEDULES = (
     (
-        ("AC1", 0), ("RA5", 1), ("A", 0), ("RF3", 3), ("AC4", 1), ("Fm", 3), ("AG4", 4), ("RB3", 5),
-        ("RG5", 3), ("AC2", 0), ("RA2", 0), ("AF2", 1), ("RF4", 3), ("C", 2), ("RB4", 5), ("Ef", 5),
-        ("RA3", 0), ("AG2", 3), ("E", 4), ("RG2", 2), ("AF3", 1), ("Eg", 4), ("RB5", 5), ("Ff", 3),
-        ("RA4", 0), ("AC5", 1), ("AC3", 0), ("RF5", 3), ("RG3", 2), ("RF2", 2), ("AG3", 3), ("Cg", 2),
-        ("K", 0), ("Em", 4), ("AF4", 1), ("RG4", 2), ("RB2", 4),
+        ("AC1", 0), ("RA5", 1), ("A", 0), ("RF3", 3), ("Fm", 3), ("RB3", 5), ("RG5", 3), ("AG4", 4),
+        ("AC4", 1), ("AC2", 0), ("RA2", 0), ("AF2", 1), ("C", 2), ("RB4", 5), ("Ef", 5), ("RF4", 3),
+        ("AG2", 3), ("RA3", 0), ("E", 4), ("AF3", 1), ("Eg", 4), ("RG2", 2), ("RB5", 5), ("Ff", 3),
+        ("RA4", 0), ("AC3", 0), ("Em", 4), ("AC5", 1), ("RG3", 2), ("RF2", 2), ("AG3", 3), ("Cg", 2),
+        ("RF5", 3), ("K", 0), ("RG4", 2), ("RB2", 4), ("AF4", 1),
     ),
 )
 CHANGES = ()
@@ -1031,11 +1031,8 @@
     def choose(self, i, table):
         self.chosen = {}
         for count in self.pairs:
-            chosen = i < 0
-            for k in range(len(table)):
-                if table[k] == count:
-                    chosen = chosen | (i == k)
-            self.chosen[count] = chosen
+            places = sum(1 << k for k in range(len(table)) if table[k] == count)
+            self.chosen[count] = (places >> (i % 16)) % 2 == 1
         return self
 
     def both(self, run):
@@ -1208,8 +1205,16 @@
 
     groups = pairs_of
 
+    tile_row = lax.broadcasted_iota(jnp.int32, (8, depth), 0)
+
+    def tile_of(p):
+        return pl.ds(pl.multiple_of((p // 8) * 8, 8), 8)
+
     def gain_of(which, p):
-        return gains_ref[which, pl.ds(p, 1), :]
+        return jnp.sum(jnp.where(tile_row == p % 8, gains_ref[which, tile_of(p)], 0.0), axis=0, keepdims=True)
+
+    def set_gain_sum(which, p, value):
+        gain_s[which, tile_of(p)] = jnp.where(tile_row == p % 8, value, gain_s[which, tile_of(p)])
 
     def normalise(p, c):
         residual = x_ref[p].astype(f32)
@@ -1462,7 +1467,7 @@
             back = dot(gg_s[...], gu_v[0], NT) + dot(gup_s[...], gu_v[1], NT)
             p_gin[...] = back.astype(bf16).reshape(blocks)
             self.RG().t1()
-            gain_s[1, pl.ds(p, 1), :] = jnp.sum(back * x.astype(f32), axis=0, keepdims=True)
+            set_gain_sum(1, p, jnp.sum(back * x.astype(f32), axis=0, keepdims=True))
             p_ffn[par] = dot(act_s[...], dn_v[...], NN).astype(bf16).reshape(blocks)
             self.RF().t1()
 
@@ -1528,7 +1533,7 @@
             back = back + dot(gproj_s[2], iw_v[0, 2], NT)
             p_back[par] = back.astype(bf16).reshape(blocks)
             self.RB().t1()
-            gain_s[0, pl.ds(p, 1), :] = jnp.sum(back * xb[...].reshape(rows, depth).astype(f32), axis=0, keepdims=True)
+            set_gain_sum(0, p, jnp.sum(back * xb[...].reshape(rows, depth).astype(f32), axis=0, keepdims=True))
 
             @pl.when(p == 0)
             def _():
@@ -1744,11 +1749,11 @@
 def widened(*arrays):
     def spec(a):
         rank = a.ndim
-        return pl.BlockSpec((1,) + a.shape[1:], lambda i: (i,) + (0,) * (rank - 1))
+        return pl.BlockSpec((2,) + a.shape[1:], lambda i: (i,) + (0,) * (rank - 1))
 
     return pl.pallas_call(
         widen_kernel,
-        grid=(arrays[0].shape[0],),
+        grid=(arrays[0].shape[0] // 2,),
         in_specs=[spec(a) for a in arrays],
         out_specs=[spec(a) for a in arrays],
         out_shape=[jax.ShapeDtypeStruct(a.shape, f32) for a in arrays],

time: 886 us -> 885 us (level)
  no operation moved by 1% of the time
where the time goes in v8:
time: 885 us; the launch traced here: 884 us
  Pallas kernels  871 us (98%)
  local copies, waits for them, and re-layouts  11.4 us (1%)
    pallas_call x1, Pallas kernels, layer(): pl.pallas_call(layer_kernel, in_specs=[in_vmem] * 4 + [anywhere] * 4, out...  853 us
    pallas_call x1, Pallas kernels, widened(): pl.pallas_call(widen_kernel, grid=(arrays[0].shape[0] // 2,), in_specs=[s...  18 us

profile of v8, /device:TPU:0, one launch (start us, length us, event | category | flops | bytes accessed | tf_op | source)
XLA Modules:
  0.0 883.9 jit_solution(18083611426238999875)
XLA Ops:
  1.3 0.6 fusion.mask_ref
  1.9 5.3 copy_bitcast_fusion
  7.2 852.6 %layer.1 = (bf16[16,48,1024]{2,1,0:T(8,128)(2,1)}, bf16[16,48,1024]{2,1,0:T(8,128)(2,1)}, bf16[16,2,256,512]{3,2,1,0:T(8,128)(2,1)}, bf16[16,512,256]{2,1,0:T(8,...) custom-call(bf16[16,48,1024]{2,1,0:T(8,128)(2,1)} %get-tuple-element, ...), custom_call_target="tpu_custom_call" | custom-call | tf_op jit(solution)/shard_map/layer/pallas_call | solution.py:1720
  859.8 0.0 copy-start
  859.8 3.5 copy.22
  863.3 0.0 copy-done
  863.3 2.0 copy.23
  865.3 0.0 copy-start.1
  865.3 18.0 %widen.1 = (f32[16,3,256,128]{3,2,1,0:T(8,128)}, f32[16,128,256]{2,1,0:T(8,128)}, f32[16,2,256,512]{3,2,1,0:T(8,128)}, f32[16,512,256]{2,1,0:T(8,128)}) custom-call(bf16[16,3,256,128]{3,2,1,0:T(8,128)(2,1)} %get-tuple-element.20.refs_0_, bf16[16,128,256]{2,1,0:T(8,128)(2,1)} %get-tuple-element.21.refs_1_, ...), custom_call_target="tpu_custom_call" | custom-call | tf_op jit(solution)/shard_map/widen/pallas_call | solution.py:1754
  883.3 0.0 copy-done.1
  883.3 0.6 copy.28
Async XLA Ops:
  859.8 3.5 copy-start
  865.3 18.0 %copy-start.1 = (f32[2,16,256]{2,1,0:T(8,128)S(1)}, f32[2,16,256]{2,1,0:T(8,128)}, u32[]{:S(2)}) copy-start(f32[2,16,256]{2,1,0:T(8,128)} %get-tuple-element.58) | copy-start | bytes 98308
